TPU v7x, 32 devices: a whole 2x2x4 slice. The times are simulated.
32 devices in a mesh: ens: 2 (over y), gz: 4 (over z), ta: 2 (over x), gy: 2 (over core).
Axes of the slice: x: 2, y: 2, z: 4, core: 2. Of those that a mesh axis runs over, the one named last changes fastest.
Arguments:
- pole_vectors: float32 [8, 2, 3, 4, 16, 128], P('ens', None, None, 'ta', ('gz', 'gy')), parts along dimension 0, may hold values from -6 to 6
- gauge_links: bfloat16 [8, 2, 3, 3, 4, 16, 128], P('ens', None, None, None, 'ta', ('gz', 'gy')), parts along dimension 0, may hold values from -2.5 to 2.5
- pole_coeff: float32 [4], replicated, may hold values from 0.2 to 1
- naik_coeff: float32 [4], replicated, may hold values from 0.1 to 0.5
- staple_weight: float32 [4], replicated, may hold values from 0.1 to 0.4
Outputs:
- force: float32 [8, 2, 3, 3, 4, 16, 128], P('ens', None, None, None, 'ta', ('gz', 'gy')), parts along dimension 0
There are 2 independent parts, one for each index of `ens`. A program takes and returns all parts, laid end to end along the dimension named above; an argument that names none is the same for every part. Nothing has to cross between parts.
All inputs are finite; a program needn't handle non-finite values.
Results may differ from a plain program's by a relative error of at most 0.0003.
Values sent between devices are 32-bit elements; how exact they have to be, the bound alone decides.
No kernel may reach another device: no remote copies, remote signals or barrier semaphores. Data moves between devices by JAX's collectives and lax.ppermute only.
A program may use at most 64 MiB of HBM per device.

v0:
```python
import jax
import jax.numpy as jnp
from jax import lax
from jax.sharding import PartitionSpec as P

NX = 8
NY = 16
ZL = 2
TL = 2
NP = 4


def passed_along(value, axis, steps):
    count = lax.axis_size(axis)
    pairs = [(source, (source + steps) % count) for source in range(count)]
    return lax.ppermute(value, axis, pairs)


def real_product(left_mat, right_mat):
    return jnp.sum(left_mat[:, :, None] * right_mat[None, :, :], axis=1)


def mat_mul(left_mat, right_mat):
    real_part = real_product(left_mat[0], right_mat[0]) - real_product(left_mat[1], right_mat[1])
    imag_part = real_product(left_mat[0], right_mat[1]) + real_product(left_mat[1], right_mat[0])
    return jnp.stack([real_part, imag_part])


def dagger(matrix):
    return jnp.stack([jnp.swapaxes(matrix[0], 0, 1), -jnp.swapaxes(matrix[1], 0, 1)])


def outer_product(column, row_vec):
    real_part = column[0][:, None] * row_vec[0][None] + column[1][:, None] * row_vec[1][None]
    imag_part = column[1][:, None] * row_vec[0][None] - column[0][:, None] * row_vec[1][None]
    return jnp.stack([real_part, imag_part])


def cyclic(values, stride, period, offset):
    count = values.shape[-1]
    coord = jnp.arange(count, dtype=jnp.int32) // stride % period
    main_part = jnp.roll(values, -offset * stride, axis=values.ndim - 1)
    if offset > 0:
        wrapped = jnp.roll(values, (period - offset) * stride, axis=values.ndim - 1)
        beyond = coord + offset >= period
    else:
        wrapped = jnp.roll(values, -(offset + period) * stride, axis=values.ndim - 1)
        beyond = coord + offset < 0
    return jnp.where(beyond, wrapped, main_part)


def shift_dir(values, direction, offset):
    if direction == 0:
        return cyclic(values, 1, NX, offset)
    return cyclic(values, NX, NY, offset)


def as_blocks(values):
    return values.reshape((values.shape[0], TL, ZL, NY * NX))


def z_extend(values, thickness):
    blocks = as_blocks(values)
    received = passed_along(blocks[:, :, :thickness], ("gz", "gy"), -1)
    return jnp.concatenate([blocks, received], axis=2)


def z_window(extended, start):
    return extended[:, :, start : start + ZL].reshape((extended.shape[0], -1))


def t_extend(values, thickness):
    blocks = as_blocks(values)
    received = passed_along(blocks[:, :thickness], "ta", -1)
    return jnp.concatenate([blocks, received], axis=1)


def t_window(extended, start):
    return extended[:, start : start + TL].reshape((extended.shape[0], -1))


def z_back(values):
    blocks = as_blocks(values)
    received = passed_along(blocks[:, :, ZL - 1 :], ("gz", "gy"), 1)
    return jnp.concatenate([received, blocks[:, :, : ZL - 1]], axis=2).reshape(
        (values.shape[0], -1)
    )


def t_back(values):
    blocks = as_blocks(values)
    received = passed_along(blocks[:, TL - 1 :], "ta", 1)
    return jnp.concatenate([received, blocks[:, : TL - 1]], axis=1).reshape((values.shape[0], -1))


def pole_sum(ahead_flat, here_flat, coeffs):
    sites = here_flat.shape[-1]
    ahead_view = ahead_flat.reshape((NP, 2, 3, sites))
    here_view = here_flat.reshape((NP, 2, 3, sites))
    total = jnp.zeros((2, 3, 3, sites), jnp.float32)
    for pole in range(NP):
        total = total + coeffs[pole] * outer_product(ahead_view[pole], here_view[pole])
    return total


def on_device(pole_vectors, gauge_links, pole_coeff, naik_coeff, staple_weight):
    width_v = NP * 6
    vectors = pole_vectors.reshape((width_v, -1))
    gauge = gauge_links.astype(jnp.float32).reshape((72, -1))
    sites = vectors.shape[1]
    joined_z = z_window(z_extend(jnp.concatenate([vectors, gauge]), 1), 1)
    step_one_z = joined_z[:width_v]
    links_z = joined_z[width_v:]
    step_two_z = z_window(z_extend(step_one_z, 1), 1)
    step_three_z = z_window(z_extend(step_two_z, 1), 1)
    joined_t = t_window(t_extend(jnp.concatenate([vectors, gauge]), 1), 1)
    step_one_t = joined_t[:width_v]
    links_t = joined_t[width_v:]
    step_two_t = t_window(t_extend(step_one_t, 1), 1)
    step_three_t = t_window(t_extend(step_two_t, 1), 1)
    one_ahead = [shift_dir(vectors, 0, 1), shift_dir(vectors, 1, 1), step_one_z, step_one_t]
    three_ahead = [shift_dir(vectors, 0, 3), shift_dir(vectors, 1, 3), step_three_z, step_three_t]
    links_ahead = [shift_dir(gauge, 0, 1), shift_dir(gauge, 1, 1), links_z, links_t]
    matrix_shape = (2, 3, 3, sites)
    one_link = []
    three_link = []
    for direction in range(4):
        one_link.append(pole_sum(one_ahead[direction], vectors, pole_coeff))
        three_link.append(pole_sum(three_ahead[direction], vectors, naik_coeff))
    others_z = [0, 1, 3]
    others_t = [0, 1, 2]
    z_faces = {}
    t_faces = {}
    moved_z = z_window(
        z_extend(jnp.concatenate([one_link[index].reshape((18, sites)) for index in others_z]), 1),
        1,
    )
    moved_t = t_window(
        t_extend(jnp.concatenate([one_link[index].reshape((18, sites)) for index in others_t]), 1),
        1,
    )
    for position in range(3):
        z_faces[others_z[position]] = moved_z[18 * position : 18 * position + 18].reshape(
            matrix_shape
        )
        t_faces[others_t[position]] = moved_t[18 * position : 18 * position + 18].reshape(
            matrix_shape
        )
    link_mats = gauge.reshape((4,) + matrix_shape)
    moved_mats = [links_ahead[index].reshape((4,) + matrix_shape) for index in range(4)]
    forward_terms = {}
    backward_terms = {}
    for direction in range(4):
        for across in range(4):
            if across == direction:
                continue
            if across < 2:
                moved_force = shift_dir(one_link[direction], across, 1)
            elif across == 2:
                moved_force = z_faces[direction]
            else:
                moved_force = t_faces[direction]
            forward_terms[direction, across] = mat_mul(
                mat_mul(link_mats[across], moved_force), dagger(moved_mats[direction][across])
            )
    z_pack = jnp.concatenate(
        [one_link[index].reshape((18, sites)) for index in others_z]
        + [gauge[36:54]]
        + [links_ahead[index][36:54] for index in others_z]
    )
    behind_z = z_back(z_pack)
    t_pack = jnp.concatenate(
        [one_link[index].reshape((18, sites)) for index in others_t]
        + [gauge[54:72]]
        + [links_ahead[index][54:72] for index in others_t]
    )
    behind_t = t_back(t_pack)
    for direction in range(4):
        for across in range(4):
            if across == direction:
                continue
            if across < 2:
                force_back = shift_dir(one_link[direction], across, -1)
                link_back = shift_dir(gauge[18 * across : 18 * across + 18], across, -1)
                corner_link = shift_dir(
                    links_ahead[direction][18 * across : 18 * across + 18], across, -1
                )
            else:
                packed = behind_z if across == 2 else behind_t
                others = [index for index in range(4) if index != across]
                position = others.index(direction)
                force_back = packed[18 * position : 18 * position + 18]
                link_back = packed[54:72]
                corner_link = packed[72 + 18 * position : 90 + 18 * position]
            backward_terms[direction, across] = mat_mul(
                mat_mul(dagger(link_back.reshape(matrix_shape)), force_back.reshape(matrix_shape)),
                corner_link.reshape(matrix_shape),
            )
    forces = []
    for direction in range(4):
        staple_sum = jnp.zeros(matrix_shape, jnp.float32)
        for across in range(4):
            if across == direction:
                continue
            staple_sum = staple_sum + forward_terms[direction, across]
            staple_sum = staple_sum + backward_terms[direction, across]
        forces.append(
            one_link[direction] + three_link[direction] + staple_weight[direction] * staple_sum
        )
    return jnp.stack(forces).reshape((4, 2, 3, 3, TL, ZL, NY * NX))


def solution(mesh):
    return jax.shard_map(
        on_device,
        mesh=mesh,
        in_specs=(
            P("ens", None, None, "ta", ("gz", "gy"), None),
            P("ens", None, None, None, "ta", ("gz", "gy"), None),
            P(),
            P(),
            P(),
        ),
        out_specs=P("ens", None, None, None, "ta", ("gz", "gy"), None),
        check_vma=False,
    )
```

profile of v0, /device:TPU:1, one launch (start us, length us, event | category | flops | bytes accessed | tf_op | source)
XLA Modules:
  0.0 156.6 jit_solution(2158190008171002556)
XLA Ops:
  0.0 1.5 slice.2496
  2.2 2.7 %collective-permute-start.8 = (f32[24,1,2,128]{3,2,1,0:T(2,128)}, f32[24,1,2,128]{3,2,1,0:T(2,128)}, u32[]{:S(2)}, u32[]{:S(2)}) collective-permute-start(f32[24,1,2,128]{3,2,1,0:T(2,128)} %slice.2541), channel_id=1, source_target_pairs={{0,2},{2,0},{1,3},{3,1},{4,6},{6,4},{5,7},{7,5},{8,10},{10,8},{9,1... | collective-permute-start | bytes 73736 | tf_op jit(solution)/shard_map/ppermute | solution.py:16
  4.8 0.9 convert_element_type.3
  6.0 3.9 %collective-permute-start.3 = (f32[96,2,1,128]{3,2,1,0:T(1,128)S(1)}, f32[96,2,1,128]{3,2,1,0:T(1,128)S(1)}, u32[]{:S(2)}, u32[]{:S(2)}) collective-permute-start(f32[96,2,1,128]{3,2,1,0:T(1,128)S(1)} %pad_maximum_fusion.3), channel_id=1, source_target_pairs={{0,13},{1,0},{4,1},{5,4},{8,5},{9,8},{12,9},{13,12},{2,15},{3,2},{... | collective-permute-start | bytes 294920 | tf_op jit(solution)/shard_map/ppermute | solution.py:16
  11.1 0.6 fusion.139
  13.1 0.7 slice.2471
  14.1 0.7 slice.2367
  15.7 0.7 slice.2459
  17.0 0.7 slice.2355
  19.0 0.7 fusion.142
  19.7 0.7 fusion.141
  20.3 0.7 fusion.140
  45.1 0.6 mul.6521
  46.4 0.6 copy_bitcast_fusion.6
  50.7 2.5 %fusion.12 = f32[2,3,3,512]{3,2,1,0:T(4,128)S(1)} fusion(f32[1,3,3,512]{3,2,1,0:T(4,128)S(1)} %get-tuple-element.472, f32[1,3,3,512]{3,2,1,0:T(4,128)S(1)} %get-tuple-element.471, f32[1,3,3,512]{3,2,1,0:T(4,128)S(1)} %get-tuple-element.470, f32[1,3,3,512]{3,2,1,0:T(4,128)S(1)} %get-tuple-element.469, f32[1,3,3,512]{3,2,1,0:T(4,128)S(1)} %get-tuple-element.468, ...), kind=kLoop, calls=%fused_computation.284 | loop fusion | flops 101376 | bytes 184336 | tf_op jit(solution)/shard_map/add | solution.py:102
  53.2 0.7 fusion.128
  53.8 0.7 fusion.129
  54.5 0.7 fusion.114
  55.2 0.7 fusion.115
  55.9 2.5 %fusion.6 = f32[2,3,3,512]{3,2,1,0:T(4,128)S(1)} fusion(f32[1,3,3,512]{3,2,1,0:T(4,128)S(1)} %get-tuple-element.579, f32[1,3,3,512]{3,2,1,0:T(4,128)S(1)} %get-tuple-element.580, f32[1,3,3,512]{3,2,1,0:T(4,128)S(1)} %get-tuple-element.573, f32[1,3,3,512]{3,2,1,0:T(4,128)S(1)} %get-tuple-element.574, f32[1,3,3,512]{3,2,1,0:T(4,128)S(1)} %get-tuple-element.567, ...), kind=kLoop, calls=%fused_computation.270 | loop fusion | flops 101376 | bytes 184336 | tf_op jit(solution)/shard_map/add | solution.py:102
  58.3 0.7 fusion.118
  59.0 0.7 fusion.119
  59.7 2.5 %fusion.9 = f32[2,3,3,512]{3,2,1,0:T(4,128)S(1)} fusion(f32[1,3,3,512]{3,2,1,0:T(4,128)S(1)} %get-tuple-element.581, f32[1,3,3,512]{3,2,1,0:T(4,128)S(1)} %get-tuple-element.582, f32[1,3,3,512]{3,2,1,0:T(4,128)S(1)} %get-tuple-element.575, f32[1,3,3,512]{3,2,1,0:T(4,128)S(1)} %get-tuple-element.576, f32[1,3,3,512]{3,2,1,0:T(4,128)S(1)} %get-tuple-element.569, ...), kind=kLoop, calls=%fused_computation.277 | loop fusion | flops 101376 | bytes 184336 | tf_op jit(solution)/shard_map/add | solution.py:102
  62.2 0.7 fusion.124
  62.8 0.7 fusion.125
  63.5 0.7 fusion.110
  64.2 0.7 fusion.111
  64.8 2.5 %fusion.3 = f32[2,3,3,512]{3,2,1,0:T(4,128)S(1)} fusion(f32[1,3,3,512]{3,2,1,0:T(4,128)S(1)} %get-tuple-element.583, f32[1,3,3,512]{3,2,1,0:T(4,128)S(1)} %get-tuple-element.584, f32[1,3,3,512]{3,2,1,0:T(4,128)S(1)} %get-tuple-element.577, f32[1,3,3,512]{3,2,1,0:T(4,128)S(1)} %get-tuple-element.578, f32[1,3,3,512]{3,2,1,0:T(4,128)S(1)} %get-tuple-element.571, ...), kind=kLoop, calls=%fused_computation.258 | loop fusion | flops 101376 | bytes 184336 | tf_op jit(solution)/shard_map/add | solution.py:102
  67.3 0.7 fusion.132
  68.0 0.7 fusion.133
  70.4 0.7 slice.2558
  71.9 0.7 slice.2512
  73.3 0.7 slice.2530
  74.6 0.7 slice.2576
  76.8 1.2 collective-permute-start.9
  81.2 0.7 pad_maximum_fusion.12
  82.0 0.7 copy-done.39
  82.7 0.7 copy-done.38
  89.4 0.7 copy-done.18
  90.4 0.7 copy-done.4
  92.6 0.7 copy-done.8
  94.7 0.7 copy-done.10
  97.2 0.7 copy-done.2
  99.3 0.7 copy-done.6
  101.4 0.7 copy-done.7
  104.8 0.7 slice.2386
  105.4 0.6 slice.2413
  112.5 1.2 collective-permute-start.5
  113.7 0.7 pad_maximum_fusion.29
  114.5 0.7 pad_maximum_fusion.27
  115.2 1.8 %collective-permute-start.2 = (f32[126,2,1,128]{3,2,1,0:T(1,128)S(1)}, f32[126,2,1,128]{3,2,1,0:T(1,128)S(1)}, u32[]{:S(2)}, u32[]{:S(2)}) collective-permute-start(f32[126,2,1,128]{3,2,1,0:T(1,128)S(1)} %get-tuple-element.260), channel_id=1, source_target_pairs={{0,1},{1,4},{4,5},{5,8},{8,9},{9,12},{12,13},{13,0},{2,3},{3,6},{6... | collective-permute-start | bytes 387080 | tf_op jit(solution)/shard_map/ppermute | solution.py:16
  117.0 0.7 pad_maximum_fusion.36
  117.8 0.9 pad_maximum_fusion.38
  122.3 0.8 pad_maximum_fusion.15
  123.7 0.7 copy-done.15
  124.8 0.7 copy-done.12
  130.7 5.7 %fusion.41 = f32[1,2,3,3,2,2,128]{6,5,4,3,2,1,0:T(2,128)S(1)} fusion(f32[1,1,3,3,2,2,128]{6,5,4,3,2,1,0:T(2,128)S(1)} %get-tuple-element.631, f32[1,1,3,3,2,2,128]{6,5,4,3,2,1,0:T(2,128)S(1)} %get-tuple-element.632, f32[1,1,3,3,2,2,128]{6,5,4,3,2,1,0:T(2,128)S(1)} %get-tuple-element.617, f32[1,1,3,3,2,2,128]{6,5,4,3,2,1,0:T(2,128)S(1)} %get-tuple-element.618, ...), kind=kLoop, calls=%fused_computation.375 | loop fusion | flops 331776 | bytes 552996 | tf_op jit(solution)/shard_map/add | solution.py:208
  136.4 0.7 copy-done.22
  137.1 5.7 %fusion.17 = f32[1,2,3,3,2,2,128]{6,5,4,3,2,1,0:T(2,128)S(1)} fusion(f32[1,1,3,3,2,2,128]{6,5,4,3,2,1,0:T(2,128)S(1)} %get-tuple-element.639, f32[1,1,3,3,2,2,128]{6,5,4,3,2,1,0:T(2,128)S(1)} %get-tuple-element.640, f32[1,1,3,3,2,2,128]{6,5,4,3,2,1,0:T(2,128)S(1)} %get-tuple-element.625, f32[1,1,3,3,2,2,128]{6,5,4,3,2,1,0:T(2,128)S(1)} %get-tuple-element.626, ...), kind=kLoop, calls=%fused_computation.333 | loop fusion | flops 331776 | bytes 552996 | tf_op jit(solution)/shard_map/add | solution.py:208
  142.9 0.7 copy-done.26
  143.6 5.8 %fusion.29 = f32[1,2,3,3,2,2,128]{6,5,4,3,2,1,0:T(2,128)S(1)} fusion(f32[1,1,3,3,2,2,128]{6,5,4,3,2,1,0:T(2,128)S(1)} %get-tuple-element.627, f32[1,1,3,3,2,2,128]{6,5,4,3,2,1,0:T(2,128)S(1)} %get-tuple-element.628, f32[1,1,3,3,2,2,128]{6,5,4,3,2,1,0:T(2,128)S(1)} %get-tuple-element.613, f32[1,1,3,3,2,2,128]{6,5,4,3,2,1,0:T(2,128)S(1)} %get-tuple-element.614, ...), kind=kLoop, calls=%fused_computation.354 | loop fusion | flops 331776 | bytes 552996 | tf_op jit(solution)/shard_map/add | solution.py:208
  149.5 0.7 copy-done.20
  150.1 5.7 %fusion.53 = f32[1,2,3,3,2,2,128]{6,5,4,3,2,1,0:T(2,128)S(1)} fusion(f32[1,1,3,3,2,2,128]{6,5,4,3,2,1,0:T(2,128)S(1)} %get-tuple-element.635, f32[1,1,3,3,2,2,128]{6,5,4,3,2,1,0:T(2,128)S(1)} %get-tuple-element.636, f32[1,1,3,3,2,2,128]{6,5,4,3,2,1,0:T(2,128)S(1)} %get-tuple-element.621, f32[1,1,3,3,2,2,128]{6,5,4,3,2,1,0:T(2,128)S(1)} %get-tuple-element.622, ...), kind=kLoop, calls=%fused_computation.396 | loop fusion | flops 331776 | bytes 552996 | tf_op jit(solution)/shard_map/add | solution.py:208
  155.9 0.7 pad_maximum_fusion.2
  (814 shorter events, 73.3 us)
Async XLA Ops:
  0.0 1.6 copy-start
  1.5 113.7 %collective-permute-start.6 = (f32[24,2,1,128]{3,2,1,0:T(1,128)}, f32[24,2,1,128]{3,2,1,0:T(1,128)}, u32[]{:S(2)}, u32[]{:S(2)}) collective-permute-start(f32[24,2,1,128]{3,2,1,0:T(1,128)} %slice.2496), channel_id=1, source_target_pairs={{0,13},{1,0},{4,1},{5,4},{8,5},{9,8},{12,9},{13,12},{2,15},{3,2},{... | collective-permute-start | bytes 73736 | tf_op jit(solution)/shard_map/ppermute | solution.py:16
  2.2 109.7 %collective-permute-start.8 = (f32[24,1,2,128]{3,2,1,0:T(2,128)}, f32[24,1,2,128]{3,2,1,0:T(2,128)}, u32[]{:S(2)}, u32[]{:S(2)}) collective-permute-start(f32[24,1,2,128]{3,2,1,0:T(2,128)} %slice.2541), channel_id=1, source_target_pairs={{0,2},{2,0},{1,3},{3,1},{4,6},{6,4},{5,7},{7,5},{8,10},{10,8},{9,1... | collective-permute-start | bytes 73736 | tf_op jit(solution)/shard_map/ppermute | solution.py:16
  5.8 42.5 %collective-permute-start = (f32[96,1,2,128]{3,2,1,0:T(2,128)S(1)}, f32[96,1,2,128]{3,2,1,0:T(2,128)S(1)}, u32[]{:S(2)}, u32[]{:S(2)}) collective-permute-start(f32[96,1,2,128]{3,2,1,0:T(2,128)S(1)} %fusion), channel_id=1, source_target_pairs={{0,2},{2,0},{1,3},{3,1},{4,6},{6,4},{5,7},{7,5},{8,10},{10,8},{9,1... | collective-permute-start | bytes 294920 | tf_op jit(solution)/shard_map/ppermute | solution.py:16
  6.0 43.0 %collective-permute-start.3 = (f32[96,2,1,128]{3,2,1,0:T(1,128)S(1)}, f32[96,2,1,128]{3,2,1,0:T(1,128)S(1)}, u32[]{:S(2)}, u32[]{:S(2)}) collective-permute-start(f32[96,2,1,128]{3,2,1,0:T(1,128)S(1)} %pad_maximum_fusion.3), channel_id=1, source_target_pairs={{0,13},{1,0},{4,1},{5,4},{8,5},{9,8},{12,9},{13,12},{2,15},{3,2},{... | collective-permute-start | bytes 294920 | tf_op jit(solution)/shard_map/ppermute | solution.py:16
  9.9 21.1 %copy-start.153 = (pred[512]{0:T(512)(128)(4,1)}, pred[512]{0:T(512)(128)(4,1)S(1)}, u32[]{:S(2)}) copy-start(pred[512]{0:T(512)(128)(4,1)S(1)} %add_compare_fusion.5) | copy-start | bytes 1540
  9.9 21.0 %copy-start.151 = (pred[512]{0:T(512)(128)(4,1)}, pred[512]{0:T(512)(128)(4,1)S(1)}, u32[]{:S(2)}) copy-start(pred[512]{0:T(512)(128)(4,1)S(1)} %add_compare_fusion.3) | copy-start | bytes 1540
  11.1 0.9 copy-start.1
  18.3 1.3 copy-start.149
  18.4 2.0 %copy-start.150 = (f32[4]{0:T(128)S(1)}, f32[4]{0:T(128)}, u32[]{:S(2)}) copy-start(f32[4]{0:T(128)} %param.9) | copy-start | bytes 52
  76.8 35.7 %collective-permute-start.9 = (f32[24,1,2,128]{3,2,1,0:T(2,128)}, f32[24,1,2,128]{3,2,1,0:T(2,128)}, u32[]{:S(2)}, u32[]{:S(2)}) collective-permute-start(f32[24,1,2,128]{3,2,1,0:T(2,128)} %slice.2542), channel_id=1, source_target_pairs={{0,2},{2,0},{1,3},{3,1},{4,6},{6,4},{5,7},{7,5},{8,10},{10,8},{9,1... | collective-permute-start | bytes 73736 | tf_op jit(solution)/shard_map/ppermute | solution.py:16
  78.6 38.4 %collective-permute-start.7 = (f32[24,2,1,128]{3,2,1,0:T(1,128)}, f32[24,2,1,128]{3,2,1,0:T(1,128)}, u32[]{:S(2)}, u32[]{:S(2)}) collective-permute-start(f32[24,2,1,128]{3,2,1,0:T(1,128)} %slice.2497), channel_id=1, source_target_pairs={{0,13},{1,0},{4,1},{5,4},{8,5},{9,8},{12,9},{13,12},{2,15},{3,2},{... | collective-permute-start | bytes 73736 | tf_op jit(solution)/shard_map/ppermute | solution.py:16
  90.4 0.7 copy-start.5
  94.6 0.7 copy-start.11
  102.1 1.4 copy-start.75
  102.2 1.3 copy-start.80
  102.2 1.3 copy-start.81
  102.2 1.3 copy-start.82
  102.2 1.3 copy-start.83
  106.1 16.3 %collective-permute-start.4 = (f32[54,1,2,128]{3,2,1,0:T(2,128)}, f32[54,1,2,128]{3,2,1,0:T(2,128)}, u32[]{:S(2)}, u32[]{:S(2)}) collective-permute-start(f32[54,1,2,128]{3,2,1,0:T(2,128)} %slice.2413), channel_id=1, source_target_pairs={{0,2},{2,0},{1,3},{3,1},{4,6},{6,4},{5,7},{7,5},{8,10},{10,8},{9,1... | collective-permute-start | bytes 165896 | tf_op jit(solution)/shard_map/ppermute | solution.py:16
  111.9 11.5 %collective-permute-start.1 = (f32[54,2,1,128]{3,2,1,0:T(1,128)}, f32[54,2,1,128]{3,2,1,0:T(1,128)S(1)}, u32[]{:S(2)}, u32[]{:S(2)}) collective-permute-start(f32[54,2,1,128]{3,2,1,0:T(1,128)} %slice.2386), channel_id=1, source_target_pairs={{0,13},{1,0},{4,1},{5,4},{8,5},{9,8},{12,9},{13,12},{2,15},{3,2},{... | collective-permute-start | bytes 165896 | tf_op jit(solution)/shard_map/ppermute | solution.py:16
  112.5 14.3 %collective-permute-start.5 = (f32[126,1,2,128]{3,2,1,0:T(2,128)S(1)}, f32[126,1,2,128]{3,2,1,0:T(2,128)S(1)}, u32[]{:S(2)}, u32[]{:S(2)}) collective-permute-start(f32[126,1,2,128]{3,2,1,0:T(2,128)S(1)} %get-tuple-element.258), channel_id=1, source_target_pairs={{0,2},{2,0},{1,3},{3,1},{4,6},{6,4},{5,7},{7,5},{8,10},{10,8},{9,1... | collective-permute-start | bytes 387080 | tf_op jit(solution)/shard_map/ppermute | solution.py:16
  115.2 13.1 %collective-permute-start.2 = (f32[126,2,1,128]{3,2,1,0:T(1,128)S(1)}, f32[126,2,1,128]{3,2,1,0:T(1,128)S(1)}, u32[]{:S(2)}, u32[]{:S(2)}) collective-permute-start(f32[126,2,1,128]{3,2,1,0:T(1,128)S(1)} %get-tuple-element.260), channel_id=1, source_target_pairs={{0,1},{1,4},{4,5},{5,8},{8,9},{9,12},{12,13},{13,0},{2,3},{3,6},{6... | collective-permute-start | bytes 387080 | tf_op jit(solution)/shard_map/ppermute | solution.py:16
  117.7 1.0 copy-start.63
  117.7 1.0 copy-start.65
  117.7 1.0 copy-start.67
  117.7 1.0 copy-start.114
  117.7 1.0 copy-start.115
  117.7 1.0 copy-start.130
  117.7 1.0 copy-start.131
  117.7 1.0 copy-start.138
  117.7 1.0 copy-start.139
  117.7 1.0 copy-start.144
  117.8 1.0 copy-start.145
  117.8 1.0 copy-start.146
  117.8 1.0 copy-start.147
  119.4 0.8 copy-start.134
  119.4 0.8 copy-start.135
  119.4 0.8 copy-start.140
  119.4 0.8 copy-start.141
  119.4 0.8 copy-start.142
  119.4 0.8 copy-start.143
  120.3 0.8 copy-start.120
  120.3 0.8 copy-start.121
  120.3 0.8 copy-start.122
  120.3 0.8 copy-start.123
  120.3 0.8 copy-start.132
  120.3 0.8 copy-start.133
  120.4 0.8 copy-start.136
  120.4 0.8 copy-start.137
  121.3 0.8 copy-start.116
  121.3 0.8 copy-start.117
  121.3 0.8 copy-start.118
  121.3 0.8 copy-start.119
  121.3 0.8 copy-start.124
  121.3 0.8 copy-start.125
  121.3 0.8 copy-start.126
  121.3 0.8 copy-start.127
  130.7 5.8 %copy-start.23 = (f32[1,1,3,3,2,2,128]{6,5,4,3,2,1,0:T(2,128)S(1)}, f32[1,1,3,3,2,2,128]{6,5,4,3,2,1,0:T(2,128)}, u32[]{:S(2)}) copy-start(f32[1,1,3,3,2,2,128]{6,5,4,3,2,1,0:T(2,128)} %stack.596) | copy-start | bytes 55300
  137.1 5.8 %copy-start.27 = (f32[1,1,3,3,2,2,128]{6,5,4,3,2,1,0:T(2,128)S(1)}, f32[1,1,3,3,2,2,128]{6,5,4,3,2,1,0:T(2,128)}, u32[]{:S(2)}) copy-start(f32[1,1,3,3,2,2,128]{6,5,4,3,2,1,0:T(2,128)} %stack.650) | copy-start | bytes 55300
  137.1 5.8 %copy-start.32 = (f32[1,1,3,3,2,2,128]{6,5,4,3,2,1,0:T(2,128)S(1)}, f32[1,1,3,3,2,2,128]{6,5,4,3,2,1,0:T(2,128)}, u32[]{:S(2)}) copy-start(f32[1,1,3,3,2,2,128]{6,5,4,3,2,1,0:T(2,128)} %stack.653) | copy-start | bytes 55300
  143.6 5.8 %copy-start.21 = (f32[1,1,3,3,2,2,128]{6,5,4,3,2,1,0:T(2,128)S(1)}, f32[1,1,3,3,2,2,128]{6,5,4,3,2,1,0:T(2,128)}, u32[]{:S(2)}) copy-start(f32[1,1,3,3,2,2,128]{6,5,4,3,2,1,0:T(2,128)} %stack.740) | copy-start | bytes 55300
  143.6 5.8 %copy-start.28 = (f32[1,1,3,3,2,2,128]{6,5,4,3,2,1,0:T(2,128)S(1)}, f32[1,1,3,3,2,2,128]{6,5,4,3,2,1,0:T(2,128)}, u32[]{:S(2)}) copy-start(f32[1,1,3,3,2,2,128]{6,5,4,3,2,1,0:T(2,128)} %stack.733) | copy-start | bytes 55300
  143.6 5.8 %copy-start.29 = (f32[1,1,3,3,2,2,128]{6,5,4,3,2,1,0:T(2,128)S(1)}, f32[1,1,3,3,2,2,128]{6,5,4,3,2,1,0:T(2,128)}, u32[]{:S(2)}) copy-start(f32[1,1,3,3,2,2,128]{6,5,4,3,2,1,0:T(2,128)} %stack.734) | copy-start | bytes 55300
  (104 other events, 73.5 us)
where the time goes:
time: 159 us; the launch traced here: 157 us
  local copies, waits for them, and re-layouts  92.3 us (58%)
  other arithmetic  48.5 us (31%)
  starting transfers between devices  12.1 us (8%)
  between operations  3.61 us (2%)
    add x4, other arithmetic, on_device(): one_link[direction] + three_link[direction]  23 us
    unnamed x326, local copies, waits for them, and re-layouts  19.9 us
    ppermute x10, starting transfers between devices, passed_along(): return lax.ppermute(value, axis, pairs)  12.1 us
    another operation x48, local copies, waits for them, and re-layouts, mat_mul(): return jnp.stack([real_part, imag_part])  11.4 us
    slice x34, local copies, waits for them, and re-layouts, cyclic(): main_part = jnp.roll(values, -offset * stride, axis=values.ndim - 1)  10.5 us
    mul x28, local copies, waits for them, and re-layouts, outer_product(): column[1][:, None] * row_vec[1][None]  9.9 us
    add x4, other arithmetic, pole_sum(): total + coeffs[pole] * outer_product(ahead_view[pole], here_view[pole])  9.89 us
    mul x28, local copies, waits for them, and re-layouts, outer_product(): column[0][:, None] * row_vec[0][None]  9.89 us
  transfers between devices with their start and end apart: 10, of which 0 were waited for; matrix products, arithmetic and copies ran while one was open for 60% of the time, Pallas kernels for 0%

commit v1 on v0

v1 whole, which is shorter than its diff:
```python
import collections
import functools

import jax
import jax.numpy as jnp
from jax import lax
from jax.experimental import pallas as pl
from jax.experimental.pallas import tpu as pltpu
from jax.sharding import PartitionSpec as P

NX = 8
NY = 16
LANES = NX * NY
NP = 4
VEC = NP * 6
MAT = 18
SLOT = 24
TILE = 8 * SLOT
PAIRS = ((0, 1), (2, 3))
CROSS = (((1, 0), (2, 2), (3, 3)), ((0, 0), (1, 1), (3, 2)))
UNIT = ((1, 0, 0, 0), (0, 1, 0, 0), (0, 0, 1, 0), (0, 0, 0, 1))
CHUNKS = {"x": (8, 8, 8), "u": (8, 8, 2)}
F32 = jnp.float32


def plus(left, right, scale=1):
    return tuple(a + scale * b for a, b in zip(left, right))


def halo_plan(t_size):
    both = ((0, 0), (0, 1), (1, 0), (1, 1))
    t_low, t_high = ((0, 0), (0, 1)), ((1, 0), (1, 1))
    z_low, z_high = ((0, 0), (1, 0)), ((0, 1), (1, 1))

    def blocks(vec_at, links, link_at):
        found = [("x", 0) + at for at in vec_at]
        return found + [("u", n) + at for n in links for at in link_at]

    wanted = {
        (0, 1): blocks(both, (0, 1, 3), z_low),
        (0, 2): blocks(z_low, (), ()),
        (0, -1): blocks(z_high, (2,), z_high),
        (1, 0): blocks(both, (0, 1, 2), t_low),
        (2, 0): blocks(t_low, (), ()),
        (-1, 0): blocks(t_high, (3,), t_high),
        (1, 1): blocks(((0, 0),), (), ()),
        (-1, 1): blocks(((1, 0),), (3,), ((1, 0),)),
        (1, -1): blocks(((0, 1),), (2,), ((0, 1),)),
    }
    sends = collections.OrderedDict()
    for (dt, dz), items in wanted.items():
        to = (dt % t_size, dz)
        if to == (0, 0):
            continue
        held = sends.setdefault(to, [])
        held.extend(item for item in items if item not in held)
    return [(to, items) for to, items in sends.items()]


def block_rows(items):
    offsets, row = {}, 0
    for item in items:
        offsets[item] = row
        row += VEC if item[0] == "x" else MAT
    return offsets, -(-row // 8) * 8


def local_row(item):
    kind, n, t, z = item
    r = 2 * t + z
    return r * VEC if kind == "x" else (r * 4 + n) * SLOT


def copy_block(kind, src, src_row, dst, dst_rows, change=None):
    done = 0
    for size in CHUNKS[kind]:
        value = src[pl.ds(src_row + done, size), :]
        if change is not None:
            value = change(value)
        for dst_row in dst_rows:
            dst[pl.ds(dst_row + done, size), :] = value
        done += size


def pack_kernel(plan, x_ref, u_ref, xl_ref, ul_ref, *rest):
    outs, wide = rest[:-1], rest[-1]
    wide[...] = u_ref[...].astype(F32)
    for r in range(4):
        for k in range(3):
            xl_ref[pl.ds(r * VEC + 8 * k, 8), :] = x_ref[pl.ds(r + 32 * k, 8, stride=4), :]
        for n in range(4):
            done = 0
            for size in CHUNKS["u"]:
                value = wide[pl.ds((MAT * n + done) * 4 + r, size, stride=4), :]
                ul_ref[pl.ds((r * 4 + n) * SLOT + done, size), :] = value
                done += size
    for out, (_, items) in zip(outs, plan):
        offsets, _ = block_rows(items)
        for item, row in offsets.items():
            copy_block(item[0], xl_ref if item[0] == "x" else ul_ref, local_row(item), out, (row,))


def tile_fields():
    x_fields, u_fields = [], []
    zero = (0, 0, 0, 0)
    for pair, crosses in zip(PAIRS, CROSS):
        for cross in crosses:
            for sign in (1, -1):
                start = [plus(zero, UNIT[n], sign) for n in cross]
                x_fields.append([("x", 0, start[h]) for h in range(2)])
                x_fields.append([("x", 0, plus(start[h], UNIT[pair[h]])) for h in range(2)])
                base = [zero if sign > 0 else start[h] for h in range(2)]
                u_fields.append([("u", cross[h], base[h]) for h in range(2)])
                u_fields.append([("u", cross[h], plus(base[h], UNIT[pair[h]])) for h in range(2)])
    x_fields.append([("x", 0, zero)] * 2)
    for pair in PAIRS:
        x_fields.append([("x", 0, UNIT[m]) for m in pair])
        x_fields.append([("x", 0, plus(zero, UNIT[m], 3)) for m in pair])
    return x_fields, u_fields


def find_block(where, t_size, kind, n, t, z):
    dt, t_in = divmod(t, 2)
    dz, z_in = divmod(z, 2)
    to = (dt % t_size, dz)
    item = (kind, n, t_in, z_in)
    if to == (0, 0):
        return ("local", kind), local_row(item)
    return to, where[to][item]


def lane_shifted(value, dx, dy):
    if dx != 0:
        x_at = lax.broadcasted_iota(jnp.int32, value.shape, 1) % NX
        beyond = (x_at + dx >= NX) | (x_at + dx < 0)
        main = pltpu.roll(value, (-dx) % LANES, 1)
        wrapped = pltpu.roll(value, (NX - dx if dx > 0 else -NX - dx) % LANES, 1)
        value = jnp.where(beyond, wrapped, main)
    if dy != 0:
        value = pltpu.roll(value, (-dy * NX) % LANES, 1)
    return value


def build_fields(buffers, where, t_size, x_tiles, u_tiles):
    x_fields, u_fields = tile_fields()
    copies = collections.OrderedDict()
    for target, fields in ((0, x_fields), (1, u_fields)):
        for index, halves in enumerate(fields):
            for half, (kind, n, disp) in enumerate(halves):
                for r in range(4):
                    source = find_block(where, t_size, kind, n, r // 2 + disp[3], r % 2 + disp[2])
                    row = index * TILE + (4 * half + r) * SLOT
                    group = copies.setdefault((kind,) + source, collections.OrderedDict())
                    group.setdefault((disp[0], disp[1]), []).append(row)
    for (kind, name, src_row), shifts in copies.items():
        target = x_tiles if kind == "x" else u_tiles
        for (dx, dy), rows in shifts.items():
            change = functools.partial(lane_shifted, dx=dx, dy=dy)
            copy_block(kind, buffers[name], src_row, target, rows, change)


def tile_of(ref, base, component):
    return ref[pl.ds(base + component, 8, stride=SLOT), :]


def vector_tiles(ref, base, pole):
    return [[tile_of(ref, base, pole * 6 + part * 3 + i) for i in range(3)] for part in range(2)]


def pole_sum(ref, here, ahead, scales):
    total = None
    for pole in range(NP):
        h = [[scales[pole] * v for v in part] for part in vector_tiles(ref, here, pole)]
        a = vector_tiles(ref, ahead, pole)
        real = [[a[0][i] * h[0][j] + a[1][i] * h[1][j] for j in range(3)] for i in range(3)]
        imag = [[a[1][i] * h[0][j] - a[0][i] * h[1][j] for j in range(3)] for i in range(3)]
        if total is None:
            total = [real, imag]
        else:
            total = [
                [[total[c][i][j] + new[i][j] for j in range(3)] for i in range(3)]
                for c, new in enumerate((real, imag))
            ]
    return total


def matrix_tiles(ref, base):
    return [
        [[tile_of(ref, base, part * 9 + i * 3 + j) for j in range(3)] for i in range(3)]
        for part in range(2)
    ]


def conj(matrix, transposed=True):
    return [[[matrix[part][j][i] for j in range(3)] for i in range(3)] for part in range(2)]


def row_times(row, right, row_sign, right_sign):
    result = [[], []]
    for j in range(3):
        real = imag = None
        for k in range(3):
            rr = row[0][k] * right[0][k][j]
            ii = row[1][k] * right[1][k][j]
            ri = row[0][k] * right[1][k][j]
            ir = row[1][k] * right[0][k][j]
            new_real = rr - ii if row_sign * right_sign > 0 else rr + ii
            if row_sign > 0 and right_sign > 0:
                new_imag = ri + ir
            elif row_sign > 0:
                new_imag = ir - ri
            else:
                new_imag = ri - ir
            real = new_real if real is None else real + new_real
            imag = new_imag if imag is None else imag + new_imag
        result[0].append(real)
        result[1].append(imag)
    return result


def main_kernel(names, where, t_size, near_ref, far_ref, weight_ref, xl_ref, ul_ref, *rest):
    received = rest[: len(names)]
    out_ref, x_tiles, u_tiles, acc = rest[len(names) :]
    buffers = {("local", "x"): xl_ref, ("local", "u"): ul_ref}
    buffers.update(zip(names, received))
    build_fields(buffers, where, t_size, x_tiles, u_tiles)
    near = [near_ref[p] for p in range(NP)]
    far = [far_ref[p] for p in range(NP)]
    upper = lax.broadcasted_iota(jnp.int32, (8, LANES), 0) < 4

    def term(step, first):
        group = step // 3
        for side in range(2):
            base = (step * 2 + side) * 2 * TILE
            force = pole_sum(x_tiles, base, base + TILE, near)
            left = matrix_tiles(u_tiles, base)
            right = matrix_tiles(u_tiles, base + TILE)
            if side == 1:
                left = conj(left)
            else:
                right = conj(right)
            for i in range(3):
                row = [left[0][i], left[1][i]]
                if side == 0:
                    row = row_times(row_times(row, force, 1, 1), right, 1, -1)
                else:
                    row = row_times(row_times(row, force, -1, 1), right, 1, 1)
                for part in range(2):
                    for j in range(3):
                        at = pl.ds((group * MAT + part * 9 + i * 3 + j) * 8, 8)
                        acc[at, :] = acc[at, :] + row[part][j]

    acc[...] = jnp.zeros_like(acc)
    lax.fori_loop(0, 6, lambda step, _: (term(step, False), 0)[1], 0)
    own = 24 * TILE
    for group, (top, bottom) in enumerate(PAIRS):
        near_sum = pole_sum(x_tiles, own, own + (1 + 2 * group) * TILE, near)
        far_sum = pole_sum(x_tiles, own, own + (2 + 2 * group) * TILE, far)
        weight = jnp.where(upper, weight_ref[top], weight_ref[bottom])
        done = []
        for c in range(MAT):
            part, i, j = c // 9, c // 3 % 3, c % 3
            staple = acc[pl.ds((group * MAT + c) * 8, 8), :]
            done.append(near_sum[part][i][j] + far_sum[part][i][j] + weight * staple)
        for c in range(0, MAT, 2):
            first, second = done[c], done[c + 1]
            out_ref[pl.ds((top * MAT + c) * 4, 8), :] = jnp.where(upper, first, pltpu.roll(second, 4, 0))
            out_ref[pl.ds((bottom * MAT + c) * 4, 8), :] = jnp.where(upper, pltpu.roll(first, 4, 0), second)


def on_device(pole_vectors, gauge_links, pole_coeff, naik_coeff, staple_weight):
    t_size = lax.axis_size("ta")
    z_size = lax.axis_size("gz") * lax.axis_size("gy")
    plan = halo_plan(t_size)
    vmem = pl.BlockSpec(memory_space=pltpu.VMEM)
    smem = pl.BlockSpec(memory_space=pltpu.SMEM)
    sizes = [block_rows(items)[1] for _, items in plan]
    packed = pl.pallas_call(
        functools.partial(pack_kernel, plan),
        out_shape=[
            jax.ShapeDtypeStruct((rows, LANES), F32) for rows in [4 * VEC, 16 * SLOT] + sizes
        ],
        in_specs=[vmem] * 2,
        out_specs=[vmem] * (2 + len(plan)),
        scratch_shapes=[pltpu.VMEM((4 * 4 * MAT, LANES), F32)],
        name="pack_halos",
    )(pole_vectors.reshape((4 * VEC, LANES)), gauge_links.reshape((16 * MAT, LANES)))
    local, sends = packed[:2], packed[2:]
    received = []
    for ((dt, dz), _), value in zip(plan, sends):
        if dt == 0:
            axes = ("gz", "gy")
            pairs = [((i + dz) % z_size, i) for i in range(z_size)]
        elif dz == 0:
            axes = "ta"
            pairs = [((j + dt) % t_size, j) for j in range(t_size)]
        else:
            axes = ("gz", "ta", "gy")
            halves = lax.axis_size("gy")

            def index(j, i):
                return ((i // halves) * t_size + j) * halves + i % halves

            pairs = [
                (index((j + dt) % t_size, (i + dz) % z_size), index(j, i))
                for j in range(t_size)
                for i in range(z_size)
            ]
        received.append(lax.ppermute(value, axes, pairs))
    names = [to for to, _ in plan]
    where = {to: block_rows(items)[0] for to, items in plan}
    x_fields, u_fields = tile_fields()
    force = pl.pallas_call(
        functools.partial(main_kernel, names, where, t_size),
        out_shape=jax.ShapeDtypeStruct((16 * MAT, LANES), F32),
        in_specs=[smem] * 3 + [vmem] * (2 + len(plan)),
        out_specs=vmem,
        scratch_shapes=[
            pltpu.VMEM((len(x_fields) * TILE, LANES), F32),
            pltpu.VMEM((len(u_fields) * TILE, LANES), F32),
            pltpu.VMEM((2 * MAT * 8, LANES), F32),
        ],
        compiler_params=pltpu.CompilerParams(vmem_limit_bytes=32 * 1024 * 1024),
        name="force",
    )(pole_coeff, naik_coeff, staple_weight, *local, *received)
    return force.reshape(gauge_links.shape)


def solution(mesh):
    return jax.shard_map(
        on_device,
        mesh=mesh,
        in_specs=(
            P("ens", None, None, "ta", ("gz", "gy"), None),
            P("ens", None, None, None, "ta", ("gz", "gy"), None),
            P(),
            P(),
            P(),
        ),
        out_specs=P("ens", None, None, None, "ta", ("gz", "gy"), None),
        check_vma=False,
    )
```

time: 159 us -> 27.7 us (0.17)
  the two profiles are of different devices: /device:TPU:1 before, /device:TPU:0 now
where the time goes in v1:
time: 27.7 us; the launch traced here: 27.5 us
  starting transfers between devices  10.1 us (36%)
  Pallas kernels  8.84 us (32%)
  waiting for transfers between devices  6.17 us (22%)
  local copies, waits for them, and re-layouts  2.39 us (9%)
    ppermute x6, starting transfers between devices, on_device(): received.append(lax.ppermute(value, axes, pairs))  10.1 us
    pallas_call x1, Pallas kernels, on_device(): pl.pallas_call(functools.partial(main_kernel, names, where, t_size), out_...  7.08 us
    ppermute x6, waiting for transfers between devices, on_device(): received.append(lax.ppermute(value, axes, pairs))  6.17 us
    unnamed x10, local copies, waits for them, and re-layouts  2.39 us
    pallas_call x1, Pallas kernels, on_device(): pl.pallas_call(functools.partial(pack_kernel, plan), out_shape=[jax.Shape...  1.76 us
  transfers between devices with their start and end apart: 6, of which 1 were waited for; matrix products, arithmetic and copies ran while one was open for 0% of the time, Pallas kernels for 0%

profile of v1, /device:TPU:0, one launch (start us, length us, event | category | flops | bytes accessed | tf_op | source)
XLA Modules:
  0.0 27.5 jit_solution(6279809572587546696)
XLA Ops:
  0.0 1.8 %pack_halos.1 = (f32[96,128]{1,0:T(8,128)}, f32[384,128]{1,0:T(8,128)}, f32[208,128]{1,0:T(8,128)}, f32[48,128]{1,0:T(8,128)}, f32[88,128]{1,0:T(8,128)}, /*inde...) custom-call(f32[96,128]{1,0:T(8,128)} %bitcast.4, bf16[288,128]{1,0:T(8,128)(2,1)} %bitcast.3), custom_call_target="tpu_custom_call" | custom-call | tf_op jit(solution)/shard_map/pack_halos/pallas_call | solution.py:278
  1.8 2.9 %collective-permute-start.3 = (f32[240,128]{1,0:T(8,128)}, f32[240,128]{1,0:T(8,128)S(1)}, u32[]{:S(2)}, u32[]{:S(2)}) collective-permute-start(f32[240,128]{1,0:T(8,128)} %get-tuple-element.18), channel_id=1, source_target_pairs={{2,0},{0,2},{3,1},{1,3},{6,4},{4,6},{7,5},{5,7},{10,8},{8,10},{11,... | collective-permute-start | bytes 368648 | tf_op jit(solution)/shard_map/ppermute | solution.py:309
  4.7 2.8 %collective-permute-start = (f32[208,128]{1,0:T(8,128)}, f32[208,128]{1,0:T(8,128)S(1)}, u32[]{:S(2)}, u32[]{:S(2)}) collective-permute-start(f32[208,128]{1,0:T(8,128)} %get-tuple-element.15), channel_id=1, source_target_pairs={{1,0},{4,1},{5,4},{8,5},{9,8},{12,9},{13,12},{0,13},{3,2},{6,3},{7... | collective-permute-start | bytes 319496 | tf_op jit(solution)/shard_map/ppermute | solution.py:309
  7.5 0.8 %collective-permute-start.1 = (f32[48,128]{1,0:T(8,128)}, f32[48,128]{1,0:T(8,128)S(1)}, u32[]{:S(2)}, u32[]{:S(2)}) collective-permute-start(f32[48,128]{1,0:T(8,128)} %get-tuple-element.16), channel_id=1, source_target_pairs={{4,0},{5,1},{8,4},{9,5},{12,8},{13,9},{0,12},{1,13},{6,2},{7,3},{1... | collective-permute-start | bytes 73736 | tf_op jit(solution)/shard_map/ppermute | solution.py:309
  8.3 0.2 collective-permute-start.2
  8.5 3.3 %collective-permute-start.4 = (f32[72,128]{1,0:T(8,128)}, f32[72,128]{1,0:T(8,128)S(1)}, u32[]{:S(2)}, u32[]{:S(2)}) collective-permute-start(f32[72,128]{1,0:T(8,128)} %get-tuple-element.19), channel_id=1, source_target_pairs={{3,0},{6,1},{7,4},{10,5},{11,8},{14,9},{15,12},{2,13},{1,2},{4,3},... | collective-permute-start | bytes 110600 | tf_op jit(solution)/shard_map/ppermute | solution.py:309
  11.8 0.0 collective-permute-done.1.rest_1_
  11.8 0.0 collective-permute-start.5
  11.8 6.2 %collective-permute-done.5.rest_5_ = f32[48,128]{1,0:T(8,128)S(1)} collective-permute-done((f32[48,128]{1,0:T(8,128)}, f32[48,128]{1,0:T(8,128)S(1)}, u32[]{:S(2)}, u32[]{:S(2)}) %collective-permute-start.5) | collective-permute-done | bytes 24608 | tf_op jit(solution)/shard_map/ppermute | solution.py:309
  18.0 0.0 collective-permute-done.4.rest_4_
  18.0 0.0 collective-permute-done.2.rest_2_
  18.0 0.0 collective-permute-done.rest_0_
  18.0 0.0 collective-permute-done.3.rest_3_
  18.0 0.0 copy-start.2
  18.0 0.0 copy-start.3
  18.0 0.0 copy-start.4
  18.0 0.6 %copy-done.2 = f32[4]{0:T(128)S(1)} copy-done((f32[4]{0:T(128)S(1)}, f32[4]{0:T(128)}, u32[]{:S(2)}) %copy-start.2) | copy-done | bytes 40
  18.7 0.0 copy-done.3
  18.7 0.0 copy-done.4
  18.7 0.0 copy-start
  18.7 0.9 %copy-done = f32[384,128]{1,0:T(8,128)S(1)} copy-done((f32[384,128]{1,0:T(8,128)S(1)}, f32[384,128]{1,0:T(8,128)}, u32[]{:S(2)}) %copy-start) | copy-done | bytes 196632
  19.6 0.0 copy-start.1
  19.6 0.8 %copy-done.1 = f32[96,128]{1,0:T(8,128)S(1)} copy-done((f32[96,128]{1,0:T(8,128)S(1)}, f32[96,128]{1,0:T(8,128)}, u32[]{:S(2)}) %copy-start.1) | copy-done | bytes 49176
  20.4 7.1 %force.1 = f32[288,128]{1,0:T(8,128)} custom-call(f32[4]{0:T(128)S(1)} %copy-done.2, f32[4]{0:T(128)S(1)} %copy-done.3, f32[4]{0:T(128)S(1)} %copy-done.4, f32[96,128]{1,0:T(8,128)S(1)} %copy-done.1, f32[384,128]{1,0:T(8,128)S(1)} %copy-done, f32[208,128]{1,0:T(8,128)S(1)} %collective-permute-done.rest_0_, f32[48,128]{1,0:T(8,128)S(1)} %collective-permute-done.1.rest_1_, ...), custom_call_target="tpu_custom_call" | custom-call | tf_op jit(solution)/shard_map/force/pallas_call | solution.py:313
Async XLA Ops:
  1.8 16.2 %collective-permute-start.3 = (f32[240,128]{1,0:T(8,128)}, f32[240,128]{1,0:T(8,128)S(1)}, u32[]{:S(2)}, u32[]{:S(2)}) collective-permute-start(f32[240,128]{1,0:T(8,128)} %get-tuple-element.18), channel_id=1, source_target_pairs={{2,0},{0,2},{3,1},{1,3},{6,4},{4,6},{7,5},{5,7},{10,8},{8,10},{11,... | collective-permute-start | bytes 368648 | tf_op jit(solution)/shard_map/ppermute | solution.py:309
  4.7 13.3 %collective-permute-start = (f32[208,128]{1,0:T(8,128)}, f32[208,128]{1,0:T(8,128)S(1)}, u32[]{:S(2)}, u32[]{:S(2)}) collective-permute-start(f32[208,128]{1,0:T(8,128)} %get-tuple-element.15), channel_id=1, source_target_pairs={{1,0},{4,1},{5,4},{8,5},{9,8},{12,9},{13,12},{0,13},{3,2},{6,3},{7... | collective-permute-start | bytes 319496 | tf_op jit(solution)/shard_map/ppermute | solution.py:309
  7.5 4.4 %collective-permute-start.1 = (f32[48,128]{1,0:T(8,128)}, f32[48,128]{1,0:T(8,128)S(1)}, u32[]{:S(2)}, u32[]{:S(2)}) collective-permute-start(f32[48,128]{1,0:T(8,128)} %get-tuple-element.16), channel_id=1, source_target_pairs={{4,0},{5,1},{8,4},{9,5},{12,8},{13,9},{0,12},{1,13},{6,2},{7,3},{1... | collective-permute-start | bytes 73736 | tf_op jit(solution)/shard_map/ppermute | solution.py:309
  8.3 9.7 %collective-permute-start.2 = (f32[88,128]{1,0:T(8,128)}, f32[88,128]{1,0:T(8,128)S(1)}, u32[]{:S(2)}, u32[]{:S(2)}) collective-permute-start(f32[88,128]{1,0:T(8,128)} %get-tuple-element.17), channel_id=1, source_target_pairs={{13,0},{0,1},{1,4},{4,5},{5,8},{8,9},{9,12},{12,13},{15,2},{2,3},{... | collective-permute-start | bytes 135176 | tf_op jit(solution)/shard_map/ppermute | solution.py:309
  8.5 9.5 %collective-permute-start.4 = (f32[72,128]{1,0:T(8,128)}, f32[72,128]{1,0:T(8,128)S(1)}, u32[]{:S(2)}, u32[]{:S(2)}) collective-permute-start(f32[72,128]{1,0:T(8,128)} %get-tuple-element.19), channel_id=1, source_target_pairs={{3,0},{6,1},{7,4},{10,5},{11,8},{14,9},{15,12},{2,13},{1,2},{4,3},... | collective-permute-start | bytes 110600 | tf_op jit(solution)/shard_map/ppermute | solution.py:309
  11.8 6.2 %collective-permute-start.5 = (f32[48,128]{1,0:T(8,128)}, f32[48,128]{1,0:T(8,128)S(1)}, u32[]{:S(2)}, u32[]{:S(2)}) collective-permute-start(f32[48,128]{1,0:T(8,128)} %get-tuple-element.20), channel_id=1, source_target_pairs={{15,0},{2,1},{3,4},{6,5},{7,8},{10,9},{11,12},{14,13},{13,2},{0,3}... | collective-permute-start | bytes 73736 | tf_op jit(solution)/shard_map/ppermute | solution.py:309
  18.0 0.7 %copy-start.2 = (f32[4]{0:T(128)S(1)}, f32[4]{0:T(128)}, u32[]{:S(2)}) copy-start(f32[4]{0:T(128)} %near_ref.1) | copy-start | bytes 52
  18.0 0.7 %copy-start.3 = (f32[4]{0:T(128)S(1)}, f32[4]{0:T(128)}, u32[]{:S(2)}) copy-start(f32[4]{0:T(128)} %far_ref.1) | copy-start | bytes 52
  18.0 0.7 %copy-start.4 = (f32[4]{0:T(128)S(1)}, f32[4]{0:T(128)}, u32[]{:S(2)}) copy-start(f32[4]{0:T(128)} %weight_ref.1) | copy-start | bytes 52
  18.7 0.9 %copy-start = (f32[384,128]{1,0:T(8,128)S(1)}, f32[384,128]{1,0:T(8,128)}, u32[]{:S(2)}) copy-start(f32[384,128]{1,0:T(8,128)} %get-tuple-element.14.ul_ref) | copy-start | bytes 589828
  19.6 0.8 %copy-start.1 = (f32[96,128]{1,0:T(8,128)S(1)}, f32[96,128]{1,0:T(8,128)}, u32[]{:S(2)}) copy-start(f32[96,128]{1,0:T(8,128)} %get-tuple-element.13.xl_ref) | copy-start | bytes 147460

commit v2 on v1

--- a/solution.py
+++ b/solution.py
@@ -82,8 +82,14 @@
         done += size
 
 
-def pack_kernel(plan, x_ref, u_ref, xl_ref, ul_ref, *rest):
+def pack_kernel(plan, near_ref, far_ref, weight_ref, x_ref, u_ref, scale_ref, xl_ref, ul_ref, *rest):
     outs, wide = rest[:-1], rest[-1]
+    upper = lax.broadcasted_iota(jnp.int32, (8, LANES), 0) < 4
+    for p in range(NP):
+        scale_ref[pl.ds(8 * p, 8), :] = jnp.full((8, LANES), near_ref[p], F32)
+        scale_ref[pl.ds(8 * (NP + p), 8), :] = jnp.full((8, LANES), far_ref[p], F32)
+    for group, (top, bottom) in enumerate(PAIRS):
+        scale_ref[pl.ds(8 * (2 * NP + group), 8), :] = jnp.where(upper, weight_ref[top], weight_ref[bottom])
     wide[...] = u_ref[...].astype(F32)
     for r in range(4):
         for k in range(3):
@@ -218,14 +224,14 @@
     return result
 
 
-def main_kernel(names, where, t_size, near_ref, far_ref, weight_ref, xl_ref, ul_ref, *rest):
+def main_kernel(names, where, t_size, scale_ref, xl_ref, ul_ref, *rest):
     received = rest[: len(names)]
     out_ref, x_tiles, u_tiles, acc = rest[len(names) :]
     buffers = {("local", "x"): xl_ref, ("local", "u"): ul_ref}
     buffers.update(zip(names, received))
     build_fields(buffers, where, t_size, x_tiles, u_tiles)
-    near = [near_ref[p] for p in range(NP)]
-    far = [far_ref[p] for p in range(NP)]
+    near = [scale_ref[pl.ds(8 * p, 8), :] for p in range(NP)]
+    far = [scale_ref[pl.ds(8 * (NP + p), 8), :] for p in range(NP)]
     upper = lax.broadcasted_iota(jnp.int32, (8, LANES), 0) < 4
 
     def term(step, first):
@@ -256,7 +262,7 @@
     for group, (top, bottom) in enumerate(PAIRS):
         near_sum = pole_sum(x_tiles, own, own + (1 + 2 * group) * TILE, near)
         far_sum = pole_sum(x_tiles, own, own + (2 + 2 * group) * TILE, far)
-        weight = jnp.where(upper, weight_ref[top], weight_ref[bottom])
+        weight = scale_ref[pl.ds(8 * (2 * NP + group), 8), :]
         done = []
         for c in range(MAT):
             part, i, j = c // 9, c // 3 % 3, c % 3
@@ -278,14 +284,15 @@
     packed = pl.pallas_call(
         functools.partial(pack_kernel, plan),
         out_shape=[
-            jax.ShapeDtypeStruct((rows, LANES), F32) for rows in [4 * VEC, 16 * SLOT] + sizes
+            jax.ShapeDtypeStruct((rows, LANES), F32) for rows in [8 * (2 * NP + 2), 4 * VEC, 16 * SLOT] + sizes
         ],
-        in_specs=[vmem] * 2,
-        out_specs=[vmem] * (2 + len(plan)),
+        in_specs=[smem] * 3 + [vmem] * 2,
+        out_specs=[vmem] * (3 + len(plan)),
         scratch_shapes=[pltpu.VMEM((4 * 4 * MAT, LANES), F32)],
+        compiler_params=pltpu.CompilerParams(vmem_limit_bytes=4 * 1024 * 1024),
         name="pack_halos",
-    )(pole_vectors.reshape((4 * VEC, LANES)), gauge_links.reshape((16 * MAT, LANES)))
-    local, sends = packed[:2], packed[2:]
+    )(pole_coeff, naik_coeff, staple_weight, pole_vectors.reshape((4 * VEC, LANES)), gauge_links.reshape((16 * MAT, LANES)))
+    local, sends = packed[:3], packed[3:]
     received = []
     for ((dt, dz), _), value in zip(plan, sends):
         if dt == 0:
@@ -313,16 +320,16 @@
     force = pl.pallas_call(
         functools.partial(main_kernel, names, where, t_size),
         out_shape=jax.ShapeDtypeStruct((16 * MAT, LANES), F32),
-        in_specs=[smem] * 3 + [vmem] * (2 + len(plan)),
+        in_specs=[vmem] * (3 + len(plan)),
         out_specs=vmem,
         scratch_shapes=[
             pltpu.VMEM((len(x_fields) * TILE, LANES), F32),
             pltpu.VMEM((len(u_fields) * TILE, LANES), F32),
             pltpu.VMEM((2 * MAT * 8, LANES), F32),
         ],
-        compiler_params=pltpu.CompilerParams(vmem_limit_bytes=32 * 1024 * 1024),
+        compiler_params=pltpu.CompilerParams(vmem_limit_bytes=12 * 1024 * 1024),
         name="force",
-    )(pole_coeff, naik_coeff, staple_weight, *local, *received)
+    )(*local, *received)
     return force.reshape(gauge_links.shape)
 
 

time: 27.7 us -> 25.8 us (0.931)
  Pallas kernels: 8.84 us -> 7.15 us
    pallas_call x1, Pallas kernels: 1.76 us -> 0.62 us  [on_device(): pl.pallas_call(functools.partial(pack_kernel, plan), out_shape=[jax.Shape...]
    pallas_call x1, Pallas kernels: 7.08 us -> 6.53 us  [on_device(): pl.pallas_call(functools.partial(main_kernel, names, where, t_size), out_...]
where the time goes in v2:
time: 25.8 us; the launch traced here: 25.6 us
  starting transfers between devices  10.1 us (39%)
  Pallas kernels  7.15 us (28%)
  waiting for transfers between devices  5.96 us (23%)
  local copies, waits for them, and re-layouts  2.37 us (9%)
    ppermute x6, starting transfers between devices, on_device(): received.append(lax.ppermute(value, axes, pairs))  10.1 us
    pallas_call x1, Pallas kernels, on_device(): pl.pallas_call(functools.partial(main_kernel, names, where, t_size), out_...  6.53 us
    ppermute x6, waiting for transfers between devices, on_device(): received.append(lax.ppermute(value, axes, pairs))  5.96 us
    unnamed x10, local copies, waits for them, and re-layouts  2.37 us
    pallas_call x1, Pallas kernels, on_device(): pl.pallas_call(functools.partial(pack_kernel, plan), out_shape=[jax.Shape...  0.62 us
  transfers between devices with their start and end apart: 6, of which 1 were waited for; matrix products, arithmetic and copies ran while one was open for 0% of the time, Pallas kernels for 0%

profile of v2, /device:TPU:0, one launch (start us, length us, event | category | flops | bytes accessed | tf_op | source)
XLA Modules:
  0.0 25.6 jit_solution(8883712888611556543)
XLA Ops:
  0.0 0.0 copy-start.2
  0.0 0.0 copy-start.3
  0.0 0.0 copy-start.4
  0.0 0.6 %copy-done.2 = f32[4]{0:T(128)S(1)} copy-done((f32[4]{0:T(128)S(1)}, f32[4]{0:T(128)}, u32[]{:S(2)}) %copy-start.2) | copy-done | bytes 40
  0.7 0.0 copy-done.3
  0.7 0.0 copy-done.4
  0.7 0.0 copy-start
  0.7 0.9 %copy-done = bf16[4,2,3,3,2,2,128]{6,5,4,3,2,1,0:T(2,128)(2,1)S(1)} copy-done((bf16[4,2,3,3,2,2,128]{6,5,4,3,2,1,0:T(2,128)(2,1)S(1)}, bf16[4,2,3,3,2,2,128]{6,5,4,3,2,1,0:T(2,128)(2,1)}, u32[]{:S(2)}) %copy-start) | copy-done | bytes 73752
  1.6 0.0 copy-start.1
  1.6 0.8 %copy-done.1 = f32[4,2,3,2,2,128]{5,4,3,2,1,0:T(2,128)S(1)} copy-done((f32[4,2,3,2,2,128]{5,4,3,2,1,0:T(2,128)S(1)}, f32[4,2,3,2,2,128]{5,4,3,2,1,0:T(2,128)}, u32[]{:S(2)}) %copy-start.1) | copy-done | bytes 49176
  2.4 0.6 %pack_halos.1 = (f32[80,128]{1,0:T(8,128)S(1)}, f32[96,128]{1,0:T(8,128)S(1)}, f32[384,128]{1,0:T(8,128)S(1)}, f32[208,128]{1,0:T(8,128)S(1)}, f32[48,128]{1,0:T...) custom-call(f32[4]{0:T(128)S(1)} %copy-done.2, ...), custom_call_target="tpu_custom_call" | custom-call | tf_op jit(solution)/shard_map/pack_halos/pallas_call | solution.py:284
  3.0 3.0 %collective-permute-start.3 = (f32[240,128]{1,0:T(8,128)S(1)}, f32[240,128]{1,0:T(8,128)S(1)}, u32[]{:S(2)}, u32[]{:S(2)}) collective-permute-start(f32[240,128]{1,0:T(8,128)S(1)} %get-tuple-element.20), channel_id=1, source_target_pairs={{2,0},{0,2},{3,1},{1,3},{6,4},{4,6},{7,5},{5,7},{10,8},{8,10},{11,... | collective-permute-start | bytes 368648 | tf_op jit(solution)/shard_map/ppermute | solution.py:316
  6.0 2.8 %collective-permute-start = (f32[208,128]{1,0:T(8,128)S(1)}, f32[208,128]{1,0:T(8,128)S(1)}, u32[]{:S(2)}, u32[]{:S(2)}) collective-permute-start(f32[208,128]{1,0:T(8,128)S(1)} %get-tuple-element.17), channel_id=1, source_target_pairs={{1,0},{4,1},{5,4},{8,5},{9,8},{12,9},{13,12},{0,13},{3,2},{6,3},{7... | collective-permute-start | bytes 319496 | tf_op jit(solution)/shard_map/ppermute | solution.py:316
  8.8 0.8 %collective-permute-start.1 = (f32[48,128]{1,0:T(8,128)S(1)}, f32[48,128]{1,0:T(8,128)S(1)}, u32[]{:S(2)}, u32[]{:S(2)}) collective-permute-start(f32[48,128]{1,0:T(8,128)S(1)} %get-tuple-element.18), channel_id=1, source_target_pairs={{4,0},{5,1},{8,4},{9,5},{12,8},{13,9},{0,12},{1,13},{6,2},{7,3},{1... | collective-permute-start | bytes 73736 | tf_op jit(solution)/shard_map/ppermute | solution.py:316
  9.6 0.2 collective-permute-start.2
  9.8 3.3 %collective-permute-start.4 = (f32[72,128]{1,0:T(8,128)S(1)}, f32[72,128]{1,0:T(8,128)S(1)}, u32[]{:S(2)}, u32[]{:S(2)}) collective-permute-start(f32[72,128]{1,0:T(8,128)S(1)} %get-tuple-element.21), channel_id=1, source_target_pairs={{3,0},{6,1},{7,4},{10,5},{11,8},{14,9},{15,12},{2,13},{1,2},{4,3},... | collective-permute-start | bytes 110600 | tf_op jit(solution)/shard_map/ppermute | solution.py:316
  13.1 0.0 collective-permute-done.1.rest_1_
  13.1 0.0 collective-permute-start.5
  13.1 5.9 %collective-permute-done.5.rest_5_ = f32[48,128]{1,0:T(8,128)S(1)} collective-permute-done((f32[48,128]{1,0:T(8,128)S(1)}, f32[48,128]{1,0:T(8,128)S(1)}, u32[]{:S(2)}, u32[]{:S(2)}) %collective-permute-start.5) | collective-permute-done | bytes 24608 | tf_op jit(solution)/shard_map/ppermute | solution.py:316
  19.1 0.0 collective-permute-done.4.rest_4_
  19.1 0.0 collective-permute-done.2.rest_2_
  19.1 0.0 collective-permute-done.rest_0_
  19.1 0.0 collective-permute-done.3.rest_3_
  19.1 6.5 %force.1 = f32[288,128]{1,0:T(8,128)} custom-call(f32[80,128]{1,0:T(8,128)S(1)} %get-tuple-element.14.scale_ref, f32[96,128]{1,0:T(8,128)S(1)} %get-tuple-element.15.xl_ref, f32[384,128]{1,0:T(8,128)S(1)} %get-tuple-element.16.ul_ref, f32[208,128]{1,0:T(8,128)S(1)} %collective-permute-done.rest_0_, f32[48,128]{1,0:T(8,128)S(1)} %collective-permute-done.1.rest_1_, ...), custom_call_target="tpu_custom_call" | custom-call | tf_op jit(solution)/shard_map/force/pallas_call | solution.py:320
Async XLA Ops:
  0.0 0.7 %copy-start.2 = (f32[4]{0:T(128)S(1)}, f32[4]{0:T(128)}, u32[]{:S(2)}) copy-start(f32[4]{0:T(128)} %near_ref.1) | copy-start | bytes 52
  0.0 0.7 %copy-start.3 = (f32[4]{0:T(128)S(1)}, f32[4]{0:T(128)}, u32[]{:S(2)}) copy-start(f32[4]{0:T(128)} %far_ref.1) | copy-start | bytes 52
  0.0 0.7 %copy-start.4 = (f32[4]{0:T(128)S(1)}, f32[4]{0:T(128)}, u32[]{:S(2)}) copy-start(f32[4]{0:T(128)} %weight_ref.1) | copy-start | bytes 52
  0.7 0.9 %copy-start = (bf16[4,2,3,3,2,2,128]{6,5,4,3,2,1,0:T(2,128)(2,1)S(1)}, bf16[4,2,3,3,2,2,128]{6,5,4,3,2,1,0:T(2,128)(2,1)}, u32[]{:S(2)}) copy-start(bf16[4,2,3,3,2,2,128]{6,5,4,3,2,1,0:T(2,128)(2,1)} %param.6) | copy-start | bytes 221188
  1.6 0.8 %copy-start.1 = (f32[4,2,3,2,2,128]{5,4,3,2,1,0:T(2,128)S(1)}, f32[4,2,3,2,2,128]{5,4,3,2,1,0:T(2,128)}, u32[]{:S(2)}) copy-start(f32[4,2,3,2,2,128]{5,4,3,2,1,0:T(2,128)} %param.5) | copy-start | bytes 147460
  3.0 16.1 %collective-permute-start.3 = (f32[240,128]{1,0:T(8,128)S(1)}, f32[240,128]{1,0:T(8,128)S(1)}, u32[]{:S(2)}, u32[]{:S(2)}) collective-permute-start(f32[240,128]{1,0:T(8,128)S(1)} %get-tuple-element.20), channel_id=1, source_target_pairs={{2,0},{0,2},{3,1},{1,3},{6,4},{4,6},{7,5},{5,7},{10,8},{8,10},{11,... | collective-permute-start | bytes 368648 | tf_op jit(solution)/shard_map/ppermute | solution.py:316
  6.0 13.1 %collective-permute-start = (f32[208,128]{1,0:T(8,128)S(1)}, f32[208,128]{1,0:T(8,128)S(1)}, u32[]{:S(2)}, u32[]{:S(2)}) collective-permute-start(f32[208,128]{1,0:T(8,128)S(1)} %get-tuple-element.17), channel_id=1, source_target_pairs={{1,0},{4,1},{5,4},{8,5},{9,8},{12,9},{13,12},{0,13},{3,2},{6,3},{7... | collective-permute-start | bytes 319496 | tf_op jit(solution)/shard_map/ppermute | solution.py:316
  8.8 4.4 %collective-permute-start.1 = (f32[48,128]{1,0:T(8,128)S(1)}, f32[48,128]{1,0:T(8,128)S(1)}, u32[]{:S(2)}, u32[]{:S(2)}) collective-permute-start(f32[48,128]{1,0:T(8,128)S(1)} %get-tuple-element.18), channel_id=1, source_target_pairs={{4,0},{5,1},{8,4},{9,5},{12,8},{13,9},{0,12},{1,13},{6,2},{7,3},{1... | collective-permute-start | bytes 73736 | tf_op jit(solution)/shard_map/ppermute | solution.py:316
  9.6 9.5 %collective-permute-start.2 = (f32[88,128]{1,0:T(8,128)S(1)}, f32[88,128]{1,0:T(8,128)S(1)}, u32[]{:S(2)}, u32[]{:S(2)}) collective-permute-start(f32[88,128]{1,0:T(8,128)S(1)} %get-tuple-element.19), channel_id=1, source_target_pairs={{13,0},{0,1},{1,4},{4,5},{5,8},{8,9},{9,12},{12,13},{15,2},{2,3},{... | collective-permute-start | bytes 135176 | tf_op jit(solution)/shard_map/ppermute | solution.py:316
  9.8 9.2 %collective-permute-start.4 = (f32[72,128]{1,0:T(8,128)S(1)}, f32[72,128]{1,0:T(8,128)S(1)}, u32[]{:S(2)}, u32[]{:S(2)}) collective-permute-start(f32[72,128]{1,0:T(8,128)S(1)} %get-tuple-element.21), channel_id=1, source_target_pairs={{3,0},{6,1},{7,4},{10,5},{11,8},{14,9},{15,12},{2,13},{1,2},{4,3},... | collective-permute-start | bytes 110600 | tf_op jit(solution)/shard_map/ppermute | solution.py:316
  13.1 5.9 %collective-permute-start.5 = (f32[48,128]{1,0:T(8,128)S(1)}, f32[48,128]{1,0:T(8,128)S(1)}, u32[]{:S(2)}, u32[]{:S(2)}) collective-permute-start(f32[48,128]{1,0:T(8,128)S(1)} %get-tuple-element.22), channel_id=1, source_target_pairs={{15,0},{2,1},{3,4},{6,5},{7,8},{10,9},{11,12},{14,13},{13,2},{0,3}... | collective-permute-start | bytes 73736 | tf_op jit(solution)/shard_map/ppermute | solution.py:316

commit v3 on v1

v3 whole, which is shorter than its diff:
```python
import collections
import functools

import jax
import jax.numpy as jnp
from jax import lax
from jax.experimental import pallas as pl
from jax.experimental.pallas import tpu as pltpu
from jax.sharding import PartitionSpec as P

NX = 8
NY = 16
LANES = NX * NY
NP = 4
F32 = jnp.float32
REGS = {"x": NP * 3, "u": 9}
UNIT = ((1, 0, 0, 0), (0, 1, 0, 0), (0, 0, 1, 0), (0, 0, 0, 1))
ZERO = (0, 0, 0, 0)
SITES = ((0, 0), (0, 1), (1, 0), (1, 1))
NEAR_TERMS = ((0, ((0, 1), (1, 0))), (0, ((0, 2), (1, 2))), (1, ((2, 0), (2, 1))))
FAR_TERMS = ((0, ((0, 3), (1, 3))), (1, ((3, 0), (3, 1))), (2, ((2, 3), (3, 2))))


def plus(left, right, scale=1):
    return tuple(a + scale * b for a, b in zip(left, right))


class Message:
    def __init__(self):
        self.places = collections.OrderedDict()
        self.count = 0

    def add_full(self, kind, n):
        for k in range(REGS[kind]):
            for t, z in SITES:
                self.places[0, kind, n, k, t, z] = (self.count, 2 * t + z)
            self.count += 1

    def add_halves(self, entries, axis):
        half = -(-len(entries) // 2)
        for index, (kind, n, k, layer) in enumerate(entries):
            reg, part = self.count + index % half, index // half
            for other in range(2):
                t, z = (layer, other) if axis == "t" else (other, layer)
                slot = 2 * part + other if axis == "t" else 2 * other + part
                self.places[0, kind, n, k, t, z] = (reg, slot)
        self.count += half

    def add_single(self, entries):
        quarter = -(-len(entries) // 4)
        for index, entry in enumerate(entries):
            self.places[entry] = (self.count + index % quarter, index // quarter)
        self.count += quarter

    def by_register(self):
        found = [[None] * 4 for _ in range(self.count)]
        for item, (reg, slot) in self.places.items():
            found[reg][slot] = item
        return found


def regs_of(kind, directions, layer):
    return [(kind, n, k, layer) for n in directions for k in range(REGS[kind])]


def message_plan(t_size):
    plan = collections.OrderedDict()
    ahead = plan["z", 1] = Message()
    ahead.add_full("x", 0)
    ahead.add_halves(regs_of("u", (0, 1, 3), 0), "z")
    behind = plan["z", -1] = Message()
    behind.add_halves(regs_of("x", (0,), 1) + regs_of("u", (2,), 1), "z")
    second = plan["z", 2] = Message()
    second.add_halves(regs_of("x", (0,), 0), "z")
    halves, corners = collections.OrderedDict(), collections.OrderedDict()
    for dt, entries in (
        (1, regs_of("u", (0, 1, 2), 0)),
        (-1, regs_of("x", (0,), 1) + regs_of("u", (3,), 1)),
        (2, regs_of("x", (0,), 0)),
    ):
        if dt % t_size != 0:
            halves.setdefault(dt % t_size, []).extend(entries)
    for dt, entries in halves.items():
        message = plan["t", dt] = Message()
        if dt == 1:
            message.add_full("x", 0)
        held = {item[1:4] for item in message.places}
        message.add_halves([e for e in entries if e[:3] not in held], "t")
    for dt, entries in (
        (1, [(1, "x", 0, k, 0, 0) for k in range(REGS["x"])]),
        (1, [(-1, "x", 0, k, 0, 1) for k in range(REGS["x"])]),
        (1, [(-1, "u", 2, k, 0, 1) for k in range(REGS["u"])]),
        (-1, [(1, "x", 0, k, 1, 0) for k in range(REGS["x"])]),
        (-1, [(1, "u", 3, k, 1, 0) for k in range(REGS["u"])]),
    ):
        corners.setdefault(dt % t_size, []).extend(entries)
    for dt, entries in corners.items():
        plan["c", dt] = Message()
        plan["c", dt].add_single(entries)
    return plan


class Locator:
    def __init__(self, plan, t_size, buffers):
        self.plan, self.t_size, self.buffers = plan, t_size, buffers

    def local(self, kind, n, k, t, z):
        return ("own", kind), n * REGS[kind] + k, 2 * t + z

    def find(self, kind, n, k, t_at, z_at):
        (dt, t), (dz, z) = divmod(t_at, 2), divmod(z_at, 2)
        dt %= self.t_size
        if (dt, dz) == (0, 0):
            return self.local(kind, n, k, t, z)
        name = ("z", dz) if dt == 0 else ("t", dt) if dz == 0 else ("c", dt)
        item = (dz if name[0] == "c" else 0, kind, n, k, t, z)
        return (name,) + self.plan[name].places[item]

    def load(self, name, reg):
        return self.buffers[name][pl.ds(8 * reg, 8), :]

    def assemble(self, spots):
        groups = collections.OrderedDict()
        for r, spot in enumerate(spots):
            if spot is not None:
                groups.setdefault((spot[0], spot[1], r - spot[2]), []).append(r)
        row = lax.broadcasted_iota(jnp.int32, (8, LANES), 0) % 4
        result = None
        for (name, reg, move), rows in groups.items():
            value = self.load(name, reg)
            if move != 0:
                value = pltpu.roll(value, move % 8, 0)
            if result is None:
                result = value
            else:
                mask = functools.reduce(jnp.logical_or, [row == r for r in rows])
                result = jnp.where(mask, value, result)
        return result

    def field_register(self, kind, n, k, dt, dz):
        return self.assemble([self.find(kind, n, k, t + dt, z + dz) for t, z in SITES])


def lane_shifted(value, dx, dy):
    if dx != 0:
        x_at = lax.broadcasted_iota(jnp.int32, value.shape, 1) % NX
        beyond = (x_at + dx >= NX) | (x_at + dx < 0)
        main = pltpu.roll(value, (-dx) % LANES, 1)
        wrapped = pltpu.roll(value, (NX - dx if dx > 0 else -NX - dx) % LANES, 1)
        value = jnp.where(beyond, wrapped, main)
    if dy != 0:
        value = pltpu.roll(value, (-dy * NX) % LANES, 1)
    return value


def term_fields(halves, sign):
    here, ahead, left, right = [], [], [], []
    for m, n in halves:
        start = plus(ZERO, UNIT[n], sign)
        base = ZERO if sign > 0 else start
        here.append(("x", 0, start))
        ahead.append(("x", 0, plus(start, UNIT[m])))
        left.append(("u", n, base))
        right.append(("u", n, plus(base, UNIT[m])))
    return here, ahead, left, right


def needed_fields(terms, own):
    keys = collections.OrderedDict()
    for _, halves in terms:
        for sign in (1, -1):
            for pair in term_fields(halves, sign):
                keys.update((key, None) for key in pair)
    for m in own:
        for scale in (1, 3):
            keys["x", 0, plus(ZERO, UNIT[m], scale)] = None
    return [key for key in keys if key[2] != ZERO]


def lay_out(keys):
    rows, total = collections.OrderedDict(), 0
    for key in keys:
        rows[key] = total
        total += 8 * REGS[key[0]]
    return rows, total


def field_split():
    near = needed_fields(NEAR_TERMS, (0, 1, 2))
    far = needed_fields(FAR_TERMS, (3,))
    still = [key for key in far if key[2][3] == 0]
    shared = lay_out(still)
    first = lay_out([key for key in near if key not in shared[0]])
    second = lay_out([key for key in far if key not in shared[0]])
    return shared, first, second


def build_fields(locator, stores):
    groups = collections.OrderedDict()
    for ref, rows in stores:
        for (kind, n, disp), row in rows.items():
            shifts = groups.setdefault((kind, n, disp[3], disp[2]), collections.OrderedDict())
            shifts[disp[0], disp[1]] = (ref, row)
    for (kind, n, dt, dz), shifts in groups.items():
        for k in range(REGS[kind]):
            value = locator.field_register(kind, n, k, dt, dz)
            by_x = {0: value}
            for (dx, dy), (ref, row) in shifts.items():
                if dx not in by_x:
                    by_x[dx] = lane_shifted(value, dx, 0)
                ref[pl.ds(row + 8 * k, 8), :] = lane_shifted(by_x[dx], 0, dy)


class Fields:
    def __init__(self, own_x, own_u, stores):
        self.place = {("x", 0, ZERO): (own_x, 0)}
        for n in range(4):
            self.place["u", n, ZERO] = (own_u, 8 * REGS["u"] * n)
        for ref, rows in stores:
            for key, row in rows.items():
                self.place[key] = (ref, row)
        self.upper = lax.broadcasted_iota(jnp.int32, (8, LANES), 0) < 4

    def reg(self, key, k):
        ref, row = self.place[key]
        return ref[pl.ds(row + 8 * k, 8), :]

    def two_tiles(self, keys, k):
        top = self.reg(keys[0], k)
        turned_top = pltpu.roll(top, 4, 0)
        if keys[0] == keys[1]:
            low, turned_low = top, turned_top
        else:
            low = self.reg(keys[1], k)
            turned_low = pltpu.roll(low, 4, 0)
        return [jnp.where(self.upper, top, turned_low), jnp.where(self.upper, turned_top, low)]

    def vector(self, keys, pole):
        flat = [tile for k in range(3) for tile in self.two_tiles(keys, 3 * pole + k)]
        return [flat[:3], flat[3:]]

    def matrix(self, keys):
        flat = [tile for k in range(9) for tile in self.two_tiles(keys, k)]
        return [[flat[9 * c + 3 * i : 9 * c + 3 * i + 3] for i in range(3)] for c in range(2)]

    def compact_halves(self, first, second):
        top = jnp.where(self.upper, first, pltpu.roll(second, 4, 0))
        return top, jnp.where(self.upper, pltpu.roll(first, 4, 0), second)

    def compact_sum(self, first, second):
        kept = jnp.where(self.upper, first, second)
        return kept + pltpu.roll(jnp.where(self.upper, second, first), 4, 0)


def pole_sum(fields, here, ahead, scales):
    total = None
    for pole in range(NP):
        h = [[scales[pole] * v for v in part] for part in fields.vector(here, pole)]
        a = fields.vector(ahead, pole)
        real = [[a[0][i] * h[0][j] + a[1][i] * h[1][j] for j in range(3)] for i in range(3)]
        imag = [[a[1][i] * h[0][j] - a[0][i] * h[1][j] for j in range(3)] for i in range(3)]
        if total is None:
            total = [real, imag]
        else:
            total = [
                [[total[c][i][j] + new[i][j] for j in range(3)] for i in range(3)]
                for c, new in enumerate((real, imag))
            ]
    return total


def transposed(matrix):
    return [[[part[j][i] for j in range(3)] for i in range(3)] for part in matrix]


def row_times(row, right, row_sign, right_sign):
    result = [[], []]
    for j in range(3):
        real = imag = None
        for k in range(3):
            rr = row[0][k] * right[0][k][j]
            ii = row[1][k] * right[1][k][j]
            ri = row[0][k] * right[1][k][j]
            ir = row[1][k] * right[0][k][j]
            new_real = rr - ii if row_sign * right_sign > 0 else rr + ii
            if row_sign > 0 and right_sign > 0:
                new_imag = ri + ir
            elif row_sign > 0:
                new_imag = ir - ri
            else:
                new_imag = ri - ir
            real = new_real if real is None else real + new_real
            imag = new_imag if imag is None else imag + new_imag
        result[0].append(real)
        result[1].append(imag)
    return result


def add_terms(fields, terms, near, acc):
    started = set()
    for target, halves in terms:
        for sign in (1, -1):
            here, ahead, left, right = term_fields(halves, sign)
            force = pole_sum(fields, here, ahead, near)
            left = fields.matrix(left)
            right = fields.matrix(right)
            if sign > 0:
                right = transposed(right)
            else:
                left = transposed(left)
            rows = [row_times([left[0][i], left[1][i]], force, sign, 1) for i in range(3)]
            for i in range(3):
                row = row_times(rows[i], right, 1, -sign)
                for part in range(2):
                    for j in range(3):
                        at = pl.ds((target * 18 + part * 9 + i * 3 + j) * 8, 8)
                        new = row[part][j]
                        acc[at, :] = acc[at, :] + new if target in started else new
            started.add(target)


def acc_tile(acc, target, c):
    return acc[pl.ds((target * 18 + c) * 8, 8), :]


def scale_tiles(scale_ref):
    tiles = [scale_ref[pl.ds(8 * p, 8), :] for p in range(3 * NP)]
    return tiles[:NP], tiles[NP : 2 * NP], tiles[2 * NP :]


def own_force(fields, m, both):
    total = pole_sum(
        fields,
        [("x", 0, ZERO)] * 2,
        [("x", 0, UNIT[m]), ("x", 0, plus(ZERO, UNIT[m], 3))],
        both,
    )
    flat = [total[c][i][j] for c in range(2) for i in range(3) for j in range(3)]
    return [fields.compact_sum(flat[2 * k], flat[2 * k + 1]) for k in range(9)]


def pack_kernel(plan, names, near_in, far_in, weight_in, x_in, u_in, *rest):
    outs = rest[: len(names)]
    scale_ref, x_ref, u_ref, near_ref, far_ref, weight_ref, u_held, sems = rest[len(names) :]
    copies = [
        pltpu.make_async_copy(source, target, sems.at[index])
        for index, (source, target) in enumerate(
            ((u_in, u_held), (x_in, x_ref), (near_in, near_ref), (far_in, far_ref), (weight_in, weight_ref))
        )
    ]
    for copy in copies:
        copy.start()
    for copy in copies:
        copy.wait()
    u_ref[...] = u_held[...].astype(F32)
    locator = Locator(plan, 1, {("own", "x"): x_ref, ("own", "u"): u_ref})
    for name, out in zip(names, outs):
        for reg, items in enumerate(plan[name].by_register()):
            spots = [item and locator.local(*item[1:]) for item in items]
            out[pl.ds(8 * reg, 8), :] = locator.assemble(spots)
    upper = lax.broadcasted_iota(jnp.int32, (8, LANES), 0) < 4
    for p in range(NP):
        scale_ref[pl.ds(8 * p, 8), :] = jnp.full((8, LANES), near_ref[p], F32)
        scale_ref[pl.ds(8 * (NP + p), 8), :] = jnp.where(upper, near_ref[p], far_ref[p])
        scale_ref[pl.ds(8 * (2 * NP + p), 8), :] = jnp.full((8, LANES), weight_ref[p], F32)


def corner_kernel(plan, names, ahead_ref, behind_ref, *outs):
    locator = Locator(plan, 1, {("z", 1): ahead_ref, ("z", -1): behind_ref})
    for name, out in zip(names, outs):
        for reg, items in enumerate(plan[name].by_register()):
            spots = [
                item and (("z", item[0]),) + plan["z", item[0]].places[(0,) + item[1:]] for item in items
            ]
            out[pl.ds(8 * reg, 8), :] = locator.assemble(spots)


def near_kernel(plan, t_size, names, scale_ref, x_ref, u_ref, *rest):
    received = rest[: len(names)]
    shared_ref, part_ref, first_ref, acc = rest[len(names) :]
    buffers = {("own", "x"): x_ref, ("own", "u"): u_ref}
    buffers.update(zip(names, received))
    shared, first, _ = field_split()
    stores = [(shared_ref, shared[0]), (first_ref, first[0])]
    build_fields(Locator(plan, t_size, buffers), stores)
    fields = Fields(x_ref, u_ref, stores)
    near, both, weight = scale_tiles(scale_ref)
    add_terms(fields, NEAR_TERMS, near, acc)
    own = [own_force(fields, m, both) for m in range(3)]
    for k in range(9):
        staples = list(fields.compact_halves(acc_tile(acc, 0, 2 * k), acc_tile(acc, 0, 2 * k + 1)))
        staples.append(fields.compact_sum(acc_tile(acc, 1, 2 * k), acc_tile(acc, 1, 2 * k + 1)))
        for m in range(3):
            part_ref[pl.ds((9 * m + k) * 8, 8), :] = own[m][k] + weight[m] * staples[m]


def far_kernel(plan, t_size, names, scale_ref, x_ref, u_ref, shared_ref, part_ref, *rest):
    received = rest[: len(names)]
    out_ref, second_ref, acc = rest[len(names) :]
    buffers = {("own", "x"): x_ref, ("own", "u"): u_ref}
    buffers.update(zip(names, received))
    shared, _, second = field_split()
    build_fields(Locator(plan, t_size, buffers), [(second_ref, second[0])])
    fields = Fields(x_ref, u_ref, [(shared_ref, shared[0]), (second_ref, second[0])])
    near, both, weight = scale_tiles(scale_ref)
    add_terms(fields, FAR_TERMS, near, acc)
    own = own_force(fields, 3, both)
    for k in range(9):
        pairs = [[acc_tile(acc, target, 2 * k + c) for c in range(2)] for target in range(3)]
        in_x, in_y = fields.compact_halves(*pairs[0])
        in_z, in_t = fields.compact_halves(*pairs[2])
        in_t = in_t + fields.compact_sum(*pairs[1])
        for m, staple in enumerate((in_x, in_y, in_z, in_t)):
            start = own[k] if m == 3 else part_ref[pl.ds((9 * m + k) * 8, 8), :]
            out_ref[pl.ds((9 * m + k) * 8, 8), :] = start + weight[m] * staple


def rows_of(count):
    return jax.ShapeDtypeStruct((count, LANES), F32)


def on_device(pole_vectors, gauge_links, pole_coeff, naik_coeff, staple_weight):
    t_size = lax.axis_size("ta")
    z_size = lax.axis_size("gz") * lax.axis_size("gy")
    plan = message_plan(t_size)
    x_rows, u_rows = 8 * REGS["x"], 4 * 8 * REGS["u"]
    vmem = pl.BlockSpec(memory_space=pltpu.VMEM)
    hbm = pl.BlockSpec(memory_space=pltpu.HBM)
    limit = pltpu.CompilerParams(vmem_limit_bytes=4 * 1024 * 1024)

    def moved(name, value):
        kind, step = name
        if kind == "z":
            return lax.ppermute(value, ("gz", "gy"), [((i + step) % z_size, i) for i in range(z_size)])
        return lax.ppermute(value, "ta", [((j + step) % t_size, j) for j in range(t_size)])

    first_names = [name for name in plan if name[0] != "c"]
    corner_names = [name for name in plan if name[0] == "c"]
    z_names = [name for name in first_names if name[0] == "z"]
    packed = pl.pallas_call(
        functools.partial(pack_kernel, plan, first_names),
        out_shape=[rows_of(8 * plan[name].count) for name in first_names]
        + [rows_of(8 * 3 * NP), rows_of(x_rows), rows_of(u_rows)],
        in_specs=[hbm] * 5,
        out_specs=[vmem] * (len(first_names) + 3),
        scratch_shapes=[pltpu.SMEM((NP,), F32)] * 3
        + [pltpu.VMEM((u_rows, LANES), jnp.bfloat16), pltpu.SemaphoreType.DMA((5,))],
        compiler_params=limit,
        name="pack_halos",
    )(
        pole_coeff,
        naik_coeff,
        staple_weight,
        pole_vectors.reshape((x_rows, LANES)),
        gauge_links.reshape((u_rows, LANES)),
    )
    local = packed[len(first_names) :]
    received = {name: moved(name, value) for name, value in zip(first_names, packed)}
    corners = pl.pallas_call(
        functools.partial(corner_kernel, plan, corner_names),
        out_shape=[rows_of(8 * plan[name].count) for name in corner_names],
        in_specs=[vmem] * 2,
        out_specs=[vmem] * len(corner_names),
        compiler_params=limit,
        name="pack_corners",
    )(received["z", 1], received["z", -1])
    received.update({name: moved(name, value) for name, value in zip(corner_names, corners)})
    shared, first, second = field_split()
    shared_values, part = pl.pallas_call(
        functools.partial(near_kernel, plan, t_size, z_names),
        out_shape=[rows_of(shared[1]), rows_of(3 * 8 * REGS["u"])],
        in_specs=[vmem] * (3 + len(z_names)),
        out_specs=[vmem] * 2,
        scratch_shapes=[pltpu.VMEM((first[1], LANES), F32), pltpu.VMEM((2 * 18 * 8, LANES), F32)],
        cost_estimate=pl.CostEstimate(flops=4 * 10**6, bytes_accessed=4 * 10**6, transcendentals=0),
        compiler_params=pltpu.CompilerParams(vmem_limit_bytes=8 * 1024 * 1024),
        name="force_without_t",
    )(*local, *[received[name] for name in z_names])
    far_names = [name for name in received if name != ("z", 2)]
    force = pl.pallas_call(
        functools.partial(far_kernel, plan, t_size, far_names),
        out_shape=rows_of(u_rows),
        in_specs=[vmem] * (5 + len(far_names)),
        out_specs=vmem,
        scratch_shapes=[pltpu.VMEM((second[1], LANES), F32), pltpu.VMEM((3 * 18 * 8, LANES), F32)],
        compiler_params=pltpu.CompilerParams(vmem_limit_bytes=8 * 1024 * 1024),
        name="force_with_t",
    )(*local, shared_values, part, *[received[name] for name in far_names])
    return force.reshape(gauge_links.shape)


def solution(mesh):
    return jax.shard_map(
        on_device,
        mesh=mesh,
        in_specs=(
            P("ens", None, None, "ta", ("gz", "gy"), None),
            P("ens", None, None, None, "ta", ("gz", "gy"), None),
            P(),
            P(),
            P(),
        ),
        out_specs=P("ens", None, None, None, "ta", ("gz", "gy"), None),
        check_vma=False,
    )
```

time: 27.7 us -> 23.6 us (0.85)
  Pallas kernels: 8.84 us -> 5.11 us
  starting transfers between devices: 10.1 us -> 6.65 us
  waiting for transfers between devices: 6.17 us -> 9.21 us
    pallas_call x2 -> x4, Pallas kernels: 8.84 us -> 5.11 us  [the longest x1 2.75 us: on_device(): pl.pallas_call(functools.partial(near_kernel, plan, t_size, z_names), out...]
    ppermute x6 -> x5, starting transfers between devices: 10.1 us -> 6.65 us  [the longest x3 4.55 us: moved(): lax.ppermute(value, ('gz', 'gy'), [((i + step) % z_size, i) for i in rang...]
    ppermute x6 -> x5, waiting for transfers between devices: 6.17 us -> 9.21 us  [the longest x3 9.2 us: moved(): lax.ppermute(value, ('gz', 'gy'), [((i + step) % z_size, i) for i in rang...]
  transfers between devices with their start and end apart: 6 -> 5, of which waited for: 1 -> 2; matrix products, arithmetic and copies ran while one was open for 0% -> 0% of each run, Pallas kernels for 0% -> 12%
where the time goes in v3:
time: 23.6 us; the launch traced here: 23.4 us
  waiting for transfers between devices  9.21 us (39%)
  starting transfers between devices  6.65 us (28%)
  Pallas kernels  5.11 us (22%)
  local copies, waits for them, and re-layouts  2.37 us (10%)
    ppermute x3, waiting for transfers between devices, moved(): lax.ppermute(value, ('gz', 'gy'), [((i + step) % z_size, i) for i in rang...  9.2 us
    ppermute x3, starting transfers between devices, moved(): lax.ppermute(value, ('gz', 'gy'), [((i + step) % z_size, i) for i in rang...  4.55 us
    pallas_call x1, Pallas kernels, on_device(): pl.pallas_call(functools.partial(near_kernel, plan, t_size, z_names), out...  2.75 us
    unnamed x10, local copies, waits for them, and re-layouts  2.37 us
    ppermute x2, starting transfers between devices, moved(): lax.ppermute(value, 'ta', [((j + step) % t_size, j) for j in range(t_size)])  2.1 us
    pallas_call x1, Pallas kernels, on_device(): pl.pallas_call(functools.partial(far_kernel, plan, t_size, far_names), ou...  1.58 us
    pallas_call x1, Pallas kernels, on_device(): pl.pallas_call(functools.partial(pack_kernel, plan, first_names), out_sha...  0.76 us
  transfers between devices with their start and end apart: 5, of which 2 were waited for; matrix products, arithmetic and copies ran while one was open for 0% of the time, Pallas kernels for 12%

profile of v3, /device:TPU:0, one launch (start us, length us, event | category | flops | bytes accessed | tf_op | source)
XLA Modules:
  0.0 23.4 jit_solution(15412391121977951900)
XLA Ops:
  0.0 0.0 copy-start.2
  0.0 0.0 copy-start.3
  0.0 0.0 copy-start.4
  0.0 0.6 %copy-done.2 = f32[4]{0:T(128)S(1)} copy-done((f32[4]{0:T(128)S(1)}, f32[4]{0:T(128)}, u32[]{:S(2)}) %copy-start.2) | copy-done | bytes 40
  0.7 0.0 copy-done.3
  0.7 0.0 copy-done.4
  0.7 0.0 copy-start
  0.7 0.9 %copy-done = bf16[4,2,3,3,2,2,128]{6,5,4,3,2,1,0:T(2,128)(2,1)S(1)} copy-done((bf16[4,2,3,3,2,2,128]{6,5,4,3,2,1,0:T(2,128)(2,1)S(1)}, bf16[4,2,3,3,2,2,128]{6,5,4,3,2,1,0:T(2,128)(2,1)}, u32[]{:S(2)}) %copy-start) | copy-done | bytes 73752
  1.6 0.0 copy-start.1
  1.6 0.8 %copy-done.1 = f32[4,2,3,2,2,128]{5,4,3,2,1,0:T(2,128)S(1)} copy-done((f32[4,2,3,2,2,128]{5,4,3,2,1,0:T(2,128)S(1)}, f32[4,2,3,2,2,128]{5,4,3,2,1,0:T(2,128)}, u32[]{:S(2)}) %copy-start.1) | copy-done | bytes 49176
  2.4 0.8 %pack_halos.1 = (f32[208,128]{1,0:T(8,128)S(1)}, f32[88,128]{1,0:T(8,128)S(1)}, f32[48,128]{1,0:T(8,128)S(1)}, f32[240,128]{1,0:T(8,128)S(1)}, f32[96,128]{1,0:T...) custom-call(f32[4]{0:T(128)S(1)} %copy-done.2, f32[4]{0:T(128)S(1)} %copy-done.3, f32[4]{0:T(128)S(1)} %copy-done.4, ...), custom_call_target="tpu_custom_call" | custom-call | tf_op jit(solution)/shard_map/pack_halos/pallas_call | solution.py:440
  3.1 4.5 %collective-permute-start = (f32[208,128]{1,0:T(8,128)S(1)}, f32[208,128]{1,0:T(8,128)S(1)}, u32[]{:S(2)}, u32[]{:S(2)}) collective-permute-start(f32[208,128]{1,0:T(8,128)S(1)} %get-tuple-element.17), channel_id=1, source_target_pairs={{1,0},{4,1},{5,4},{8,5},{9,8},{12,9},{13,12},{0,13},{3,2},{6,3},{7... | collective-permute-start | bytes 319496 | tf_op jit(solution)/shard_map/ppermute | solution.py:434
  7.7 1.5 %collective-permute-start.3 = (f32[240,128]{1,0:T(8,128)S(1)}, f32[240,128]{1,0:T(8,128)S(1)}, u32[]{:S(2)}, u32[]{:S(2)}) collective-permute-start(f32[240,128]{1,0:T(8,128)S(1)} %get-tuple-element.22), channel_id=1, source_target_pairs={{2,0},{0,2},{3,1},{1,3},{6,4},{4,6},{7,5},{5,7},{10,8},{8,10},{11,... | collective-permute-start | bytes 368648 | tf_op jit(solution)/shard_map/ppermute | solution.py:435
  9.2 0.0 collective-permute-start.1
  9.2 5.4 %collective-permute-done.1.rest_1_.behind_ref = f32[88,128]{1,0:T(8,128)S(1)} collective-permute-done((f32[88,128]{1,0:T(8,128)S(1)}, f32[88,128]{1,0:T(8,128)S(1)}, u32[]{:S(2)}, u32[]{:S(2)}) %collective-permute-start.1) | collective-permute-done | bytes 45088 | tf_op jit(solution)/shard_map/ppermute | solution.py:434
  14.6 0.0 collective-permute-done.rest_0_.ahead_ref
  14.6 0.6 %collective-permute-start.4 = (f32[112,128]{1,0:T(8,128)S(1)}, f32[112,128]{1,0:T(8,128)S(1)}, u32[]{:S(2)}, u32[]{:S(2)}) collective-permute-start(f32[112,128]{1,0:T(8,128)S(1)} %pack_corners.1), channel_id=1, source_target_pairs={{2,0},{0,2},{3,1},{1,3},{6,4},{4,6},{7,5},{5,7},{10,8},{8,10},{11,... | collective-permute-start | bytes 172040 | tf_op jit(solution)/shard_map/ppermute | solution.py:435
  15.2 0.0 collective-permute-start.2
  15.2 3.8 %collective-permute-done.2.rest_2_ = f32[48,128]{1,0:T(8,128)S(1)} collective-permute-done((f32[48,128]{1,0:T(8,128)S(1)}, f32[48,128]{1,0:T(8,128)S(1)}, u32[]{:S(2)}, u32[]{:S(2)}) %collective-permute-start.2) | collective-permute-done | bytes 24608 | tf_op jit(solution)/shard_map/ppermute | solution.py:434
  19.0 2.7 %force_without_t.1 = (f32[1008,128]{1,0:T(8,128)S(1)}, f32[216,128]{1,0:T(8,128)S(1)}) custom-call(f32[96,128]{1,0:T(8,128)S(1)} %get-tuple-element.14.scale_ref, f32[96,128]{1,0:T(8,128)S(1)} %get-tuple-element.15.x_ref, f32[288,128]{1,0:T(8,128)S(1)} %get-tuple-element.16.u_ref, f32[208,128]{1,0:T(8,128)S(1)} %collective-permute-done.rest_0_.ahead_ref, ...), custom_call_target="tpu_custom_call" | custom-call | flops 4000000 | bytes 4000000 | tf_op jit(solution)/shard_map/force_without_t/pallas_call | solution.py:469
  21.8 0.0 collective-permute-done.3.rest_2_
  21.8 0.0 collective-permute-done.4.rest_3_
  21.8 1.6 %force_with_t.1 = f32[288,128]{1,0:T(8,128)} custom-call(f32[96,128]{1,0:T(8,128)S(1)} %get-tuple-element.14.scale_ref, f32[96,128]{1,0:T(8,128)S(1)} %get-tuple-element.15.x_ref, f32[288,128]{1,0:T(8,128)S(1)} %get-tuple-element.16.u_ref, f32[1008,128]{1,0:T(8,128)S(1)} %get-tuple-element.20.shared_ref, f32[216,128]{1,0:T(8,128)S(1)} %get-tuple-element.21.part_ref, ...), custom_call_target="tpu_custom_call" | custom-call | tf_op jit(solution)/shard_map/force_with_t/pallas_call | solution.py:480
  (1 shorter events, 0.0 us)
Async XLA Ops:
  0.0 0.7 %copy-start.2 = (f32[4]{0:T(128)S(1)}, f32[4]{0:T(128)}, u32[]{:S(2)}) copy-start(f32[4]{0:T(128)} %near_in.1) | copy-start | bytes 52
  0.0 0.7 %copy-start.3 = (f32[4]{0:T(128)S(1)}, f32[4]{0:T(128)}, u32[]{:S(2)}) copy-start(f32[4]{0:T(128)} %far_in.1) | copy-start | bytes 52
  0.0 0.7 %copy-start.4 = (f32[4]{0:T(128)S(1)}, f32[4]{0:T(128)}, u32[]{:S(2)}) copy-start(f32[4]{0:T(128)} %weight_in.1) | copy-start | bytes 52
  0.7 0.9 %copy-start = (bf16[4,2,3,3,2,2,128]{6,5,4,3,2,1,0:T(2,128)(2,1)S(1)}, bf16[4,2,3,3,2,2,128]{6,5,4,3,2,1,0:T(2,128)(2,1)}, u32[]{:S(2)}) copy-start(bf16[4,2,3,3,2,2,128]{6,5,4,3,2,1,0:T(2,128)(2,1)} %param.6) | copy-start | bytes 221188
  1.6 0.8 %copy-start.1 = (f32[4,2,3,2,2,128]{5,4,3,2,1,0:T(2,128)S(1)}, f32[4,2,3,2,2,128]{5,4,3,2,1,0:T(2,128)}, u32[]{:S(2)}) copy-start(f32[4,2,3,2,2,128]{5,4,3,2,1,0:T(2,128)} %param.5) | copy-start | bytes 147460
  3.1 11.4 %collective-permute-start = (f32[208,128]{1,0:T(8,128)S(1)}, f32[208,128]{1,0:T(8,128)S(1)}, u32[]{:S(2)}, u32[]{:S(2)}) collective-permute-start(f32[208,128]{1,0:T(8,128)S(1)} %get-tuple-element.17), channel_id=1, source_target_pairs={{1,0},{4,1},{5,4},{8,5},{9,8},{12,9},{13,12},{0,13},{3,2},{6,3},{7... | collective-permute-start | bytes 319496 | tf_op jit(solution)/shard_map/ppermute | solution.py:434
  7.7 14.1 %collective-permute-start.3 = (f32[240,128]{1,0:T(8,128)S(1)}, f32[240,128]{1,0:T(8,128)S(1)}, u32[]{:S(2)}, u32[]{:S(2)}) collective-permute-start(f32[240,128]{1,0:T(8,128)S(1)} %get-tuple-element.22), channel_id=1, source_target_pairs={{2,0},{0,2},{3,1},{1,3},{6,4},{4,6},{7,5},{5,7},{10,8},{8,10},{11,... | collective-permute-start | bytes 368648 | tf_op jit(solution)/shard_map/ppermute | solution.py:435
  9.2 5.4 %collective-permute-start.1 = (f32[88,128]{1,0:T(8,128)S(1)}, f32[88,128]{1,0:T(8,128)S(1)}, u32[]{:S(2)}, u32[]{:S(2)}) collective-permute-start(f32[88,128]{1,0:T(8,128)S(1)} %get-tuple-element.18), channel_id=1, source_target_pairs={{13,0},{0,1},{1,4},{4,5},{5,8},{8,9},{9,12},{12,13},{15,2},{2,3},{... | collective-permute-start | bytes 135176 | tf_op jit(solution)/shard_map/ppermute | solution.py:434
  14.6 7.2 %collective-permute-start.4 = (f32[112,128]{1,0:T(8,128)S(1)}, f32[112,128]{1,0:T(8,128)S(1)}, u32[]{:S(2)}, u32[]{:S(2)}) collective-permute-start(f32[112,128]{1,0:T(8,128)S(1)} %pack_corners.1), channel_id=1, source_target_pairs={{2,0},{0,2},{3,1},{1,3},{6,4},{4,6},{7,5},{5,7},{10,8},{8,10},{11,... | collective-permute-start | bytes 172040 | tf_op jit(solution)/shard_map/ppermute | solution.py:435
  15.2 3.8 %collective-permute-start.2 = (f32[48,128]{1,0:T(8,128)S(1)}, f32[48,128]{1,0:T(8,128)S(1)}, u32[]{:S(2)}, u32[]{:S(2)}) collective-permute-start(f32[48,128]{1,0:T(8,128)S(1)} %get-tuple-element.19), channel_id=1, source_target_pairs={{4,0},{5,1},{8,4},{9,5},{12,8},{13,9},{0,12},{1,13},{6,2},{7,3},{1... | collective-permute-start | bytes 73736 | tf_op jit(solution)/shard_map/ppermute | solution.py:434

commit v4 on v3

--- a/solution.py
+++ b/solution.py
@@ -186,9 +186,9 @@
 
 
 def field_split():
-    near = needed_fields(NEAR_TERMS, (0, 1, 2))
-    far = needed_fields(FAR_TERMS, (3,))
-    still = [key for key in far if key[2][3] == 0]
+    near = needed_fields(NEAR_TERMS, (0, 1))
+    far = needed_fields(FAR_TERMS, (2, 3))
+    still = [key for key in far if key[2][3] == 0 and abs(key[2][2]) < 3]
     shared = lay_out(still)
     first = lay_out([key for key in near if key not in shared[0]])
     second = lay_out([key for key in far if key not in shared[0]])
@@ -339,25 +339,42 @@
     return [fields.compact_sum(flat[2 * k], flat[2 * k + 1]) for k in range(9)]
 
 
-def pack_kernel(plan, names, near_in, far_in, weight_in, x_in, u_in, *rest):
+def write_messages(locator, plan, names, outs):
+    for name, out in zip(names, outs):
+        for reg, items in enumerate(plan[name].by_register()):
+            spots = [item and locator.local(*item[1:]) for item in items]
+            out[pl.ds(8 * reg, 8), :] = locator.assemble(spots)
+
+
+def pack_z_kernel(plan, names, x_in, u_in, *rest):
     outs = rest[: len(names)]
-    scale_ref, x_ref, u_ref, near_ref, far_ref, weight_ref, u_held, sems = rest[len(names) :]
+    x_ref, u_ref, u_held, sems = rest[len(names) :]
     copies = [
-        pltpu.make_async_copy(source, target, sems.at[index])
-        for index, (source, target) in enumerate(
-            ((u_in, u_held), (x_in, x_ref), (near_in, near_ref), (far_in, far_ref), (weight_in, weight_ref))
-        )
+        pltpu.make_async_copy(u_in, u_held, sems.at[0]),
+        pltpu.make_async_copy(x_in, x_ref, sems.at[1]),
     ]
     for copy in copies:
         copy.start()
     for copy in copies:
         copy.wait()
     u_ref[...] = u_held[...].astype(F32)
-    locator = Locator(plan, 1, {("own", "x"): x_ref, ("own", "u"): u_ref})
-    for name, out in zip(names, outs):
-        for reg, items in enumerate(plan[name].by_register()):
-            spots = [item and locator.local(*item[1:]) for item in items]
-            out[pl.ds(8 * reg, 8), :] = locator.assemble(spots)
+    write_messages(Locator(plan, 1, {("own", "x"): x_ref, ("own", "u"): u_ref}), plan, names, outs)
+
+
+def pack_t_kernel(plan, names, near_in, far_in, weight_in, x_ref, u_ref, *rest):
+    outs = rest[: len(names)]
+    scale_ref, near_ref, far_ref, weight_ref, sems = rest[len(names) :]
+    copies = [
+        pltpu.make_async_copy(source, target, sems.at[index])
+        for index, (source, target) in enumerate(
+            ((near_in, near_ref), (far_in, far_ref), (weight_in, weight_ref))
+        )
+    ]
+    for copy in copies:
+        copy.start()
+    write_messages(Locator(plan, 1, {("own", "x"): x_ref, ("own", "u"): u_ref}), plan, names, outs)
+    for copy in copies:
+        copy.wait()
     upper = lax.broadcasted_iota(jnp.int32, (8, LANES), 0) < 4
     for p in range(NP):
         scale_ref[pl.ds(8 * p, 8), :] = jnp.full((8, LANES), near_ref[p], F32)
@@ -386,12 +403,13 @@
     fields = Fields(x_ref, u_ref, stores)
     near, both, weight = scale_tiles(scale_ref)
     add_terms(fields, NEAR_TERMS, near, acc)
-    own = [own_force(fields, m, both) for m in range(3)]
+    own = [own_force(fields, m, both) for m in range(2)]
     for k in range(9):
         staples = list(fields.compact_halves(acc_tile(acc, 0, 2 * k), acc_tile(acc, 0, 2 * k + 1)))
         staples.append(fields.compact_sum(acc_tile(acc, 1, 2 * k), acc_tile(acc, 1, 2 * k + 1)))
         for m in range(3):
-            part_ref[pl.ds((9 * m + k) * 8, 8), :] = own[m][k] + weight[m] * staples[m]
+            value = weight[m] * staples[m]
+            part_ref[pl.ds((9 * m + k) * 8, 8), :] = own[m][k] + value if m < 2 else value
 
 
 def far_kernel(plan, t_size, names, scale_ref, x_ref, u_ref, shared_ref, part_ref, *rest):
@@ -404,15 +422,19 @@
     fields = Fields(x_ref, u_ref, [(shared_ref, shared[0]), (second_ref, second[0])])
     near, both, weight = scale_tiles(scale_ref)
     add_terms(fields, FAR_TERMS, near, acc)
-    own = own_force(fields, 3, both)
+    own = [own_force(fields, m, both) for m in (2, 3)]
     for k in range(9):
         pairs = [[acc_tile(acc, target, 2 * k + c) for c in range(2)] for target in range(3)]
         in_x, in_y = fields.compact_halves(*pairs[0])
         in_z, in_t = fields.compact_halves(*pairs[2])
         in_t = in_t + fields.compact_sum(*pairs[1])
         for m, staple in enumerate((in_x, in_y, in_z, in_t)):
-            start = own[k] if m == 3 else part_ref[pl.ds((9 * m + k) * 8, 8), :]
-            out_ref[pl.ds((9 * m + k) * 8, 8), :] = start + weight[m] * staple
+            value = weight[m] * staple
+            if m < 3:
+                value = value + part_ref[pl.ds((9 * m + k) * 8, 8), :]
+            if m > 1:
+                value = value + own[m - 2][k]
+            out_ref[pl.ds((9 * m + k) * 8, 8), :] = value
 
 
 def rows_of(count):
@@ -437,25 +459,30 @@
     first_names = [name for name in plan if name[0] != "c"]
     corner_names = [name for name in plan if name[0] == "c"]
     z_names = [name for name in first_names if name[0] == "z"]
+    t_names = [name for name in first_names if name[0] == "t"]
+    in_hbm = functools.partial(pltpu.with_memory_space_constraint, memory_space=pltpu.HBM)
     packed = pl.pallas_call(
-        functools.partial(pack_kernel, plan, first_names),
-        out_shape=[rows_of(8 * plan[name].count) for name in first_names]
-        + [rows_of(8 * 3 * NP), rows_of(x_rows), rows_of(u_rows)],
-        in_specs=[hbm] * 5,
-        out_specs=[vmem] * (len(first_names) + 3),
-        scratch_shapes=[pltpu.SMEM((NP,), F32)] * 3
-        + [pltpu.VMEM((u_rows, LANES), jnp.bfloat16), pltpu.SemaphoreType.DMA((5,))],
+        functools.partial(pack_z_kernel, plan, z_names),
+        out_shape=[rows_of(8 * plan[name].count) for name in z_names] + [rows_of(x_rows), rows_of(u_rows)],
+        in_specs=[hbm] * 2,
+        out_specs=[vmem] * (len(z_names) + 2),
+        scratch_shapes=[pltpu.VMEM((u_rows, LANES), jnp.bfloat16), pltpu.SemaphoreType.DMA((2,))],
         compiler_params=limit,
-        name="pack_halos",
-    )(
-        pole_coeff,
-        naik_coeff,
-        staple_weight,
-        pole_vectors.reshape((x_rows, LANES)),
-        gauge_links.reshape((u_rows, LANES)),
-    )
-    local = packed[len(first_names) :]
-    received = {name: moved(name, value) for name, value in zip(first_names, packed)}
+        name="pack_z",
+    )(in_hbm(pole_vectors.reshape((x_rows, LANES))), in_hbm(gauge_links.reshape((u_rows, LANES))))
+    own = packed[len(z_names) :]
+    received = {name: moved(name, value) for name, value in zip(z_names, packed)}
+    packed = pl.pallas_call(
+        functools.partial(pack_t_kernel, plan, t_names),
+        out_shape=[rows_of(8 * plan[name].count) for name in t_names] + [rows_of(8 * 3 * NP)],
+        in_specs=[hbm] * 3 + [vmem] * 2,
+        out_specs=[vmem] * (len(t_names) + 1),
+        scratch_shapes=[pltpu.SMEM((NP,), F32)] * 3 + [pltpu.SemaphoreType.DMA((3,))],
+        compiler_params=limit,
+        name="pack_t",
+    )(in_hbm(pole_coeff), in_hbm(naik_coeff), in_hbm(staple_weight), *own)
+    received.update({name: moved(name, value) for name, value in zip(t_names, packed)})
+    local = [packed[len(t_names)], *own]
     corners = pl.pallas_call(
         functools.partial(corner_kernel, plan, corner_names),
         out_shape=[rows_of(8 * plan[name].count) for name in corner_names],
@@ -466,17 +493,18 @@
     )(received["z", 1], received["z", -1])
     received.update({name: moved(name, value) for name, value in zip(corner_names, corners)})
     shared, first, second = field_split()
+    near_names = [name for name in z_names if name != ("z", 2)]
     shared_values, part = pl.pallas_call(
-        functools.partial(near_kernel, plan, t_size, z_names),
+        functools.partial(near_kernel, plan, t_size, near_names),
         out_shape=[rows_of(shared[1]), rows_of(3 * 8 * REGS["u"])],
-        in_specs=[vmem] * (3 + len(z_names)),
+        in_specs=[vmem] * (3 + len(near_names)),
         out_specs=[vmem] * 2,
         scratch_shapes=[pltpu.VMEM((first[1], LANES), F32), pltpu.VMEM((2 * 18 * 8, LANES), F32)],
         cost_estimate=pl.CostEstimate(flops=4 * 10**6, bytes_accessed=4 * 10**6, transcendentals=0),
         compiler_params=pltpu.CompilerParams(vmem_limit_bytes=8 * 1024 * 1024),
         name="force_without_t",
-    )(*local, *[received[name] for name in z_names])
-    far_names = [name for name in received if name != ("z", 2)]
+    )(*local, *[received[name] for name in near_names])
+    far_names = list(received)
     force = pl.pallas_call(
         functools.partial(far_kernel, plan, t_size, far_names),
         out_shape=rows_of(u_rows),

time: 23.6 us -> 19.4 us (0.82)
  waiting for transfers between devices: 9.21 us -> 6.4 us
  local copies, waits for them, and re-layouts: 2.37 us -> 0 us
  Pallas kernels: 5.11 us -> 5.96 us
    ppermute x3, waiting for transfers between devices: 9.2 us -> 6.4 us  [moved(): lax.ppermute(value, ('gz', 'gy'), [((i + step) % z_size, i) for i in rang...]
    unnamed x10 -> x0, local copies, waits for them, and re-layouts: 2.37 us -> none
    pallas_call x2 -> x3, Pallas kernels: 3.51 us -> 4.32 us  [the longest x1 2.69 us: on_device(): pl.pallas_call(functools.partial(near_kernel, plan, t_size, near_names),...]
  transfers between devices with their start and end apart: 5 -> 5, of which waited for: 2 -> 2; matrix products, arithmetic and copies ran while one was open for 0% -> 0% of each run, Pallas kernels for 12% -> 18%
where the time goes in v4:
time: 19.4 us; the launch traced here: 19.2 us
  starting transfers between devices  6.83 us (35%)
  waiting for transfers between devices  6.4 us (33%)
  Pallas kernels  5.96 us (31%)
    ppermute x3, waiting for transfers between devices, moved(): lax.ppermute(value, ('gz', 'gy'), [((i + step) % z_size, i) for i in rang...  6.4 us
    ppermute x3, starting transfers between devices, moved(): lax.ppermute(value, ('gz', 'gy'), [((i + step) % z_size, i) for i in rang...  4.55 us
    pallas_call x1, Pallas kernels, on_device(): pl.pallas_call(functools.partial(near_kernel, plan, t_size, near_names),...  2.69 us
    ppermute x2, starting transfers between devices, moved(): lax.ppermute(value, 'ta', [((j + step) % t_size, j) for j in range(t_size)])  2.28 us
    pallas_call x1, Pallas kernels, on_device(): pl.pallas_call(functools.partial(far_kernel, plan, t_size, far_names), ou...  1.63 us
    pallas_call x1, Pallas kernels, on_device(): pl.pallas_call(functools.partial(pack_z_kernel, plan, z_names), out_shape...  0.92 us
    pallas_call x1, Pallas kernels, on_device(): pl.pallas_call(functools.partial(pack_t_kernel, plan, t_names), out_shape...  0.71 us
  transfers between devices with their start and end apart: 5, of which 2 were waited for; matrix products, arithmetic and copies ran while one was open for 0% of the time, Pallas kernels for 18%

profile of v4, /device:TPU:0, one launch (start us, length us, event | category | flops | bytes accessed | tf_op | source)
XLA Modules:
  0.0 19.2 jit_solution(3965196498216664023)
XLA Ops:
  0.0 0.9 %pack_z.1 = (f32[208,128]{1,0:T(8,128)S(1)}, f32[88,128]{1,0:T(8,128)S(1)}, f32[48,128]{1,0:T(8,128)S(1)}, f32[96,128]{1,0:T(8,128)S(1)}, f32[288,128]{1,0:T(8,128)S(1)}) custom-call(f32[96,128]{1,0:T(8,128)} %bitcast.4, bf16[288,128]{1,0:T(8,128)(2,1)} %bitcast.3), custom_call_target="tpu_custom_call" | custom-call | tf_op jit(solution)/shard_map/pack_z/pallas_call | solution.py:464
  0.9 4.5 %collective-permute-start = (f32[208,128]{1,0:T(8,128)S(1)}, f32[208,128]{1,0:T(8,128)S(1)}, u32[]{:S(2)}, u32[]{:S(2)}) collective-permute-start(f32[208,128]{1,0:T(8,128)S(1)} %get-tuple-element.17), channel_id=1, source_target_pairs={{1,0},{4,1},{5,4},{8,5},{9,8},{12,9},{13,12},{0,13},{3,2},{6,3},{7... | collective-permute-start | bytes 319496 | tf_op jit(solution)/shard_map/ppermute | solution.py:456
  5.5 0.7 %pack_t.1 = (f32[240,128]{1,0:T(8,128)S(1)}, f32[96,128]{1,0:T(8,128)S(1)}) custom-call(f32[4]{0:T(128)} %near_in.1, f32[4]{0:T(128)} %far_in.1, f32[4]{0:T(128)} %weight_in.1, f32[96,128]{1,0:T(8,128)S(1)} %get-tuple-element.14.x_ref, f32[288,128]{1,0:T(8,128)S(1)} %get-tuple-element.15.u_ref), custom_call_target="tpu_custom_call" | custom-call | tf_op jit(solution)/shard_map/pack_t/pallas_call | solution.py:475
  6.2 1.6 %collective-permute-start.3 = (f32[240,128]{1,0:T(8,128)S(1)}, f32[240,128]{1,0:T(8,128)S(1)}, u32[]{:S(2)}, u32[]{:S(2)}) collective-permute-start(f32[240,128]{1,0:T(8,128)S(1)} %get-tuple-element.22), channel_id=1, source_target_pairs={{2,0},{0,2},{3,1},{1,3},{6,4},{4,6},{7,5},{5,7},{10,8},{8,10},{11,... | collective-permute-start | bytes 368648 | tf_op jit(solution)/shard_map/ppermute | solution.py:457
  7.8 0.0 collective-permute-start.1
  7.8 5.3 %collective-permute-done.1.rest_1_.behind_ref = f32[88,128]{1,0:T(8,128)S(1)} collective-permute-done((f32[88,128]{1,0:T(8,128)S(1)}, f32[88,128]{1,0:T(8,128)S(1)}, u32[]{:S(2)}, u32[]{:S(2)}) %collective-permute-start.1) | collective-permute-done | bytes 45088 | tf_op jit(solution)/shard_map/ppermute | solution.py:456
  13.0 0.0 collective-permute-done.rest_0_.ahead_ref
  13.0 0.7 %collective-permute-start.4 = (f32[112,128]{1,0:T(8,128)S(1)}, f32[112,128]{1,0:T(8,128)S(1)}, u32[]{:S(2)}, u32[]{:S(2)}) collective-permute-start(f32[112,128]{1,0:T(8,128)S(1)} %pack_corners.1), channel_id=1, source_target_pairs={{2,0},{0,2},{3,1},{1,3},{6,4},{4,6},{7,5},{5,7},{10,8},{8,10},{11,... | collective-permute-start | bytes 172040 | tf_op jit(solution)/shard_map/ppermute | solution.py:457
  13.8 0.0 collective-permute-start.2
  13.8 2.7 %force_without_t.1 = (f32[1008,128]{1,0:T(8,128)S(1)}, f32[216,128]{1,0:T(8,128)S(1)}) custom-call(f32[96,128]{1,0:T(8,128)S(1)} %get-tuple-element.16.scale_ref, f32[96,128]{1,0:T(8,128)S(1)} %get-tuple-element.14.x_ref, f32[288,128]{1,0:T(8,128)S(1)} %get-tuple-element.15.u_ref, f32[208,128]{1,0:T(8,128)S(1)} %collective-permute-done.rest_0_.ahead_ref, ...), custom_call_target="tpu_custom_call" | custom-call | flops 4000000 | bytes 4000000 | tf_op jit(solution)/shard_map/force_without_t/pallas_call | solution.py:497
  16.5 1.1 %collective-permute-done.2.rest_2_ = f32[48,128]{1,0:T(8,128)S(1)} collective-permute-done((f32[48,128]{1,0:T(8,128)S(1)}, f32[48,128]{1,0:T(8,128)S(1)}, u32[]{:S(2)}, u32[]{:S(2)}) %collective-permute-start.2) | collective-permute-done | bytes 24608 | tf_op jit(solution)/shard_map/ppermute | solution.py:456
  17.6 0.0 collective-permute-done.3.rest_3_
  17.6 0.0 collective-permute-done.4.rest_4_
  17.6 1.6 %force_with_t.1 = f32[288,128]{1,0:T(8,128)} custom-call(f32[96,128]{1,0:T(8,128)S(1)} %get-tuple-element.16.scale_ref, f32[96,128]{1,0:T(8,128)S(1)} %get-tuple-element.14.x_ref, f32[288,128]{1,0:T(8,128)S(1)} %get-tuple-element.15.u_ref, f32[1008,128]{1,0:T(8,128)S(1)} %get-tuple-element.19.shared_ref, f32[216,128]{1,0:T(8,128)S(1)} %get-tuple-element.20.part_ref, ...), custom_call_target="tpu_custom_call" | custom-call | tf_op jit(solution)/shard_map/force_with_t/pallas_call | solution.py:508
  (1 shorter events, 0.0 us)
Async XLA Ops:
  0.9 12.1 %collective-permute-start = (f32[208,128]{1,0:T(8,128)S(1)}, f32[208,128]{1,0:T(8,128)S(1)}, u32[]{:S(2)}, u32[]{:S(2)}) collective-permute-start(f32[208,128]{1,0:T(8,128)S(1)} %get-tuple-element.17), channel_id=1, source_target_pairs={{1,0},{4,1},{5,4},{8,5},{9,8},{12,9},{13,12},{0,13},{3,2},{6,3},{7... | collective-permute-start | bytes 319496 | tf_op jit(solution)/shard_map/ppermute | solution.py:456
  6.2 11.4 %collective-permute-start.3 = (f32[240,128]{1,0:T(8,128)S(1)}, f32[240,128]{1,0:T(8,128)S(1)}, u32[]{:S(2)}, u32[]{:S(2)}) collective-permute-start(f32[240,128]{1,0:T(8,128)S(1)} %get-tuple-element.22), channel_id=1, source_target_pairs={{2,0},{0,2},{3,1},{1,3},{6,4},{4,6},{7,5},{5,7},{10,8},{8,10},{11,... | collective-permute-start | bytes 368648 | tf_op jit(solution)/shard_map/ppermute | solution.py:457
  7.8 5.3 %collective-permute-start.1 = (f32[88,128]{1,0:T(8,128)S(1)}, f32[88,128]{1,0:T(8,128)S(1)}, u32[]{:S(2)}, u32[]{:S(2)}) collective-permute-start(f32[88,128]{1,0:T(8,128)S(1)} %get-tuple-element.18), channel_id=1, source_target_pairs={{13,0},{0,1},{1,4},{4,5},{5,8},{8,9},{9,12},{12,13},{15,2},{2,3},{... | collective-permute-start | bytes 135176 | tf_op jit(solution)/shard_map/ppermute | solution.py:456
  13.0 4.6 %collective-permute-start.4 = (f32[112,128]{1,0:T(8,128)S(1)}, f32[112,128]{1,0:T(8,128)S(1)}, u32[]{:S(2)}, u32[]{:S(2)}) collective-permute-start(f32[112,128]{1,0:T(8,128)S(1)} %pack_corners.1), channel_id=1, source_target_pairs={{2,0},{0,2},{3,1},{1,3},{6,4},{4,6},{7,5},{5,7},{10,8},{8,10},{11,... | collective-permute-start | bytes 172040 | tf_op jit(solution)/shard_map/ppermute | solution.py:457
  13.8 3.8 %collective-permute-start.2 = (f32[48,128]{1,0:T(8,128)S(1)}, f32[48,128]{1,0:T(8,128)S(1)}, u32[]{:S(2)}, u32[]{:S(2)}) collective-permute-start(f32[48,128]{1,0:T(8,128)S(1)} %get-tuple-element.21), channel_id=1, source_target_pairs={{4,0},{5,1},{8,4},{9,5},{12,8},{13,9},{0,12},{1,13},{6,2},{7,3},{1... | collective-permute-start | bytes 73736 | tf_op jit(solution)/shard_map/ppermute | solution.py:456

commit v5 on v4

--- a/solution.py
+++ b/solution.py
@@ -346,9 +346,11 @@
             out[pl.ds(8 * reg, 8), :] = locator.assemble(spots)
 
 
-def pack_z_kernel(plan, names, x_in, u_in, *rest):
-    outs = rest[: len(names)]
-    x_ref, u_ref, u_held, sems = rest[len(names) :]
+def odd_in_z():
+    return (lax.axis_index("gz") * lax.axis_size("gy") + lax.axis_index("gy")) % 2 == 1
+
+
+def pack_z_kernel(plan, x_in, u_in, within_ref, between_ref, second_ref, x_ref, u_ref, u_held, sems):
     copies = [
         pltpu.make_async_copy(u_in, u_held, sems.at[0]),
         pltpu.make_async_copy(x_in, x_ref, sems.at[1]),
@@ -358,7 +360,18 @@
     for copy in copies:
         copy.wait()
     u_ref[...] = u_held[...].astype(F32)
-    write_messages(Locator(plan, 1, {("own", "x"): x_ref, ("own", "u"): u_ref}), plan, names, outs)
+    locator = Locator(plan, 1, {("own", "x"): x_ref, ("own", "u"): u_ref})
+    names = [("z", 1), ("z", -1)]
+
+    @pl.when(odd_in_z())
+    def _():
+        write_messages(locator, plan, names, (within_ref, between_ref))
+
+    @pl.when(jnp.logical_not(odd_in_z()))
+    def _():
+        write_messages(locator, plan, names, (between_ref, within_ref))
+
+    write_messages(locator, plan, [("z", 2)], [second_ref])
 
 
 def pack_t_kernel(plan, names, near_in, far_in, weight_in, x_ref, u_ref, *rest):
@@ -382,7 +395,19 @@
         scale_ref[pl.ds(8 * (2 * NP + p), 8), :] = jnp.full((8, LANES), weight_ref[p], F32)
 
 
-def corner_kernel(plan, names, ahead_ref, behind_ref, *outs):
+def corner_kernel(plan, names, within_ref, between_ref, second_ref, ahead_ref, behind_ref, *outs):
+    def split(from_ahead, from_behind):
+        ahead_ref[...] = from_ahead[pl.ds(0, ahead_ref.shape[0]), :]
+        behind_ref[...] = from_behind[pl.ds(0, behind_ref.shape[0]), :]
+
+    @pl.when(odd_in_z())
+    def _():
+        split(between_ref, within_ref)
+
+    @pl.when(jnp.logical_not(odd_in_z()))
+    def _():
+        split(within_ref, between_ref)
+
     locator = Locator(plan, 1, {("z", 1): ahead_ref, ("z", -1): behind_ref})
     for name, out in zip(names, outs):
         for reg, items in enumerate(plan[name].by_register()):
@@ -456,22 +481,28 @@
             return lax.ppermute(value, ("gz", "gy"), [((i + step) % z_size, i) for i in range(z_size)])
         return lax.ppermute(value, "ta", [((j + step) % t_size, j) for j in range(t_size)])
 
+    def exchanged(value, first):
+        pairs = [(i, (i + 1) % z_size) for i in range(first, z_size, 2)]
+        return lax.ppermute(value, ("gz", "gy"), pairs + [(j, i) for i, j in pairs])
+
     first_names = [name for name in plan if name[0] != "c"]
     corner_names = [name for name in plan if name[0] == "c"]
-    z_names = [name for name in first_names if name[0] == "z"]
     t_names = [name for name in first_names if name[0] == "t"]
     in_hbm = functools.partial(pltpu.with_memory_space_constraint, memory_space=pltpu.HBM)
-    packed = pl.pallas_call(
-        functools.partial(pack_z_kernel, plan, z_names),
-        out_shape=[rows_of(8 * plan[name].count) for name in z_names] + [rows_of(x_rows), rows_of(u_rows)],
+    ahead_rows, behind_rows = [8 * plan["z", step].count for step in (1, -1)]
+    shared_rows = max(ahead_rows, behind_rows)
+    within, between, beyond, *own = pl.pallas_call(
+        functools.partial(pack_z_kernel, plan),
+        out_shape=[rows_of(shared_rows), rows_of(shared_rows + 8), rows_of(8 * plan["z", 2].count)]
+        + [rows_of(x_rows), rows_of(u_rows)],
         in_specs=[hbm] * 2,
-        out_specs=[vmem] * (len(z_names) + 2),
+        out_specs=[vmem] * 5,
         scratch_shapes=[pltpu.VMEM((u_rows, LANES), jnp.bfloat16), pltpu.SemaphoreType.DMA((2,))],
         compiler_params=limit,
         name="pack_z",
     )(in_hbm(pole_vectors.reshape((x_rows, LANES))), in_hbm(gauge_links.reshape((u_rows, LANES))))
-    own = packed[len(z_names) :]
-    received = {name: moved(name, value) for name, value in zip(z_names, packed)}
+    between, within = exchanged(between, 1), exchanged(within, 0)
+    received = {("z", 2): moved(("z", 2), beyond)}
     packed = pl.pallas_call(
         functools.partial(pack_t_kernel, plan, t_names),
         out_shape=[rows_of(8 * plan[name].count) for name in t_names] + [rows_of(8 * 3 * NP)],
@@ -483,17 +514,18 @@
     )(in_hbm(pole_coeff), in_hbm(naik_coeff), in_hbm(staple_weight), *own)
     received.update({name: moved(name, value) for name, value in zip(t_names, packed)})
     local = [packed[len(t_names)], *own]
-    corners = pl.pallas_call(
+    received["z", 1], received["z", -1], *corners = pl.pallas_call(
         functools.partial(corner_kernel, plan, corner_names),
-        out_shape=[rows_of(8 * plan[name].count) for name in corner_names],
-        in_specs=[vmem] * 2,
-        out_specs=[vmem] * len(corner_names),
+        out_shape=[rows_of(ahead_rows), rows_of(behind_rows)]
+        + [rows_of(8 * plan[name].count) for name in corner_names],
+        in_specs=[vmem] * 3,
+        out_specs=[vmem] * (2 + len(corner_names)),
         compiler_params=limit,
         name="pack_corners",
-    )(received["z", 1], received["z", -1])
+    )(within, between, received["z", 2])
     received.update({name: moved(name, value) for name, value in zip(corner_names, corners)})
     shared, first, second = field_split()
-    near_names = [name for name in z_names if name != ("z", 2)]
+    near_names = [("z", 1), ("z", -1)]
     shared_values, part = pl.pallas_call(
         functools.partial(near_kernel, plan, t_size, near_names),
         out_shape=[rows_of(shared[1]), rows_of(3 * 8 * REGS["u"])],

time: 19.4 us -> 17.7 us (0.912)
  waiting for transfers between devices: 6.4 us -> 3.89 us
  starting transfers between devices: 6.83 us -> 7.61 us
    ppermute x0 -> x2, starting transfers between devices: none -> 4.56 us  [exchanged(): return lax.ppermute(value, ('gz', 'gy'), pairs + [(j, i) for i, j in pairs])]
    ppermute x3 -> x1, starting transfers between devices: 4.55 us -> 0.89 us  [moved(): lax.ppermute(value, ('gz', 'gy'), [((i + step) % z_size, i) for i in rang...]
    ppermute x3 -> x1, waiting for transfers between devices: 6.4 us -> 2.93 us  [moved(): lax.ppermute(value, ('gz', 'gy'), [((i + step) % z_size, i) for i in rang...]
    ppermute x2, waiting for transfers between devices: 0.01 us -> 0.95 us  [moved(): lax.ppermute(value, 'ta', [((j + step) % t_size, j) for j in range(t_size)])]
  transfers between devices with their start and end apart: 5 -> 5, of which waited for: 2 -> 2; matrix products, arithmetic and copies ran while one was open for 0% -> 0% of each run, Pallas kernels for 18% -> 20%
where the time goes in v5:
time: 17.7 us; the launch traced here: 17.5 us
  starting transfers between devices  7.61 us (43%)
  Pallas kernels  5.98 us (34%)
  waiting for transfers between devices  3.89 us (22%)
    ppermute x2, starting transfers between devices, exchanged(): return lax.ppermute(value, ('gz', 'gy'), pairs + [(j, i) for i, j in pairs])  4.56 us
    ppermute x1, waiting for transfers between devices, moved(): lax.ppermute(value, ('gz', 'gy'), [((i + step) % z_size, i) for i in rang...  2.93 us
    pallas_call x1, Pallas kernels, on_device(): pl.pallas_call(functools.partial(near_kernel, plan, t_size, near_names),...  2.68 us
    ppermute x2, starting transfers between devices, moved(): lax.ppermute(value, 'ta', [((j + step) % t_size, j) for j in range(t_size)])  2.16 us
    pallas_call x1, Pallas kernels, on_device(): pl.pallas_call(functools.partial(far_kernel, plan, t_size, far_names), ou...  1.63 us
    ppermute x2, waiting for transfers between devices, moved(): lax.ppermute(value, 'ta', [((j + step) % t_size, j) for j in range(t_size)])  0.95 us
    pallas_call x1, Pallas kernels, on_device(): pl.pallas_call(functools.partial(pack_z_kernel, plan), out_shape=[rows_of...  0.94 us
    ppermute x1, starting transfers between devices, moved(): lax.ppermute(value, ('gz', 'gy'), [((i + step) % z_size, i) for i in rang...  0.89 us
  transfers between devices with their start and end apart: 5, of which 2 were waited for; matrix products, arithmetic and copies ran while one was open for 0% of the time, Pallas kernels for 20%

profile of v5, /device:TPU:0, one launch (start us, length us, event | category | flops | bytes accessed | tf_op | source)
XLA Modules:
  0.0 17.5 jit_solution(17769844279072251706)
XLA Ops:
  0.0 0.9 %pack_z.1 = (f32[208,128]{1,0:T(8,128)S(1)}, f32[216,128]{1,0:T(8,128)S(1)}, f32[48,128]{1,0:T(8,128)S(1)}, f32[96,128]{1,0:T(8,128)S(1)}, f32[288,128]{1,0:T(8,128)S(1)}) custom-call(f32[96,128]{1,0:T(8,128)} %bitcast.4, bf16[288,128]{1,0:T(8,128)(2,1)} %bitcast.3), custom_call_target="tpu_custom_call" | custom-call | tf_op jit(solution)/shard_map/pack_z/pallas_call | solution.py:494
  0.9 4.6 %collective-permute-start.1 = (f32[216,128]{1,0:T(8,128)S(1)}, f32[216,128]{1,0:T(8,128)S(1)}, u32[]{:S(2)}, u32[]{:S(2)}) collective-permute-start(f32[216,128]{1,0:T(8,128)S(1)} %get-tuple-element.21), channel_id=1, source_target_pairs={{1,4},{5,8},{9,12},{13,0},{4,1},{8,5},{12,9},{0,13},{3,6},{7,10},{... | collective-permute-start | bytes 331784 | tf_op jit(solution)/shard_map/ppermute | solution.py:486
  5.5 0.0 collective-permute-start
  5.5 0.7 %pack_t.1 = (f32[240,128]{1,0:T(8,128)S(1)}, f32[96,128]{1,0:T(8,128)S(1)}) custom-call(f32[4]{0:T(128)} %near_in.1, f32[4]{0:T(128)} %far_in.1, f32[4]{0:T(128)} %weight_in.1, f32[96,128]{1,0:T(8,128)S(1)} %get-tuple-element.17.x_ref, f32[288,128]{1,0:T(8,128)S(1)} %get-tuple-element.18.u_ref), custom_call_target="tpu_custom_call" | custom-call | tf_op jit(solution)/shard_map/pack_t/pallas_call | solution.py:506
  6.2 1.6 %collective-permute-start.3 = (f32[240,128]{1,0:T(8,128)S(1)}, f32[240,128]{1,0:T(8,128)S(1)}, u32[]{:S(2)}, u32[]{:S(2)}) collective-permute-start(f32[240,128]{1,0:T(8,128)S(1)} %get-tuple-element.27), channel_id=1, source_target_pairs={{2,0},{0,2},{3,1},{1,3},{6,4},{4,6},{7,5},{5,7},{10,8},{8,10},{11,... | collective-permute-start | bytes 368648 | tf_op jit(solution)/shard_map/ppermute | solution.py:482
  7.8 0.9 %collective-permute-start.2 = (f32[48,128]{1,0:T(8,128)S(1)}, f32[48,128]{1,0:T(8,128)S(1)}, u32[]{:S(2)}, u32[]{:S(2)}) collective-permute-start(f32[48,128]{1,0:T(8,128)S(1)} %get-tuple-element.22), channel_id=1, source_target_pairs={{4,0},{5,1},{8,4},{9,5},{12,8},{13,9},{0,12},{1,13},{6,2},{7,3},{1... | collective-permute-start | bytes 73736 | tf_op jit(solution)/shard_map/ppermute | solution.py:481
  8.7 2.9 %collective-permute-done.2.second_ref.rest_0_ = f32[48,128]{1,0:T(8,128)S(1)} collective-permute-done((f32[48,128]{1,0:T(8,128)S(1)}, f32[48,128]{1,0:T(8,128)S(1)}, u32[]{:S(2)}, u32[]{:S(2)}) %collective-permute-start.2) | collective-permute-done | bytes 24608 | tf_op jit(solution)/shard_map/ppermute | solution.py:481
  11.6 0.0 collective-permute-done.within_ref
  11.6 0.0 collective-permute-done.1.between_ref
  11.6 0.6 %collective-permute-start.4 = (f32[112,128]{1,0:T(8,128)S(1)}, f32[112,128]{1,0:T(8,128)S(1)}, u32[]{:S(2)}, u32[]{:S(2)}) collective-permute-start(f32[112,128]{1,0:T(8,128)S(1)} %get-tuple-element.28), channel_id=1, source_target_pairs={{2,0},{0,2},{3,1},{1,3},{6,4},{4,6},{7,5},{5,7},{10,8},{8,10},{11,... | collective-permute-start | bytes 172040 | tf_op jit(solution)/shard_map/ppermute | solution.py:482
  12.2 2.7 %force_without_t.1 = (f32[1008,128]{1,0:T(8,128)S(1)}, f32[216,128]{1,0:T(8,128)S(1)}) custom-call(f32[96,128]{1,0:T(8,128)S(1)} %get-tuple-element.19.scale_ref, f32[96,128]{1,0:T(8,128)S(1)} %get-tuple-element.17.x_ref, f32[288,128]{1,0:T(8,128)S(1)} %get-tuple-element.18.u_ref, f32[208,128]{1,0:T(8,128)S(1)} %get-tuple-element.23.rest_0_.rest_2_, ...), custom_call_target="tpu_custom_call" | custom-call | flops 4000000 | bytes 4000000 | tf_op jit(solution)/shard_map/force_without_t/pallas_call | solution.py:529
  14.9 0.0 collective-permute-done.3.rest_1_
  14.9 0.9 %collective-permute-done.4.rest_4_ = f32[112,128]{1,0:T(8,128)S(1)} collective-permute-done((f32[112,128]{1,0:T(8,128)S(1)}, f32[112,128]{1,0:T(8,128)S(1)}, u32[]{:S(2)}, u32[]{:S(2)}) %collective-permute-start.4) | collective-permute-done | bytes 57376 | tf_op jit(solution)/shard_map/ppermute | solution.py:482
  15.9 1.6 %force_with_t.1 = f32[288,128]{1,0:T(8,128)} custom-call(f32[96,128]{1,0:T(8,128)S(1)} %get-tuple-element.19.scale_ref, f32[96,128]{1,0:T(8,128)S(1)} %get-tuple-element.17.x_ref, f32[288,128]{1,0:T(8,128)S(1)} %get-tuple-element.18.u_ref, f32[1008,128]{1,0:T(8,128)S(1)} %get-tuple-element.25.shared_ref, f32[216,128]{1,0:T(8,128)S(1)} %get-tuple-element.26.part_ref, ...), custom_call_target="tpu_custom_call" | custom-call | tf_op jit(solution)/shard_map/force_with_t/pallas_call | solution.py:540
  (1 shorter events, 0.0 us)
Async XLA Ops:
  0.9 10.7 %collective-permute-start.1 = (f32[216,128]{1,0:T(8,128)S(1)}, f32[216,128]{1,0:T(8,128)S(1)}, u32[]{:S(2)}, u32[]{:S(2)}) collective-permute-start(f32[216,128]{1,0:T(8,128)S(1)} %get-tuple-element.21), channel_id=1, source_target_pairs={{1,4},{5,8},{9,12},{13,0},{4,1},{8,5},{12,9},{0,13},{3,6},{7,10},{... | collective-permute-start | bytes 331784 | tf_op jit(solution)/shard_map/ppermute | solution.py:486
  5.5 6.1 %collective-permute-start = (f32[208,128]{1,0:T(8,128)S(1)}, f32[208,128]{1,0:T(8,128)S(1)}, u32[]{:S(2)}, u32[]{:S(2)}) collective-permute-start(f32[208,128]{1,0:T(8,128)S(1)} %get-tuple-element.20), channel_id=1, source_target_pairs={{0,1},{4,5},{8,9},{12,13},{1,0},{5,4},{9,8},{13,12},{2,3},{6,7},{1... | collective-permute-start | bytes 319496 | tf_op jit(solution)/shard_map/ppermute | solution.py:486
  6.2 8.7 %collective-permute-start.3 = (f32[240,128]{1,0:T(8,128)S(1)}, f32[240,128]{1,0:T(8,128)S(1)}, u32[]{:S(2)}, u32[]{:S(2)}) collective-permute-start(f32[240,128]{1,0:T(8,128)S(1)} %get-tuple-element.27), channel_id=1, source_target_pairs={{2,0},{0,2},{3,1},{1,3},{6,4},{4,6},{7,5},{5,7},{10,8},{8,10},{11,... | collective-permute-start | bytes 368648 | tf_op jit(solution)/shard_map/ppermute | solution.py:482
  7.8 3.8 %collective-permute-start.2 = (f32[48,128]{1,0:T(8,128)S(1)}, f32[48,128]{1,0:T(8,128)S(1)}, u32[]{:S(2)}, u32[]{:S(2)}) collective-permute-start(f32[48,128]{1,0:T(8,128)S(1)} %get-tuple-element.22), channel_id=1, source_target_pairs={{4,0},{5,1},{8,4},{9,5},{12,8},{13,9},{0,12},{1,13},{6,2},{7,3},{1... | collective-permute-start | bytes 73736 | tf_op jit(solution)/shard_map/ppermute | solution.py:481
  11.6 4.2 %collective-permute-start.4 = (f32[112,128]{1,0:T(8,128)S(1)}, f32[112,128]{1,0:T(8,128)S(1)}, u32[]{:S(2)}, u32[]{:S(2)}) collective-permute-start(f32[112,128]{1,0:T(8,128)S(1)} %get-tuple-element.28), channel_id=1, source_target_pairs={{2,0},{0,2},{3,1},{1,3},{6,4},{4,6},{7,5},{5,7},{10,8},{8,10},{11,... | collective-permute-start | bytes 172040 | tf_op jit(solution)/shard_map/ppermute | solution.py:482

commit v6 on v5

--- a/solution.py
+++ b/solution.py
@@ -17,8 +17,15 @@
 UNIT = ((1, 0, 0, 0), (0, 1, 0, 0), (0, 0, 1, 0), (0, 0, 0, 1))
 ZERO = (0, 0, 0, 0)
 SITES = ((0, 0), (0, 1), (1, 0), (1, 1))
-NEAR_TERMS = ((0, ((0, 1), (1, 0))), (0, ((0, 2), (1, 2))), (1, ((2, 0), (2, 1))))
-FAR_TERMS = ((0, ((0, 3), (1, 3))), (1, ((3, 0), (3, 1))), (2, ((2, 3), (3, 2))))
+STAGES = ("own", "z", "t", "corner")
+TERMS = {
+    "own": ((0, ((0, 1), (1, 0))),),
+    "z": ((0, ((0, 2), (1, 2))), (1, ((2, 0), (2, 1)))),
+    "t": ((0, ((0, 3), (1, 3))), (1, ((3, 0), (3, 1)))),
+    "corner": ((0, ((2, 3), (3, 2))),),
+}
+COSTS = {"own": 2.0, "z": 2.0, "t": 2.0, "corner": 1.0}
+DIRECT = {"own": (0, 1), "z": (), "t": (3,), "corner": (2,)}
 
 
 def plus(left, right, scale=1):
@@ -165,16 +172,23 @@
     return here, ahead, left, right
 
 
-def needed_fields(terms, own):
+def needed_fields(stage):
     keys = collections.OrderedDict()
-    for _, halves in terms:
+    for _, halves in TERMS[stage]:
         for sign in (1, -1):
             for pair in term_fields(halves, sign):
                 keys.update((key, None) for key in pair)
-    for m in own:
+    for m in DIRECT[stage]:
         for scale in (1, 3):
             keys["x", 0, plus(ZERO, UNIT[m], scale)] = None
     return [key for key in keys if key[2] != ZERO]
+
+
+def stage_of(key):
+    dz, dt = key[2][2:]
+    if abs(dz) == 3 or (dz != 0 and dt != 0):
+        return "corner"
+    return "t" if dt != 0 else "z" if dz != 0 else "own"
 
 
 def lay_out(keys):
@@ -186,13 +200,16 @@
 
 
 def field_split():
-    near = needed_fields(NEAR_TERMS, (0, 1))
-    far = needed_fields(FAR_TERMS, (2, 3))
-    still = [key for key in far if key[2][3] == 0 and abs(key[2][2]) < 3]
-    shared = lay_out(still)
-    first = lay_out([key for key in near if key not in shared[0]])
-    second = lay_out([key for key in far if key not in shared[0]])
-    return shared, first, second
+    uses = collections.OrderedDict()
+    for stage in STAGES:
+        for key in needed_fields(stage):
+            uses.setdefault(key, []).append(stage)
+    shared, alone = {}, {}
+    for stage in STAGES:
+        built = [key for key in uses if stage_of(key) == stage]
+        shared[stage] = lay_out([key for key in built if uses[key] != [stage]])
+        alone[stage] = lay_out([key for key in built if uses[key] == [stage]])
+    return shared, alone
 
 
 def build_fields(locator, stores):
@@ -296,9 +313,9 @@
     return result
 
 
-def add_terms(fields, terms, near, acc):
+def add_terms(fields, stage, near, acc):
     started = set()
-    for target, halves in terms:
+    for target, halves in TERMS[stage]:
         for sign in (1, -1):
             here, ahead, left, right = term_fields(halves, sign)
             force = pole_sum(fields, here, ahead, near)
@@ -374,9 +391,46 @@
     write_messages(locator, plan, [("z", 2)], [second_ref])
 
 
-def pack_t_kernel(plan, names, near_in, far_in, weight_in, x_ref, u_ref, *rest):
-    outs = rest[: len(names)]
-    scale_ref, near_ref, far_ref, weight_ref, sems = rest[len(names) :]
+def pack_t_kernel(plan, names, x_ref, u_ref, *outs):
+    write_messages(Locator(plan, 1, {("own", "x"): x_ref, ("own", "u"): u_ref}), plan, names, outs)
+
+
+def corner_kernel(plan, names, within_ref, between_ref, _, ahead_ref, behind_ref, *outs):
+    def split(from_ahead, from_behind):
+        ahead_ref[...] = from_ahead[pl.ds(0, ahead_ref.shape[0]), :]
+        behind_ref[...] = from_behind[pl.ds(0, behind_ref.shape[0]), :]
+
+    @pl.when(odd_in_z())
+    def _():
+        split(between_ref, within_ref)
+
+    @pl.when(jnp.logical_not(odd_in_z()))
+    def _():
+        split(within_ref, between_ref)
+
+    locator = Locator(plan, 1, {("z", 1): ahead_ref, ("z", -1): behind_ref})
+    for name, out in zip(names, outs):
+        for reg, items in enumerate(plan[name].by_register()):
+            spots = [
+                item and (("z", item[0]),) + plan["z", item[0]].places[(0,) + item[1:]] for item in items
+            ]
+            out[pl.ds(8 * reg, 8), :] = locator.assemble(spots)
+
+
+def part_reg(ref, index, k):
+    return ref[pl.ds((9 * index + k) * 8, 8), :]
+
+
+def write_scales(near_ref, far_ref, weight_ref, scale_ref):
+    upper = lax.broadcasted_iota(jnp.int32, (8, LANES), 0) < 4
+    for p in range(NP):
+        scale_ref[pl.ds(8 * p, 8), :] = jnp.full((8, LANES), near_ref[p], F32)
+        scale_ref[pl.ds(8 * (NP + p), 8), :] = jnp.where(upper, near_ref[p], far_ref[p])
+        scale_ref[pl.ds(8 * (2 * NP + p), 8), :] = jnp.full((8, LANES), weight_ref[p], F32)
+
+
+def own_kernel(plan, t_size, near_in, far_in, weight_in, x_ref, u_ref, scale_ref, shared_ref, part_ref, *rest):
+    near_ref, far_ref, weight_ref, sems, alone_ref, acc = rest
     copies = [
         pltpu.make_async_copy(source, target, sems.at[index])
         for index, (source, target) in enumerate(
@@ -385,81 +439,96 @@
     ]
     for copy in copies:
         copy.start()
-    write_messages(Locator(plan, 1, {("own", "x"): x_ref, ("own", "u"): u_ref}), plan, names, outs)
+    shared, alone = field_split()
+    stores = [(shared_ref, shared["own"][0]), (alone_ref, alone["own"][0])]
+    build_fields(Locator(plan, t_size, {("own", "x"): x_ref, ("own", "u"): u_ref}), stores)
     for copy in copies:
         copy.wait()
-    upper = lax.broadcasted_iota(jnp.int32, (8, LANES), 0) < 4
-    for p in range(NP):
-        scale_ref[pl.ds(8 * p, 8), :] = jnp.full((8, LANES), near_ref[p], F32)
-        scale_ref[pl.ds(8 * (NP + p), 8), :] = jnp.where(upper, near_ref[p], far_ref[p])
-        scale_ref[pl.ds(8 * (2 * NP + p), 8), :] = jnp.full((8, LANES), weight_ref[p], F32)
-
-
-def corner_kernel(plan, names, within_ref, between_ref, second_ref, ahead_ref, behind_ref, *outs):
-    def split(from_ahead, from_behind):
-        ahead_ref[...] = from_ahead[pl.ds(0, ahead_ref.shape[0]), :]
-        behind_ref[...] = from_behind[pl.ds(0, behind_ref.shape[0]), :]
-
-    @pl.when(odd_in_z())
-    def _():
-        split(between_ref, within_ref)
-
-    @pl.when(jnp.logical_not(odd_in_z()))
-    def _():
-        split(within_ref, between_ref)
-
-    locator = Locator(plan, 1, {("z", 1): ahead_ref, ("z", -1): behind_ref})
-    for name, out in zip(names, outs):
-        for reg, items in enumerate(plan[name].by_register()):
-            spots = [
-                item and (("z", item[0]),) + plan["z", item[0]].places[(0,) + item[1:]] for item in items
-            ]
-            out[pl.ds(8 * reg, 8), :] = locator.assemble(spots)
-
-
-def near_kernel(plan, t_size, names, scale_ref, x_ref, u_ref, *rest):
-    received = rest[: len(names)]
-    shared_ref, part_ref, first_ref, acc = rest[len(names) :]
+    write_scales(near_ref, far_ref, weight_ref, scale_ref)
+    fields = Fields(x_ref, u_ref, stores)
+    near, both, weight = scale_tiles(scale_ref)
+    add_terms(fields, "own", near, acc)
+    direct = [own_force(fields, m, both) for m in DIRECT["own"]]
+    for k in range(9):
+        staples = fields.compact_halves(acc_tile(acc, 0, 2 * k), acc_tile(acc, 0, 2 * k + 1))
+        for m in range(2):
+            part_ref[pl.ds((9 * m + k) * 8, 8), :] = direct[m][k] + weight[m] * staples[m]
+
+
+def stage_setup(stage, plan, t_size, names, received, x_ref, u_ref, shared_refs, shared_ref, alone_ref):
     buffers = {("own", "x"): x_ref, ("own", "u"): u_ref}
     buffers.update(zip(names, received))
-    shared, first, _ = field_split()
-    stores = [(shared_ref, shared[0]), (first_ref, first[0])]
+    shared, alone = field_split()
+    stores = [(alone_ref, alone[stage][0])]
+    if shared_ref is not None:
+        stores.append((shared_ref, shared[stage][0]))
     build_fields(Locator(plan, t_size, buffers), stores)
-    fields = Fields(x_ref, u_ref, stores)
+    earlier = [(ref, shared[name][0]) for name, ref in zip(STAGES, shared_refs)]
+    return Fields(x_ref, u_ref, earlier + stores)
+
+
+def z_kernel(plan, t_size, names, scale_ref, x_ref, u_ref, own_shared, own_part, *rest):
+    received = rest[: len(names)]
+    shared_ref, part_ref, alone_ref, acc = rest[len(names) :]
+    fields = stage_setup("z", plan, t_size, names, received, x_ref, u_ref, [own_shared], shared_ref, alone_ref)
+    near, _, weight = scale_tiles(scale_ref)
+    add_terms(fields, "z", near, acc)
+    for k in range(9):
+        staples = fields.compact_halves(acc_tile(acc, 0, 2 * k), acc_tile(acc, 0, 2 * k + 1))
+        for m in range(2):
+            part_ref[pl.ds((9 * m + k) * 8, 8), :] = part_reg(own_part, m, k) + weight[m] * staples[m]
+        staple = fields.compact_sum(acc_tile(acc, 1, 2 * k), acc_tile(acc, 1, 2 * k + 1))
+        part_ref[pl.ds((18 + k) * 8, 8), :] = weight[2] * staple
+
+
+def t_kernel(plan, t_size, names, scale_ref, x_ref, u_ref, own_shared, z_shared, z_part, *rest):
+    received = rest[: len(names)]
+    shared_ref, part_ref, out_ref, alone_ref, acc, ready, sem = rest[len(names) :]
+    fields = stage_setup(
+        "t", plan, t_size, names, received, x_ref, u_ref, [own_shared, z_shared], shared_ref, alone_ref
+    )
     near, both, weight = scale_tiles(scale_ref)
-    add_terms(fields, NEAR_TERMS, near, acc)
-    own = [own_force(fields, m, both) for m in range(2)]
+    add_terms(fields, "t", near, acc)
     for k in range(9):
-        staples = list(fields.compact_halves(acc_tile(acc, 0, 2 * k), acc_tile(acc, 0, 2 * k + 1)))
-        staples.append(fields.compact_sum(acc_tile(acc, 1, 2 * k), acc_tile(acc, 1, 2 * k + 1)))
-        for m in range(3):
-            value = weight[m] * staples[m]
-            part_ref[pl.ds((9 * m + k) * 8, 8), :] = own[m][k] + value if m < 2 else value
-
-
-def far_kernel(plan, t_size, names, scale_ref, x_ref, u_ref, shared_ref, part_ref, *rest):
-    received = rest[: len(names)]
-    out_ref, second_ref, acc = rest[len(names) :]
-    buffers = {("own", "x"): x_ref, ("own", "u"): u_ref}
-    buffers.update(zip(names, received))
-    shared, _, second = field_split()
-    build_fields(Locator(plan, t_size, buffers), [(second_ref, second[0])])
-    fields = Fields(x_ref, u_ref, [(shared_ref, shared[0]), (second_ref, second[0])])
+        staples = fields.compact_halves(acc_tile(acc, 0, 2 * k), acc_tile(acc, 0, 2 * k + 1))
+        for m in range(2):
+            ready[pl.ds((9 * m + k) * 8, 8), :] = part_reg(z_part, m, k) + weight[m] * staples[m]
+    leaving = pltpu.make_async_copy(ready, out_ref.at[pl.ds(0, ready.shape[0])], sem)
+    leaving.start()
+    direct = own_force(fields, 3, both)
+    for k in range(9):
+        staple = fields.compact_sum(acc_tile(acc, 1, 2 * k), acc_tile(acc, 1, 2 * k + 1))
+        part_ref[pl.ds(k * 8, 8), :] = direct[k] + weight[3] * staple
+    leaving.wait()
+
+
+def last_kernel(plan, t_size, names, scale_ref, x_ref, u_ref, *rest):
+    own_shared, z_shared, t_shared, z_part, t_part, _ = rest[:6]
+    received = rest[6 : 6 + len(names)]
+    out_ref, alone_ref, acc, ready, sem = rest[6 + len(names) :]
+    fields = stage_setup(
+        "corner",
+        plan,
+        t_size,
+        names,
+        received,
+        x_ref,
+        u_ref,
+        [own_shared, z_shared, t_shared],
+        None,
+        alone_ref,
+    )
     near, both, weight = scale_tiles(scale_ref)
-    add_terms(fields, FAR_TERMS, near, acc)
-    own = [own_force(fields, m, both) for m in (2, 3)]
+    add_terms(fields, "corner", near, acc)
+    direct = own_force(fields, 2, both)
     for k in range(9):
-        pairs = [[acc_tile(acc, target, 2 * k + c) for c in range(2)] for target in range(3)]
-        in_x, in_y = fields.compact_halves(*pairs[0])
-        in_z, in_t = fields.compact_halves(*pairs[2])
-        in_t = in_t + fields.compact_sum(*pairs[1])
-        for m, staple in enumerate((in_x, in_y, in_z, in_t)):
-            value = weight[m] * staple
-            if m < 3:
-                value = value + part_ref[pl.ds((9 * m + k) * 8, 8), :]
-            if m > 1:
-                value = value + own[m - 2][k]
-            out_ref[pl.ds((9 * m + k) * 8, 8), :] = value
+        staples = fields.compact_halves(acc_tile(acc, 0, 2 * k), acc_tile(acc, 0, 2 * k + 1))
+        ready[pl.ds(k * 8, 8), :] = part_reg(z_part, 2, k) + direct[k] + weight[2] * staples[0]
+        ready[pl.ds((9 + k) * 8, 8), :] = part_reg(t_part, 0, k) + weight[3] * staples[1]
+    rows = ready.shape[0]
+    leaving = pltpu.make_async_copy(ready, out_ref.at[pl.ds(rows, rows)], sem)
+    leaving.start()
+    leaving.wait()
 
 
 def rows_of(count):
@@ -505,15 +574,35 @@
     received = {("z", 2): moved(("z", 2), beyond)}
     packed = pl.pallas_call(
         functools.partial(pack_t_kernel, plan, t_names),
-        out_shape=[rows_of(8 * plan[name].count) for name in t_names] + [rows_of(8 * 3 * NP)],
-        in_specs=[hbm] * 3 + [vmem] * 2,
-        out_specs=[vmem] * (len(t_names) + 1),
-        scratch_shapes=[pltpu.SMEM((NP,), F32)] * 3 + [pltpu.SemaphoreType.DMA((3,))],
+        out_shape=[rows_of(8 * plan[name].count) for name in t_names],
+        in_specs=[vmem] * 2,
+        out_specs=[vmem] * len(t_names),
         compiler_params=limit,
         name="pack_t",
+    )(*own)
+    received.update({name: moved(name, value) for name, value in zip(t_names, packed)})
+    shared, alone = field_split()
+    part_rows = 8 * REGS["u"]
+
+    def scratch(stage):
+        sums = 1 + max(target for target, _ in TERMS[stage])
+        return [pltpu.VMEM((alone[stage][1], LANES), F32), pltpu.VMEM((sums * 18 * 8, LANES), F32)]
+
+    def cost(micros):
+        return pl.CostEstimate(flops=10**6, bytes_accessed=int(3.69e6 * micros), transcendentals=0)
+
+    wide_limit = pltpu.CompilerParams(vmem_limit_bytes=6 * 1024 * 1024)
+    scale, own_shared, own_part = pl.pallas_call(
+        functools.partial(own_kernel, plan, t_size),
+        out_shape=[rows_of(8 * 3 * NP), rows_of(shared["own"][1]), rows_of(2 * part_rows)],
+        in_specs=[hbm] * 3 + [vmem] * 2,
+        out_specs=[vmem] * 3,
+        scratch_shapes=[pltpu.SMEM((NP,), F32)] * 3 + [pltpu.SemaphoreType.DMA((3,))] + scratch("own"),
+        cost_estimate=cost(COSTS["own"]),
+        compiler_params=wide_limit,
+        name="force_own",
     )(in_hbm(pole_coeff), in_hbm(naik_coeff), in_hbm(staple_weight), *own)
-    received.update({name: moved(name, value) for name, value in zip(t_names, packed)})
-    local = [packed[len(t_names)], *own]
+    local = [scale, *own]
     received["z", 1], received["z", -1], *corners = pl.pallas_call(
         functools.partial(corner_kernel, plan, corner_names),
         out_shape=[rows_of(ahead_rows), rows_of(behind_rows)]
@@ -522,30 +611,51 @@
         out_specs=[vmem] * (2 + len(corner_names)),
         compiler_params=limit,
         name="pack_corners",
-    )(within, between, received["z", 2])
+    )(within, between, scale)
     received.update({name: moved(name, value) for name, value in zip(corner_names, corners)})
-    shared, first, second = field_split()
-    near_names = [("z", 1), ("z", -1)]
-    shared_values, part = pl.pallas_call(
-        functools.partial(near_kernel, plan, t_size, near_names),
-        out_shape=[rows_of(shared[1]), rows_of(3 * 8 * REGS["u"])],
-        in_specs=[vmem] * (3 + len(near_names)),
+    names = [("z", 1), ("z", -1)]
+    z_shared, z_part = pl.pallas_call(
+        functools.partial(z_kernel, plan, t_size, names),
+        out_shape=[rows_of(shared["z"][1]), rows_of(3 * part_rows)],
+        in_specs=[vmem] * (5 + len(names)),
         out_specs=[vmem] * 2,
-        scratch_shapes=[pltpu.VMEM((first[1], LANES), F32), pltpu.VMEM((2 * 18 * 8, LANES), F32)],
-        cost_estimate=pl.CostEstimate(flops=4 * 10**6, bytes_accessed=4 * 10**6, transcendentals=0),
-        compiler_params=pltpu.CompilerParams(vmem_limit_bytes=8 * 1024 * 1024),
-        name="force_without_t",
-    )(*local, *[received[name] for name in near_names])
-    far_names = list(received)
+        scratch_shapes=scratch("z"),
+        cost_estimate=cost(COSTS["z"]),
+        compiler_params=wide_limit,
+        name="force_z",
+    )(*local, own_shared, own_part, *[received[name] for name in names])
+    t_shared, t_part, force = pl.pallas_call(
+        functools.partial(t_kernel, plan, t_size, t_names),
+        out_shape=[rows_of(shared["t"][1]), rows_of(part_rows), rows_of(u_rows)],
+        in_specs=[vmem] * (6 + len(t_names)),
+        out_specs=[vmem] * 2 + [hbm],
+        scratch_shapes=scratch("t") + [pltpu.VMEM((2 * part_rows, LANES), F32), pltpu.SemaphoreType.DMA],
+        cost_estimate=cost(COSTS["t"]),
+        compiler_params=wide_limit,
+        name="force_t",
+    )(*local, own_shared, z_shared, z_part, *[received[name] for name in t_names])
+    names = list(received)
     force = pl.pallas_call(
-        functools.partial(far_kernel, plan, t_size, far_names),
+        functools.partial(last_kernel, plan, t_size, names),
         out_shape=rows_of(u_rows),
-        in_specs=[vmem] * (5 + len(far_names)),
-        out_specs=vmem,
-        scratch_shapes=[pltpu.VMEM((second[1], LANES), F32), pltpu.VMEM((3 * 18 * 8, LANES), F32)],
-        compiler_params=pltpu.CompilerParams(vmem_limit_bytes=8 * 1024 * 1024),
-        name="force_with_t",
-    )(*local, shared_values, part, *[received[name] for name in far_names])
+        in_specs=[vmem] * 8 + [hbm] + [vmem] * len(names),
+        out_specs=hbm,
+        input_output_aliases={8: 0},
+        scratch_shapes=scratch("corner")
+        + [pltpu.VMEM((2 * part_rows, LANES), F32), pltpu.SemaphoreType.DMA],
+        cost_estimate=cost(COSTS["corner"]),
+        compiler_params=wide_limit,
+        name="force_corner",
+    )(
+        *local,
+        own_shared,
+        z_shared,
+        t_shared,
+        z_part,
+        t_part,
+        force,
+        *[received[name] for name in names],
+    )
     return force.reshape(gauge_links.shape)
 
 

time: 17.7 us -> 15.9 us (0.90)
  waiting for transfers between devices: 3.89 us -> 1.07 us
  Pallas kernels: 5.98 us -> 6.56 us
  starting transfers between devices: 7.61 us -> 8.09 us
    ppermute x1, waiting for transfers between devices: 2.93 us -> 1.06 us  [moved(): lax.ppermute(value, ('gz', 'gy'), [((i + step) % z_size, i) for i in rang...]
    pallas_call x2 -> x4, Pallas kernels: 4.31 us -> 5.56 us  [the longest x1 2.68 us: on_device(): pl.pallas_call(functools.partial(own_kernel, plan, t_size), out_shape=[ro...]
    ppermute x2, waiting for transfers between devices: 0.95 us -> 0.01 us  [moved(): lax.ppermute(value, 'ta', [((j + step) % t_size, j) for j in range(t_size)])]
    pallas_call x1, Pallas kernels: 0.71 us -> 0.01 us  [on_device(): pl.pallas_call(functools.partial(pack_t_kernel, plan, t_names), out_shape...]
    ppermute x2, starting transfers between devices: 2.16 us -> 2.65 us  [moved(): lax.ppermute(value, 'ta', [((j + step) % t_size, j) for j in range(t_size)])]
  transfers between devices with their start and end apart: 5 -> 5, of which waited for: 2 -> 1; matrix products, arithmetic and copies ran while one was open for 0% -> 0% of each run, Pallas kernels for 20% -> 29%
where the time goes in v6:
time: 15.9 us; the launch traced here: 15.8 us
  starting transfers between devices  8.09 us (51%)
  Pallas kernels  6.56 us (41%)
  waiting for transfers between devices  1.07 us (7%)
    ppermute x2, starting transfers between devices, exchanged(): return lax.ppermute(value, ('gz', 'gy'), pairs + [(j, i) for i, j in pairs])  4.56 us
    pallas_call x1, Pallas kernels, on_device(): pl.pallas_call(functools.partial(own_kernel, plan, t_size), out_shape=[ro...  2.68 us
    ppermute x2, starting transfers between devices, moved(): lax.ppermute(value, 'ta', [((j + step) % t_size, j) for j in range(t_size)])  2.65 us
    pallas_call x1, Pallas kernels, on_device(): pl.pallas_call(functools.partial(t_kernel, plan, t_size, t_names), out_sh...  1.28 us
    ppermute x1, waiting for transfers between devices, moved(): lax.ppermute(value, ('gz', 'gy'), [((i + step) % z_size, i) for i in rang...  1.06 us
    pallas_call x1, Pallas kernels, on_device(): pl.pallas_call(functools.partial(last_kernel, plan, t_size, names), out_s...  1.02 us
    pallas_call x1, Pallas kernels, on_device(): pl.pallas_call(functools.partial(pack_z_kernel, plan), out_shape=[rows_of...  0.94 us
    ppermute x1, starting transfers between devices, moved(): lax.ppermute(value, ('gz', 'gy'), [((i + step) % z_size, i) for i in rang...  0.89 us
  transfers between devices with their start and end apart: 5, of which 1 were waited for; matrix products, arithmetic and copies ran while one was open for 0% of the time, Pallas kernels for 29%

profile of v6, /device:TPU:0, one launch (start us, length us, event | category | flops | bytes accessed | tf_op | source)
XLA Modules:
  0.0 15.8 jit_solution(11550470531486757232)
XLA Ops:
  0.0 0.9 %pack_z.1 = (f32[208,128]{1,0:T(8,128)S(1)}, f32[216,128]{1,0:T(8,128)S(1)}, f32[48,128]{1,0:T(8,128)S(1)}, f32[96,128]{1,0:T(8,128)S(1)}, f32[288,128]{1,0:T(8,128)S(1)}) custom-call(f32[96,128]{1,0:T(8,128)} %bitcast.4, bf16[288,128]{1,0:T(8,128)(2,1)} %bitcast.3), custom_call_target="tpu_custom_call" | custom-call | tf_op jit(solution)/shard_map/pack_z/pallas_call | solution.py:563
  0.9 4.6 %collective-permute-start.1 = (f32[216,128]{1,0:T(8,128)S(1)}, f32[216,128]{1,0:T(8,128)S(1)}, u32[]{:S(2)}, u32[]{:S(2)}) collective-permute-start(f32[216,128]{1,0:T(8,128)S(1)} %get-tuple-element.27), channel_id=1, source_target_pairs={{1,4},{5,8},{9,12},{13,0},{4,1},{8,5},{12,9},{0,13},{3,6},{7,10},{... | collective-permute-start | bytes 331784 | tf_op jit(solution)/shard_map/ppermute | solution.py:555
  5.5 0.0 collective-permute-start
  5.5 1.6 %collective-permute-start.2 = (f32[240,128]{1,0:T(8,128)S(1)}, f32[240,128]{1,0:T(8,128)S(1)}, u32[]{:S(2)}, u32[]{:S(2)}) collective-permute-start(f32[240,128]{1,0:T(8,128)S(1)} %pack_t.1), channel_id=1, source_target_pairs={{2,0},{0,2},{3,1},{1,3},{6,4},{4,6},{7,5},{5,7},{10,8},{8,10},{11,... | collective-permute-start | bytes 368648 | tf_op jit(solution)/shard_map/ppermute | solution.py:551
  7.1 2.7 %force_own.1 = (f32[96,128]{1,0:T(8,128)S(1)}, f32[816,128]{1,0:T(8,128)S(1)}, f32[144,128]{1,0:T(8,128)S(1)}) custom-call(f32[4]{0:T(128)} %near_in.1, f32[4]{0:T(128)} %far_in.1, f32[4]{0:T(128)} %weight_in.1, f32[96,128]{1,0:T(8,128)S(1)} %get-tuple-element.21.x_ref, f32[288,128]{1,0:T(8,128)S(1)} %get-tuple-element.22.u_ref), custom_call_target="tpu_custom_call" | custom-call | flops 1000000 | bytes 7380000 | tf_op jit(solution)/shard_map/force_own/pallas_call | solution.py:595
  9.8 0.0 collective-permute-done.within_ref
  9.8 0.0 collective-permute-done.1.between_ref
  9.8 1.1 %collective-permute-start.4 = (f32[112,128]{1,0:T(8,128)S(1)}, f32[112,128]{1,0:T(8,128)S(1)}, u32[]{:S(2)}, u32[]{:S(2)}) collective-permute-start(f32[112,128]{1,0:T(8,128)S(1)} %get-tuple-element.36), channel_id=1, source_target_pairs={{2,0},{0,2},{3,1},{1,3},{6,4},{4,6},{7,5},{5,7},{10,8},{8,10},{11,... | collective-permute-start | bytes 172040 | tf_op jit(solution)/shard_map/ppermute | solution.py:551
  10.9 0.9 %collective-permute-start.3 = (f32[48,128]{1,0:T(8,128)S(1)}, f32[48,128]{1,0:T(8,128)S(1)}, u32[]{:S(2)}, u32[]{:S(2)}) collective-permute-start(f32[48,128]{1,0:T(8,128)S(1)} %get-tuple-element.35), channel_id=1, source_target_pairs={{4,0},{5,1},{8,4},{9,5},{12,8},{13,9},{0,12},{1,13},{6,2},{7,3},{1... | collective-permute-start | bytes 73736 | tf_op jit(solution)/shard_map/ppermute | solution.py:550
  11.8 0.6 %force_z.1 = (f32[336,128]{1,0:T(8,128)S(1)}, f32[216,128]{1,0:T(8,128)S(1)}) custom-call(f32[96,128]{1,0:T(8,128)S(1)} %get-tuple-element.23._.scale_ref, f32[96,128]{1,0:T(8,128)S(1)} %get-tuple-element.21.x_ref, f32[288,128]{1,0:T(8,128)S(1)} %get-tuple-element.22.u_ref, f32[816,128]{1,0:T(8,128)S(1)} %get-tuple-element.24.own_shared.rest_0_, ...), custom_call_target="tpu_custom_call" | custom-call | flops 1000000 | bytes 7380000 | tf_op jit(solution)/shard_map/force_z/pallas_call | solution.py:617
  12.4 0.0 collective-permute-done.2.rest_0_.rest_7_
  12.4 1.3 %force_t.1 = (f32[336,128]{1,0:T(8,128)S(1)}, f32[72,128]{1,0:T(8,128)S(1)}, f32[288,128]{1,0:T(8,128)}) custom-call(f32[96,128]{1,0:T(8,128)S(1)} %get-tuple-element.23._.scale_ref, f32[96,128]{1,0:T(8,128)S(1)} %get-tuple-element.21.x_ref, f32[288,128]{1,0:T(8,128)S(1)} %get-tuple-element.22.u_ref, f32[816,128]{1,0:T(8,128)S(1)} %get-tuple-element.24.own_shared.rest_0_, ...), custom_call_target="tpu_custom_call" | custom-call | flops 1000000 | bytes 7380000 | tf_op jit(solution)/shard_map/force_t/pallas_call | solution.py:627
  13.7 1.1 %collective-permute-done.3.rest_6_ = f32[48,128]{1,0:T(8,128)S(1)} collective-permute-done((f32[48,128]{1,0:T(8,128)S(1)}, f32[48,128]{1,0:T(8,128)S(1)}, u32[]{:S(2)}, u32[]{:S(2)}) %collective-permute-start.3) | collective-permute-done | bytes 24608 | tf_op jit(solution)/shard_map/ppermute | solution.py:550
  14.8 0.0 collective-permute-done.4.rest_10_
  14.8 1.0 %force_corner.1 = f32[288,128]{1,0:T(8,128)} custom-call(f32[96,128]{1,0:T(8,128)S(1)} %get-tuple-element.23._.scale_ref, f32[96,128]{1,0:T(8,128)S(1)} %get-tuple-element.21.x_ref, f32[288,128]{1,0:T(8,128)S(1)} %get-tuple-element.22.u_ref, f32[816,128]{1,0:T(8,128)S(1)} %get-tuple-element.24.own_shared.rest_0_, ...), custom_call_target="tpu_custom_call", output_to_operand_aliasing={{}: (8, {})} | custom-call | flops 1000000 | bytes 3690000 | tf_op jit(solution)/shard_map/force_corner/pallas_call | solution.py:638
  (2 shorter events, 0.1 us)
Async XLA Ops:
  0.9 8.8 %collective-permute-start.1 = (f32[216,128]{1,0:T(8,128)S(1)}, f32[216,128]{1,0:T(8,128)S(1)}, u32[]{:S(2)}, u32[]{:S(2)}) collective-permute-start(f32[216,128]{1,0:T(8,128)S(1)} %get-tuple-element.27), channel_id=1, source_target_pairs={{1,4},{5,8},{9,12},{13,0},{4,1},{8,5},{12,9},{0,13},{3,6},{7,10},{... | collective-permute-start | bytes 331784 | tf_op jit(solution)/shard_map/ppermute | solution.py:555
  5.5 4.3 %collective-permute-start = (f32[208,128]{1,0:T(8,128)S(1)}, f32[208,128]{1,0:T(8,128)S(1)}, u32[]{:S(2)}, u32[]{:S(2)}) collective-permute-start(f32[208,128]{1,0:T(8,128)S(1)} %get-tuple-element.26), channel_id=1, source_target_pairs={{0,1},{4,5},{8,9},{12,13},{1,0},{5,4},{9,8},{13,12},{2,3},{6,7},{1... | collective-permute-start | bytes 319496 | tf_op jit(solution)/shard_map/ppermute | solution.py:555
  5.5 6.9 %collective-permute-start.2 = (f32[240,128]{1,0:T(8,128)S(1)}, f32[240,128]{1,0:T(8,128)S(1)}, u32[]{:S(2)}, u32[]{:S(2)}) collective-permute-start(f32[240,128]{1,0:T(8,128)S(1)} %pack_t.1), channel_id=1, source_target_pairs={{2,0},{0,2},{3,1},{1,3},{6,4},{4,6},{7,5},{5,7},{10,8},{8,10},{11,... | collective-permute-start | bytes 368648 | tf_op jit(solution)/shard_map/ppermute | solution.py:551
  9.8 4.9 %collective-permute-start.4 = (f32[112,128]{1,0:T(8,128)S(1)}, f32[112,128]{1,0:T(8,128)S(1)}, u32[]{:S(2)}, u32[]{:S(2)}) collective-permute-start(f32[112,128]{1,0:T(8,128)S(1)} %get-tuple-element.36), channel_id=1, source_target_pairs={{2,0},{0,2},{3,1},{1,3},{6,4},{4,6},{7,5},{5,7},{10,8},{8,10},{11,... | collective-permute-start | bytes 172040 | tf_op jit(solution)/shard_map/ppermute | solution.py:551
  10.9 3.8 %collective-permute-start.3 = (f32[48,128]{1,0:T(8,128)S(1)}, f32[48,128]{1,0:T(8,128)S(1)}, u32[]{:S(2)}, u32[]{:S(2)}) collective-permute-start(f32[48,128]{1,0:T(8,128)S(1)} %get-tuple-element.35), channel_id=1, source_target_pairs={{4,0},{5,1},{8,4},{9,5},{12,8},{13,9},{0,12},{1,13},{6,2},{7,3},{1... | collective-permute-start | bytes 73736 | tf_op jit(solution)/shard_map/ppermute | solution.py:550

commit v7 on v6

--- a/solution.py
+++ b/solution.py
@@ -25,7 +25,7 @@
     "corner": ((0, ((2, 3), (3, 2))),),
 }
 COSTS = {"own": 2.0, "z": 2.0, "t": 2.0, "corner": 1.0}
-DIRECT = {"own": (0, 1), "z": (), "t": (3,), "corner": (2,)}
+DIRECT = {"own": (0, 1), "z": (2,), "t": (3,), "corner": ()}
 
 
 def plus(left, right, scale=1):
@@ -186,7 +186,7 @@
 
 def stage_of(key):
     dz, dt = key[2][2:]
-    if abs(dz) == 3 or (dz != 0 and dt != 0):
+    if dz != 0 and dt != 0:
         return "corner"
     return "t" if dt != 0 else "z" if dz != 0 else "own"
 
@@ -429,8 +429,8 @@
         scale_ref[pl.ds(8 * (2 * NP + p), 8), :] = jnp.full((8, LANES), weight_ref[p], F32)
 
 
-def own_kernel(plan, t_size, near_in, far_in, weight_in, x_ref, u_ref, scale_ref, shared_ref, part_ref, *rest):
-    near_ref, far_ref, weight_ref, sems, alone_ref, acc = rest
+def own_fields_kernel(plan, t_size, near_in, far_in, weight_in, x_ref, u_ref, scale_ref, shared_ref, alone_ref, *rest):
+    near_ref, far_ref, weight_ref, sems = rest
     copies = [
         pltpu.make_async_copy(source, target, sems.at[index])
         for index, (source, target) in enumerate(
@@ -445,7 +445,11 @@
     for copy in copies:
         copy.wait()
     write_scales(near_ref, far_ref, weight_ref, scale_ref)
-    fields = Fields(x_ref, u_ref, stores)
+
+
+def own_kernel(scale_ref, x_ref, u_ref, shared_ref, alone_ref, part_ref, acc):
+    shared, alone = field_split()
+    fields = Fields(x_ref, u_ref, [(shared_ref, shared["own"][0]), (alone_ref, alone["own"][0])])
     near, both, weight = scale_tiles(scale_ref)
     add_terms(fields, "own", near, acc)
     direct = [own_force(fields, m, both) for m in DIRECT["own"]]
@@ -471,14 +475,15 @@
     received = rest[: len(names)]
     shared_ref, part_ref, alone_ref, acc = rest[len(names) :]
     fields = stage_setup("z", plan, t_size, names, received, x_ref, u_ref, [own_shared], shared_ref, alone_ref)
-    near, _, weight = scale_tiles(scale_ref)
+    near, both, weight = scale_tiles(scale_ref)
     add_terms(fields, "z", near, acc)
+    direct = own_force(fields, 2, both)
     for k in range(9):
         staples = fields.compact_halves(acc_tile(acc, 0, 2 * k), acc_tile(acc, 0, 2 * k + 1))
         for m in range(2):
             part_ref[pl.ds((9 * m + k) * 8, 8), :] = part_reg(own_part, m, k) + weight[m] * staples[m]
         staple = fields.compact_sum(acc_tile(acc, 1, 2 * k), acc_tile(acc, 1, 2 * k + 1))
-        part_ref[pl.ds((18 + k) * 8, 8), :] = weight[2] * staple
+        part_ref[pl.ds((18 + k) * 8, 8), :] = direct[k] + weight[2] * staple
 
 
 def t_kernel(plan, t_size, names, scale_ref, x_ref, u_ref, own_shared, z_shared, z_part, *rest):
@@ -518,12 +523,11 @@
         None,
         alone_ref,
     )
-    near, both, weight = scale_tiles(scale_ref)
+    near, _, weight = scale_tiles(scale_ref)
     add_terms(fields, "corner", near, acc)
-    direct = own_force(fields, 2, both)
     for k in range(9):
         staples = fields.compact_halves(acc_tile(acc, 0, 2 * k), acc_tile(acc, 0, 2 * k + 1))
-        ready[pl.ds(k * 8, 8), :] = part_reg(z_part, 2, k) + direct[k] + weight[2] * staples[0]
+        ready[pl.ds(k * 8, 8), :] = part_reg(z_part, 2, k) + weight[2] * staples[0]
         ready[pl.ds((9 + k) * 8, 8), :] = part_reg(t_part, 0, k) + weight[3] * staples[1]
     rows = ready.shape[0]
     leaving = pltpu.make_async_copy(ready, out_ref.at[pl.ds(rows, rows)], sem)
@@ -558,11 +562,12 @@
     corner_names = [name for name in plan if name[0] == "c"]
     t_names = [name for name in first_names if name[0] == "t"]
     in_hbm = functools.partial(pltpu.with_memory_space_constraint, memory_space=pltpu.HBM)
+    beyond_rows = 8 * max([plan["z", 2].count] + [plan[name].count for name in corner_names])
     ahead_rows, behind_rows = [8 * plan["z", step].count for step in (1, -1)]
     shared_rows = max(ahead_rows, behind_rows)
     within, between, beyond, *own = pl.pallas_call(
         functools.partial(pack_z_kernel, plan),
-        out_shape=[rows_of(shared_rows), rows_of(shared_rows + 8), rows_of(8 * plan["z", 2].count)]
+        out_shape=[rows_of(shared_rows), rows_of(shared_rows + 8), rows_of(beyond_rows)]
         + [rows_of(x_rows), rows_of(u_rows)],
         in_specs=[hbm] * 2,
         out_specs=[vmem] * 5,
@@ -592,16 +597,25 @@
         return pl.CostEstimate(flops=10**6, bytes_accessed=int(3.69e6 * micros), transcendentals=0)
 
     wide_limit = pltpu.CompilerParams(vmem_limit_bytes=6 * 1024 * 1024)
-    scale, own_shared, own_part = pl.pallas_call(
-        functools.partial(own_kernel, plan, t_size),
-        out_shape=[rows_of(8 * 3 * NP), rows_of(shared["own"][1]), rows_of(2 * part_rows)],
+    scale, own_shared, own_alone = pl.pallas_call(
+        functools.partial(own_fields_kernel, plan, t_size),
+        out_shape=[rows_of(8 * 3 * NP), rows_of(shared["own"][1]), rows_of(alone["own"][1])],
         in_specs=[hbm] * 3 + [vmem] * 2,
         out_specs=[vmem] * 3,
-        scratch_shapes=[pltpu.SMEM((NP,), F32)] * 3 + [pltpu.SemaphoreType.DMA((3,))] + scratch("own"),
+        scratch_shapes=[pltpu.SMEM((NP,), F32)] * 3 + [pltpu.SemaphoreType.DMA((3,))],
+        compiler_params=wide_limit,
+        name="fields_own",
+    )(in_hbm(pole_coeff), in_hbm(naik_coeff), in_hbm(staple_weight), *own)
+    own_part = pl.pallas_call(
+        own_kernel,
+        out_shape=rows_of(2 * part_rows),
+        in_specs=[vmem] * 5,
+        out_specs=vmem,
+        scratch_shapes=scratch("own")[1:],
         cost_estimate=cost(COSTS["own"]),
         compiler_params=wide_limit,
         name="force_own",
-    )(in_hbm(pole_coeff), in_hbm(naik_coeff), in_hbm(staple_weight), *own)
+    )(scale, *own, own_shared, own_alone)
     local = [scale, *own]
     received["z", 1], received["z", -1], *corners = pl.pallas_call(
         functools.partial(corner_kernel, plan, corner_names),
@@ -611,9 +625,9 @@
         out_specs=[vmem] * (2 + len(corner_names)),
         compiler_params=limit,
         name="pack_corners",
-    )(within, between, scale)
+    )(within, between, own_part)
     received.update({name: moved(name, value) for name, value in zip(corner_names, corners)})
-    names = [("z", 1), ("z", -1)]
+    names = [("z", 1), ("z", -1), ("z", 2)]
     z_shared, z_part = pl.pallas_call(
         functools.partial(z_kernel, plan, t_size, names),
         out_shape=[rows_of(shared["z"][1]), rows_of(3 * part_rows)],
@@ -634,7 +648,7 @@
         compiler_params=wide_limit,
         name="force_t",
     )(*local, own_shared, z_shared, z_part, *[received[name] for name in t_names])
-    names = list(received)
+    names = [name for name in received if name != ("z", 2)]
     force = pl.pallas_call(
         functools.partial(last_kernel, plan, t_size, names),
         out_shape=rows_of(u_rows),

time: 15.9 us -> 15.7 us (0.987)
  waiting for transfers between devices: 1.07 us -> 1.69 us
  starting transfers between devices: 8.09 us -> 7.63 us
  Pallas kernels: 6.56 us -> 6.11 us
    ppermute x2, waiting for transfers between devices: 0.01 us -> 1.37 us  [moved(): lax.ppermute(value, 'ta', [((j + step) % t_size, j) for j in range(t_size)])]
    ppermute x1, waiting for transfers between devices: 1.06 us -> 0.32 us  [moved(): lax.ppermute(value, ('gz', 'gy'), [((i + step) % z_size, i) for i in rang...]
    ppermute x2, starting transfers between devices: 2.65 us -> 2.18 us  [moved(): lax.ppermute(value, 'ta', [((j + step) % t_size, j) for j in range(t_size)])]
    pallas_call x1 -> x2, Pallas kernels: 2.68 us -> 2.26 us  [the longest x1 1.9 us: on_device(): pl.pallas_call(functools.partial(own_fields_kernel, plan, t_size), out_sh...]
  transfers between devices with their start and end apart: 5 -> 5, of which waited for: 1 -> 2; matrix products, arithmetic and copies ran while one was open for 0% -> 0% of each run, Pallas kernels for 29% -> 27%
where the time goes in v7:
time: 15.7 us; the launch traced here: 15.5 us
  starting transfers between devices  7.63 us (49%)
  Pallas kernels  6.11 us (39%)
  waiting for transfers between devices  1.69 us (11%)
    ppermute x2, starting transfers between devices, exchanged(): return lax.ppermute(value, ('gz', 'gy'), pairs + [(j, i) for i, j in pairs])  4.56 us
    ppermute x2, starting transfers between devices, moved(): lax.ppermute(value, 'ta', [((j + step) % t_size, j) for j in range(t_size)])  2.18 us
    pallas_call x1, Pallas kernels, on_device(): pl.pallas_call(functools.partial(own_fields_kernel, plan, t_size), out_sh...  1.9 us
    ppermute x2, waiting for transfers between devices, moved(): lax.ppermute(value, 'ta', [((j + step) % t_size, j) for j in range(t_size)])  1.37 us
    pallas_call x1, Pallas kernels, on_device(): pl.pallas_call(functools.partial(t_kernel, plan, t_size, t_names), out_sh...  1.28 us
    pallas_call x1, Pallas kernels, on_device(): pl.pallas_call(functools.partial(last_kernel, plan, t_size, names), out_s...  0.95 us
    pallas_call x1, Pallas kernels, on_device(): pl.pallas_call(functools.partial(pack_z_kernel, plan), out_shape=[rows_of...  0.94 us
    ppermute x1, starting transfers between devices, moved(): lax.ppermute(value, ('gz', 'gy'), [((i + step) % z_size, i) for i in rang...  0.89 us
  transfers between devices with their start and end apart: 5, of which 2 were waited for; matrix products, arithmetic and copies ran while one was open for 0% of the time, Pallas kernels for 27%

profile of v7, /device:TPU:0, one launch (start us, length us, event | category | flops | bytes accessed | tf_op | source)
XLA Modules:
  0.0 15.5 jit_solution(14468322390098294588)
XLA Ops:
  0.0 0.9 %pack_z.1 = (f32[208,128]{1,0:T(8,128)S(1)}, f32[216,128]{1,0:T(8,128)S(1)}, f32[112,128]{1,0:T(8,128)S(1)}, f32[96,128]{1,0:T(8,128)S(1)}, f32[288,128]{1,0:T(8,128)S(1)}) custom-call(f32[96,128]{1,0:T(8,128)} %bitcast.4, bf16[288,128]{1,0:T(8,128)(2,1)} %bitcast.3), custom_call_target="tpu_custom_call" | custom-call | tf_op jit(solution)/shard_map/pack_z/pallas_call | solution.py:568
  0.9 4.6 %collective-permute-start.1 = (f32[216,128]{1,0:T(8,128)S(1)}, f32[216,128]{1,0:T(8,128)S(1)}, u32[]{:S(2)}, u32[]{:S(2)}) collective-permute-start(f32[216,128]{1,0:T(8,128)S(1)} %get-tuple-element.27), channel_id=1, source_target_pairs={{1,4},{5,8},{9,12},{13,0},{4,1},{8,5},{12,9},{0,13},{3,6},{7,10},{... | collective-permute-start | bytes 331784 | tf_op jit(solution)/shard_map/ppermute | solution.py:559
  5.5 0.0 collective-permute-start
  5.5 1.6 %collective-permute-start.3 = (f32[240,128]{1,0:T(8,128)S(1)}, f32[240,128]{1,0:T(8,128)S(1)}, u32[]{:S(2)}, u32[]{:S(2)}) collective-permute-start(f32[240,128]{1,0:T(8,128)S(1)} %pack_t.1), channel_id=1, source_target_pairs={{2,0},{0,2},{3,1},{1,3},{6,4},{4,6},{7,5},{5,7},{10,8},{8,10},{11,... | collective-permute-start | bytes 368648 | tf_op jit(solution)/shard_map/ppermute | solution.py:555
  7.1 0.9 %collective-permute-start.2 = (f32[112,128]{1,0:T(8,128)S(1)}, f32[112,128]{1,0:T(8,128)S(1)}, u32[]{:S(2)}, u32[]{:S(2)}) collective-permute-start(f32[112,128]{1,0:T(8,128)S(1)} %get-tuple-element.30), channel_id=1, source_target_pairs={{4,0},{5,1},{8,4},{9,5},{12,8},{13,9},{0,12},{1,13},{6,2},{7,3},{1... | collective-permute-start | bytes 172040 | tf_op jit(solution)/shard_map/ppermute | solution.py:554
  8.0 1.9 %fields_own.1 = (f32[96,128]{1,0:T(8,128)S(1)}, f32[816,128]{1,0:T(8,128)S(1)}, f32[768,128]{1,0:T(8,128)S(1)}) custom-call(f32[4]{0:T(128)} %near_in.1, f32[4]{0:T(128)} %far_in.1, f32[4]{0:T(128)} %weight_in.1, f32[96,128]{1,0:T(8,128)S(1)} %get-tuple-element.21.x_ref, f32[288,128]{1,0:T(8,128)S(1)} %get-tuple-element.22.u_ref), custom_call_target="tpu_custom_call" | custom-call | tf_op jit(solution)/shard_map/fields_own/pallas_call | solution.py:600
  9.9 0.4 %force_own.1._.own_part = f32[144,128]{1,0:T(8,128)S(1)} custom-call(f32[96,128]{1,0:T(8,128)S(1)} %get-tuple-element.23.scale_ref, f32[96,128]{1,0:T(8,128)S(1)} %get-tuple-element.21.x_ref, f32[288,128]{1,0:T(8,128)S(1)} %get-tuple-element.22.u_ref, f32[816,128]{1,0:T(8,128)S(1)} %get-tuple-element.24.shared_ref.own_shared.rest_0_, ...), custom_call_target="tpu_custom_call" | custom-call | flops 1000000 | bytes 7380000 | tf_op jit(solution)/shard_map/force_own/pallas_call | solution.py:609
  10.2 0.0 collective-permute-done.within_ref
  10.2 0.0 collective-permute-done.1.between_ref
  10.3 0.6 %collective-permute-start.4 = (f32[112,128]{1,0:T(8,128)S(1)}, f32[112,128]{1,0:T(8,128)S(1)}, u32[]{:S(2)}, u32[]{:S(2)}) collective-permute-start(f32[112,128]{1,0:T(8,128)S(1)} %get-tuple-element.36), channel_id=1, source_target_pairs={{2,0},{0,2},{3,1},{1,3},{6,4},{4,6},{7,5},{5,7},{10,8},{8,10},{11,... | collective-permute-start | bytes 172040 | tf_op jit(solution)/shard_map/ppermute | solution.py:555
  10.9 0.3 %collective-permute-done.2.rest_2_ = f32[112,128]{1,0:T(8,128)S(1)} collective-permute-done((f32[112,128]{1,0:T(8,128)S(1)}, f32[112,128]{1,0:T(8,128)S(1)}, u32[]{:S(2)}, u32[]{:S(2)}) %collective-permute-start.2) | collective-permute-done | bytes 57376 | tf_op jit(solution)/shard_map/ppermute | solution.py:554
  11.3 0.6 %force_z.1 = (f32[336,128]{1,0:T(8,128)S(1)}, f32[216,128]{1,0:T(8,128)S(1)}) custom-call(f32[96,128]{1,0:T(8,128)S(1)} %get-tuple-element.23.scale_ref, f32[96,128]{1,0:T(8,128)S(1)} %get-tuple-element.21.x_ref, f32[288,128]{1,0:T(8,128)S(1)} %get-tuple-element.22.u_ref, f32[816,128]{1,0:T(8,128)S(1)} %get-tuple-element.24.shared_ref.own_shared.rest_0_, ...), custom_call_target="tpu_custom_call" | custom-call | flops 1000000 | bytes 7380000 | tf_op jit(solution)/shard_map/force_z/pallas_call | solution.py:631
  11.9 0.0 collective-permute-done.3.rest_0_.rest_6_
  11.9 1.3 %force_t.1 = (f32[336,128]{1,0:T(8,128)S(1)}, f32[72,128]{1,0:T(8,128)S(1)}, f32[288,128]{1,0:T(8,128)}) custom-call(f32[96,128]{1,0:T(8,128)S(1)} %get-tuple-element.23.scale_ref, f32[96,128]{1,0:T(8,128)S(1)} %get-tuple-element.21.x_ref, f32[288,128]{1,0:T(8,128)S(1)} %get-tuple-element.22.u_ref, ...), custom_call_target="tpu_custom_call" | custom-call | flops 1000000 | bytes 7380000 | tf_op jit(solution)/shard_map/force_t/pallas_call | solution.py:641
  13.2 1.4 %collective-permute-done.4.rest_9_ = f32[112,128]{1,0:T(8,128)S(1)} collective-permute-done((f32[112,128]{1,0:T(8,128)S(1)}, f32[112,128]{1,0:T(8,128)S(1)}, u32[]{:S(2)}, u32[]{:S(2)}) %collective-permute-start.4) | collective-permute-done | bytes 57376 | tf_op jit(solution)/shard_map/ppermute | solution.py:555
  14.6 1.0 %force_corner.1 = f32[288,128]{1,0:T(8,128)} custom-call(f32[96,128]{1,0:T(8,128)S(1)} %get-tuple-element.23.scale_ref, f32[96,128]{1,0:T(8,128)S(1)} %get-tuple-element.21.x_ref, f32[288,128]{1,0:T(8,128)S(1)} %get-tuple-element.22.u_ref, f32[816,128]{1,0:T(8,128)S(1)} %get-tuple-element.24.shared_ref.own_shared.rest_0_, ...), custom_call_target="tpu_custom_call", output_to_operand_aliasing={{}: (8, {})} | custom-call | flops 1000000 | bytes 3690000 | tf_op jit(solution)/shard_map/force_corner/pallas_call | solution.py:652
  (2 shorter events, 0.1 us)
Async XLA Ops:
  0.9 9.3 %collective-permute-start.1 = (f32[216,128]{1,0:T(8,128)S(1)}, f32[216,128]{1,0:T(8,128)S(1)}, u32[]{:S(2)}, u32[]{:S(2)}) collective-permute-start(f32[216,128]{1,0:T(8,128)S(1)} %get-tuple-element.27), channel_id=1, source_target_pairs={{1,4},{5,8},{9,12},{13,0},{4,1},{8,5},{12,9},{0,13},{3,6},{7,10},{... | collective-permute-start | bytes 331784 | tf_op jit(solution)/shard_map/ppermute | solution.py:559
  5.5 4.7 %collective-permute-start = (f32[208,128]{1,0:T(8,128)S(1)}, f32[208,128]{1,0:T(8,128)S(1)}, u32[]{:S(2)}, u32[]{:S(2)}) collective-permute-start(f32[208,128]{1,0:T(8,128)S(1)} %get-tuple-element.26), channel_id=1, source_target_pairs={{0,1},{4,5},{8,9},{12,13},{1,0},{5,4},{9,8},{13,12},{2,3},{6,7},{1... | collective-permute-start | bytes 319496 | tf_op jit(solution)/shard_map/ppermute | solution.py:559
  5.5 6.4 %collective-permute-start.3 = (f32[240,128]{1,0:T(8,128)S(1)}, f32[240,128]{1,0:T(8,128)S(1)}, u32[]{:S(2)}, u32[]{:S(2)}) collective-permute-start(f32[240,128]{1,0:T(8,128)S(1)} %pack_t.1), channel_id=1, source_target_pairs={{2,0},{0,2},{3,1},{1,3},{6,4},{4,6},{7,5},{5,7},{10,8},{8,10},{11,... | collective-permute-start | bytes 368648 | tf_op jit(solution)/shard_map/ppermute | solution.py:555
  7.1 4.2 %collective-permute-start.2 = (f32[112,128]{1,0:T(8,128)S(1)}, f32[112,128]{1,0:T(8,128)S(1)}, u32[]{:S(2)}, u32[]{:S(2)}) collective-permute-start(f32[112,128]{1,0:T(8,128)S(1)} %get-tuple-element.30), channel_id=1, source_target_pairs={{4,0},{5,1},{8,4},{9,5},{12,8},{13,9},{0,12},{1,13},{6,2},{7,3},{1... | collective-permute-start | bytes 172040 | tf_op jit(solution)/shard_map/ppermute | solution.py:554
  10.3 4.2 %collective-permute-start.4 = (f32[112,128]{1,0:T(8,128)S(1)}, f32[112,128]{1,0:T(8,128)S(1)}, u32[]{:S(2)}, u32[]{:S(2)}) collective-permute-start(f32[112,128]{1,0:T(8,128)S(1)} %get-tuple-element.36), channel_id=1, source_target_pairs={{2,0},{0,2},{3,1},{1,3},{6,4},{4,6},{7,5},{5,7},{10,8},{8,10},{11,... | collective-permute-start | bytes 172040 | tf_op jit(solution)/shard_map/ppermute | solution.py:555

commit v8 on v7

--- a/solution.py
+++ b/solution.py
@@ -367,10 +367,14 @@
     return (lax.axis_index("gz") * lax.axis_size("gy") + lax.axis_index("gy")) % 2 == 1
 
 
-def pack_z_kernel(plan, x_in, u_in, within_ref, between_ref, second_ref, x_ref, u_ref, u_held, sems):
+def pack_z_kernel(plan, near_in, far_in, weight_in, x_in, u_in, *rest):
+    within_ref, between_ref, second_ref, scale_ref, x_ref, u_ref = rest[:6]
+    near_ref, far_ref, weight_ref, u_held, sems = rest[6:]
     copies = [
-        pltpu.make_async_copy(u_in, u_held, sems.at[0]),
-        pltpu.make_async_copy(x_in, x_ref, sems.at[1]),
+        pltpu.make_async_copy(source, target, sems.at[index])
+        for index, (source, target) in enumerate(
+            ((u_in, u_held), (x_in, x_ref), (near_in, near_ref), (far_in, far_ref), (weight_in, weight_ref))
+        )
     ]
     for copy in copies:
         copy.start()
@@ -389,6 +393,7 @@
         write_messages(locator, plan, names, (between_ref, within_ref))
 
     write_messages(locator, plan, [("z", 2)], [second_ref])
+    write_scales(near_ref, far_ref, weight_ref, scale_ref)
 
 
 def pack_t_kernel(plan, names, x_ref, u_ref, *outs):
@@ -429,22 +434,10 @@
         scale_ref[pl.ds(8 * (2 * NP + p), 8), :] = jnp.full((8, LANES), weight_ref[p], F32)
 
 
-def own_fields_kernel(plan, t_size, near_in, far_in, weight_in, x_ref, u_ref, scale_ref, shared_ref, alone_ref, *rest):
-    near_ref, far_ref, weight_ref, sems = rest
-    copies = [
-        pltpu.make_async_copy(source, target, sems.at[index])
-        for index, (source, target) in enumerate(
-            ((near_in, near_ref), (far_in, far_ref), (weight_in, weight_ref))
-        )
-    ]
-    for copy in copies:
-        copy.start()
+def own_fields_kernel(plan, t_size, x_ref, u_ref, shared_ref, alone_ref):
     shared, alone = field_split()
     stores = [(shared_ref, shared["own"][0]), (alone_ref, alone["own"][0])]
     build_fields(Locator(plan, t_size, {("own", "x"): x_ref, ("own", "u"): u_ref}), stores)
-    for copy in copies:
-        copy.wait()
-    write_scales(near_ref, far_ref, weight_ref, scale_ref)
 
 
 def own_kernel(scale_ref, x_ref, u_ref, shared_ref, alone_ref, part_ref, acc):
@@ -565,16 +558,23 @@
     beyond_rows = 8 * max([plan["z", 2].count] + [plan[name].count for name in corner_names])
     ahead_rows, behind_rows = [8 * plan["z", step].count for step in (1, -1)]
     shared_rows = max(ahead_rows, behind_rows)
-    within, between, beyond, *own = pl.pallas_call(
+    within, between, beyond, scale, *own = pl.pallas_call(
         functools.partial(pack_z_kernel, plan),
         out_shape=[rows_of(shared_rows), rows_of(shared_rows + 8), rows_of(beyond_rows)]
-        + [rows_of(x_rows), rows_of(u_rows)],
-        in_specs=[hbm] * 2,
-        out_specs=[vmem] * 5,
-        scratch_shapes=[pltpu.VMEM((u_rows, LANES), jnp.bfloat16), pltpu.SemaphoreType.DMA((2,))],
+        + [rows_of(8 * 3 * NP), rows_of(x_rows), rows_of(u_rows)],
+        in_specs=[hbm] * 5,
+        out_specs=[vmem] * 6,
+        scratch_shapes=[pltpu.SMEM((NP,), F32)] * 3
+        + [pltpu.VMEM((u_rows, LANES), jnp.bfloat16), pltpu.SemaphoreType.DMA((5,))],
         compiler_params=limit,
         name="pack_z",
-    )(in_hbm(pole_vectors.reshape((x_rows, LANES))), in_hbm(gauge_links.reshape((u_rows, LANES))))
+    )(
+        in_hbm(pole_coeff),
+        in_hbm(naik_coeff),
+        in_hbm(staple_weight),
+        in_hbm(pole_vectors.reshape((x_rows, LANES))),
+        in_hbm(gauge_links.reshape((u_rows, LANES))),
+    )
     between, within = exchanged(between, 1), exchanged(within, 0)
     received = {("z", 2): moved(("z", 2), beyond)}
     packed = pl.pallas_call(
@@ -597,15 +597,14 @@
         return pl.CostEstimate(flops=10**6, bytes_accessed=int(3.69e6 * micros), transcendentals=0)
 
     wide_limit = pltpu.CompilerParams(vmem_limit_bytes=6 * 1024 * 1024)
-    scale, own_shared, own_alone = pl.pallas_call(
+    own_shared, own_alone = pl.pallas_call(
         functools.partial(own_fields_kernel, plan, t_size),
-        out_shape=[rows_of(8 * 3 * NP), rows_of(shared["own"][1]), rows_of(alone["own"][1])],
-        in_specs=[hbm] * 3 + [vmem] * 2,
-        out_specs=[vmem] * 3,
-        scratch_shapes=[pltpu.SMEM((NP,), F32)] * 3 + [pltpu.SemaphoreType.DMA((3,))],
+        out_shape=[rows_of(shared["own"][1]), rows_of(alone["own"][1])],
+        in_specs=[vmem] * 2,
+        out_specs=[vmem] * 2,
         compiler_params=wide_limit,
         name="fields_own",
-    )(in_hbm(pole_coeff), in_hbm(naik_coeff), in_hbm(staple_weight), *own)
+    )(*own)
     own_part = pl.pallas_call(
         own_kernel,
         out_shape=rows_of(2 * part_rows),

time: 15.7 us -> 15.6 us (level)
  no operation moved by 1% of the time
where the time goes in v8:
time: 15.6 us; the launch traced here: 15.5 us
  starting transfers between devices  7.7 us (49%)
  Pallas kernels  6.11 us (39%)
  waiting for transfers between devices  1.62 us (10%)
    ppermute x2, starting transfers between devices, exchanged(): return lax.ppermute(value, ('gz', 'gy'), pairs + [(j, i) for i, j in pairs])  4.56 us
    ppermute x2, starting transfers between devices, moved(): lax.ppermute(value, 'ta', [((j + step) % t_size, j) for j in range(t_size)])  2.25 us
    pallas_call x1, Pallas kernels, on_device(): pl.pallas_call(functools.partial(own_fields_kernel, plan, t_size), out_sh...  1.83 us
    ppermute x2, waiting for transfers between devices, moved(): lax.ppermute(value, 'ta', [((j + step) % t_size, j) for j in range(t_size)])  1.3 us
    pallas_call x1, Pallas kernels, on_device(): pl.pallas_call(functools.partial(t_kernel, plan, t_size, t_names), out_sh...  1.29 us
    pallas_call x1, Pallas kernels, on_device(): pl.pallas_call(functools.partial(pack_z_kernel, plan), out_shape=[rows_of...  1 us
    pallas_call x1, Pallas kernels, on_device(): pl.pallas_call(functools.partial(last_kernel, plan, t_size, names), out_s...  0.95 us
    ppermute x1, starting transfers between devices, moved(): lax.ppermute(value, ('gz', 'gy'), [((i + step) % z_size, i) for i in rang...  0.89 us
  transfers between devices with their start and end apart: 5, of which 2 were waited for; matrix products, arithmetic and copies ran while one was open for 0% of the time, Pallas kernels for 27%

profile of v8, /device:TPU:0, one launch (start us, length us, event | category | flops | bytes accessed | tf_op | source)
XLA Modules:
  0.0 15.5 jit_solution(9525915051886275213)
XLA Ops:
  0.0 1.0 %pack_z.1 = (f32[208,128]{1,0:T(8,128)S(1)}, f32[216,128]{1,0:T(8,128)S(1)}, f32[112,128]{1,0:T(8,128)S(1)}, f32[96,128]{1,0:T(8,128)S(1)}, f32[96,128]{1,0:T(8,128)S(1)}, /*index=5*/f32[288,128]{1,0:T(8,128)S(1)}) custom-call(f32[4]{0:T(128)} %near_in.1, f32[4]{0:T(128)} %far_in.1, f32[4]{0:T(128)} %weight_in.1, f32[96,128]{1,0:T(8,128)} %bitcast.4, ...), custom_call_target="tpu_custom_call" | custom-call | tf_op jit(solution)/shard_map/pack_z/pallas_call | solution.py:561
  1.0 4.6 %collective-permute-start.1 = (f32[216,128]{1,0:T(8,128)S(1)}, f32[216,128]{1,0:T(8,128)S(1)}, u32[]{:S(2)}, u32[]{:S(2)}) collective-permute-start(f32[216,128]{1,0:T(8,128)S(1)} %get-tuple-element.27), channel_id=1, source_target_pairs={{1,4},{5,8},{9,12},{13,0},{4,1},{8,5},{12,9},{0,13},{3,6},{7,10},{... | collective-permute-start | bytes 331784 | tf_op jit(solution)/shard_map/ppermute | solution.py:552
  5.6 0.0 collective-permute-start
  5.6 1.6 %collective-permute-start.3 = (f32[240,128]{1,0:T(8,128)S(1)}, f32[240,128]{1,0:T(8,128)S(1)}, u32[]{:S(2)}, u32[]{:S(2)}) collective-permute-start(f32[240,128]{1,0:T(8,128)S(1)} %pack_t.1), channel_id=1, source_target_pairs={{2,0},{0,2},{3,1},{1,3},{6,4},{4,6},{7,5},{5,7},{10,8},{8,10},{11,... | collective-permute-start | bytes 368648 | tf_op jit(solution)/shard_map/ppermute | solution.py:548
  7.1 0.9 %collective-permute-start.2 = (f32[112,128]{1,0:T(8,128)S(1)}, f32[112,128]{1,0:T(8,128)S(1)}, u32[]{:S(2)}, u32[]{:S(2)}) collective-permute-start(f32[112,128]{1,0:T(8,128)S(1)} %get-tuple-element.30), channel_id=1, source_target_pairs={{4,0},{5,1},{8,4},{9,5},{12,8},{13,9},{0,12},{1,13},{6,2},{7,3},{1... | collective-permute-start | bytes 172040 | tf_op jit(solution)/shard_map/ppermute | solution.py:547
  8.0 1.8 %fields_own.1 = (f32[816,128]{1,0:T(8,128)S(1)}, f32[768,128]{1,0:T(8,128)S(1)}) custom-call(f32[96,128]{1,0:T(8,128)S(1)} %get-tuple-element.22.x_ref, f32[288,128]{1,0:T(8,128)S(1)} %get-tuple-element.23.u_ref), custom_call_target="tpu_custom_call" | custom-call | tf_op jit(solution)/shard_map/fields_own/pallas_call | solution.py:600
  9.9 0.4 %force_own.1._.own_part = f32[144,128]{1,0:T(8,128)S(1)} custom-call(f32[96,128]{1,0:T(8,128)S(1)} %get-tuple-element.21.scale_ref, f32[96,128]{1,0:T(8,128)S(1)} %get-tuple-element.22.x_ref, f32[288,128]{1,0:T(8,128)S(1)} %get-tuple-element.23.u_ref, f32[816,128]{1,0:T(8,128)S(1)} %get-tuple-element.24.shared_ref.own_shared.rest_0_, ...), custom_call_target="tpu_custom_call" | custom-call | flops 1000000 | bytes 7380000 | tf_op jit(solution)/shard_map/force_own/pallas_call | solution.py:608
  10.2 0.0 collective-permute-done.within_ref
  10.2 0.0 collective-permute-done.1.between_ref
  10.3 0.7 %collective-permute-start.4 = (f32[112,128]{1,0:T(8,128)S(1)}, f32[112,128]{1,0:T(8,128)S(1)}, u32[]{:S(2)}, u32[]{:S(2)}) collective-permute-start(f32[112,128]{1,0:T(8,128)S(1)} %get-tuple-element.36), channel_id=1, source_target_pairs={{2,0},{0,2},{3,1},{1,3},{6,4},{4,6},{7,5},{5,7},{10,8},{8,10},{11,... | collective-permute-start | bytes 172040 | tf_op jit(solution)/shard_map/ppermute | solution.py:548
  11.0 0.3 %collective-permute-done.2.rest_2_ = f32[112,128]{1,0:T(8,128)S(1)} collective-permute-done((f32[112,128]{1,0:T(8,128)S(1)}, f32[112,128]{1,0:T(8,128)S(1)}, u32[]{:S(2)}, u32[]{:S(2)}) %collective-permute-start.2) | collective-permute-done | bytes 57376 | tf_op jit(solution)/shard_map/ppermute | solution.py:547
  11.3 0.6 %force_z.1 = (f32[336,128]{1,0:T(8,128)S(1)}, f32[216,128]{1,0:T(8,128)S(1)}) custom-call(f32[96,128]{1,0:T(8,128)S(1)} %get-tuple-element.21.scale_ref, f32[96,128]{1,0:T(8,128)S(1)} %get-tuple-element.22.x_ref, f32[288,128]{1,0:T(8,128)S(1)} %get-tuple-element.23.u_ref, f32[816,128]{1,0:T(8,128)S(1)} %get-tuple-element.24.shared_ref.own_shared.rest_0_, ...), custom_call_target="tpu_custom_call" | custom-call | flops 1000000 | bytes 7380000 | tf_op jit(solution)/shard_map/force_z/pallas_call | solution.py:630
  11.9 0.0 collective-permute-done.3.rest_0_.rest_6_
  12.0 1.3 %force_t.1 = (f32[336,128]{1,0:T(8,128)S(1)}, f32[72,128]{1,0:T(8,128)S(1)}, f32[288,128]{1,0:T(8,128)}) custom-call(f32[96,128]{1,0:T(8,128)S(1)} %get-tuple-element.21.scale_ref, f32[96,128]{1,0:T(8,128)S(1)} %get-tuple-element.22.x_ref, f32[288,128]{1,0:T(8,128)S(1)} %get-tuple-element.23.u_ref, ...), custom_call_target="tpu_custom_call" | custom-call | flops 1000000 | bytes 7380000 | tf_op jit(solution)/shard_map/force_t/pallas_call | solution.py:640
  13.3 1.3 %collective-permute-done.4.rest_9_ = f32[112,128]{1,0:T(8,128)S(1)} collective-permute-done((f32[112,128]{1,0:T(8,128)S(1)}, f32[112,128]{1,0:T(8,128)S(1)}, u32[]{:S(2)}, u32[]{:S(2)}) %collective-permute-start.4) | collective-permute-done | bytes 57376 | tf_op jit(solution)/shard_map/ppermute | solution.py:548
  14.5 1.0 %force_corner.1 = f32[288,128]{1,0:T(8,128)} custom-call(f32[96,128]{1,0:T(8,128)S(1)} %get-tuple-element.21.scale_ref, f32[96,128]{1,0:T(8,128)S(1)} %get-tuple-element.22.x_ref, f32[288,128]{1,0:T(8,128)S(1)} %get-tuple-element.23.u_ref, f32[816,128]{1,0:T(8,128)S(1)} %get-tuple-element.24.shared_ref.own_shared.rest_0_, ...), custom_call_target="tpu_custom_call", output_to_operand_aliasing={{}: (8, {})} | custom-call | flops 1000000 | bytes 3690000 | tf_op jit(solution)/shard_map/force_corner/pallas_call | solution.py:651
  (2 shorter events, 0.1 us)
Async XLA Ops:
  1.0 9.2 %collective-permute-start.1 = (f32[216,128]{1,0:T(8,128)S(1)}, f32[216,128]{1,0:T(8,128)S(1)}, u32[]{:S(2)}, u32[]{:S(2)}) collective-permute-start(f32[216,128]{1,0:T(8,128)S(1)} %get-tuple-element.27), channel_id=1, source_target_pairs={{1,4},{5,8},{9,12},{13,0},{4,1},{8,5},{12,9},{0,13},{3,6},{7,10},{... | collective-permute-start | bytes 331784 | tf_op jit(solution)/shard_map/ppermute | solution.py:552
  5.6 4.7 %collective-permute-start = (f32[208,128]{1,0:T(8,128)S(1)}, f32[208,128]{1,0:T(8,128)S(1)}, u32[]{:S(2)}, u32[]{:S(2)}) collective-permute-start(f32[208,128]{1,0:T(8,128)S(1)} %get-tuple-element.26), channel_id=1, source_target_pairs={{0,1},{4,5},{8,9},{12,13},{1,0},{5,4},{9,8},{13,12},{2,3},{6,7},{1... | collective-permute-start | bytes 319496 | tf_op jit(solution)/shard_map/ppermute | solution.py:552
  5.6 6.4 %collective-permute-start.3 = (f32[240,128]{1,0:T(8,128)S(1)}, f32[240,128]{1,0:T(8,128)S(1)}, u32[]{:S(2)}, u32[]{:S(2)}) collective-permute-start(f32[240,128]{1,0:T(8,128)S(1)} %pack_t.1), channel_id=1, source_target_pairs={{2,0},{0,2},{3,1},{1,3},{6,4},{4,6},{7,5},{5,7},{10,8},{8,10},{11,... | collective-permute-start | bytes 368648 | tf_op jit(solution)/shard_map/ppermute | solution.py:548
  7.1 4.2 %collective-permute-start.2 = (f32[112,128]{1,0:T(8,128)S(1)}, f32[112,128]{1,0:T(8,128)S(1)}, u32[]{:S(2)}, u32[]{:S(2)}) collective-permute-start(f32[112,128]{1,0:T(8,128)S(1)} %get-tuple-element.30), channel_id=1, source_target_pairs={{4,0},{5,1},{8,4},{9,5},{12,8},{13,9},{0,12},{1,13},{6,2},{7,3},{1... | collective-permute-start | bytes 172040 | tf_op jit(solution)/shard_map/ppermute | solution.py:547
  10.3 4.2 %collective-permute-start.4 = (f32[112,128]{1,0:T(8,128)S(1)}, f32[112,128]{1,0:T(8,128)S(1)}, u32[]{:S(2)}, u32[]{:S(2)}) collective-permute-start(f32[112,128]{1,0:T(8,128)S(1)} %get-tuple-element.36), channel_id=1, source_target_pairs={{2,0},{0,2},{3,1},{1,3},{6,4},{4,6},{7,5},{5,7},{10,8},{8,10},{11,... | collective-permute-start | bytes 172040 | tf_op jit(solution)/shard_map/ppermute | solution.py:548

commit v9 on v8

--- a/solution.py
+++ b/solution.py
@@ -148,18 +148,6 @@
         return self.assemble([self.find(kind, n, k, t + dt, z + dz) for t, z in SITES])
 
 
-def lane_shifted(value, dx, dy):
-    if dx != 0:
-        x_at = lax.broadcasted_iota(jnp.int32, value.shape, 1) % NX
-        beyond = (x_at + dx >= NX) | (x_at + dx < 0)
-        main = pltpu.roll(value, (-dx) % LANES, 1)
-        wrapped = pltpu.roll(value, (NX - dx if dx > 0 else -NX - dx) % LANES, 1)
-        value = jnp.where(beyond, wrapped, main)
-    if dy != 0:
-        value = pltpu.roll(value, (-dy * NX) % LANES, 1)
-    return value
-
-
 def term_fields(halves, sign):
     here, ahead, left, right = [], [], [], []
     for m, n in halves:
@@ -212,20 +200,51 @@
     return shared, alone
 
 
-def build_fields(locator, stores):
+def all_shifts():
+    found = collections.OrderedDict()
+    for stage in STAGES:
+        for _, _, (dx, dy, _, _) in needed_fields(stage):
+            if (dx, dy) != (0, 0):
+                found[dx, dy] = None
+    return list(found)
+
+
+def write_shifts(perm_ref):
+    lane = lax.broadcasted_iota(jnp.int32, (LANES, LANES), 1)
+    source = lax.broadcasted_iota(jnp.int32, (LANES, LANES), 0)
+    for index, (dx, dy) in enumerate(all_shifts()):
+        wanted = (lane // NX + dy + NY) % NY * NX + (lane + dx + NX) % NX
+        perm_ref[pl.ds(index * LANES, LANES), :] = (source == wanted).astype(F32).astype(jnp.bfloat16)
+
+
+def parts_of(kind, value):
+    if kind == "u":
+        return [value.astype(jnp.bfloat16)]
+    high = value.astype(jnp.bfloat16)
+    rest = value - high.astype(F32)
+    middle = rest.astype(jnp.bfloat16)
+    return [high, middle, (rest - middle.astype(F32)).astype(jnp.bfloat16)]
+
+
+def build_fields(locator, perm_ref, stores):
     groups = collections.OrderedDict()
     for ref, rows in stores:
         for (kind, n, disp), row in rows.items():
             shifts = groups.setdefault((kind, n, disp[3], disp[2]), collections.OrderedDict())
             shifts[disp[0], disp[1]] = (ref, row)
+    order = all_shifts()
     for (kind, n, dt, dz), shifts in groups.items():
-        for k in range(REGS[kind]):
-            value = locator.field_register(kind, n, k, dt, dz)
-            by_x = {0: value}
-            for (dx, dy), (ref, row) in shifts.items():
-                if dx not in by_x:
-                    by_x[dx] = lane_shifted(value, dx, 0)
-                ref[pl.ds(row + 8 * k, 8), :] = lane_shifted(by_x[dx], 0, dy)
+        regs = [locator.field_register(kind, n, k, dt, dz) for k in range(REGS[kind])]
+        if (0, 0) in shifts:
+            ref, row = shifts[0, 0]
+            for k, value in enumerate(regs):
+                ref[pl.ds(row + 8 * k, 8), :] = value
+        parts = parts_of(kind, jnp.concatenate(regs, axis=0))
+        for shift, (ref, row) in shifts.items():
+            if shift != (0, 0):
+                perm = perm_ref[pl.ds(order.index(shift) * LANES, LANES), :]
+                moved = [jnp.dot(part, perm, preferred_element_type=F32) for part in parts]
+                ref[pl.ds(row, 8 * REGS[kind]), :] = functools.reduce(jnp.add, moved)
 
 
 class Fields:
@@ -368,8 +387,8 @@
 
 
 def pack_z_kernel(plan, near_in, far_in, weight_in, x_in, u_in, *rest):
-    within_ref, between_ref, second_ref, scale_ref, x_ref, u_ref = rest[:6]
-    near_ref, far_ref, weight_ref, u_held, sems = rest[6:]
+    within_ref, between_ref, second_ref, scale_ref, perm_ref, x_ref, u_ref = rest[:7]
+    near_ref, far_ref, weight_ref, u_held, sems = rest[7:]
     copies = [
         pltpu.make_async_copy(source, target, sems.at[index])
         for index, (source, target) in enumerate(
@@ -378,6 +397,7 @@
     ]
     for copy in copies:
         copy.start()
+    write_shifts(perm_ref)
     for copy in copies:
         copy.wait()
     u_ref[...] = u_held[...].astype(F32)
@@ -434,10 +454,10 @@
         scale_ref[pl.ds(8 * (2 * NP + p), 8), :] = jnp.full((8, LANES), weight_ref[p], F32)
 
 
-def own_fields_kernel(plan, t_size, x_ref, u_ref, shared_ref, alone_ref):
+def own_fields_kernel(plan, t_size, perm_ref, x_ref, u_ref, shared_ref, alone_ref):
     shared, alone = field_split()
     stores = [(shared_ref, shared["own"][0]), (alone_ref, alone["own"][0])]
-    build_fields(Locator(plan, t_size, {("own", "x"): x_ref, ("own", "u"): u_ref}), stores)
+    build_fields(Locator(plan, t_size, {("own", "x"): x_ref, ("own", "u"): u_ref}), perm_ref, stores)
 
 
 def own_kernel(scale_ref, x_ref, u_ref, shared_ref, alone_ref, part_ref, acc):
@@ -452,22 +472,24 @@
             part_ref[pl.ds((9 * m + k) * 8, 8), :] = direct[m][k] + weight[m] * staples[m]
 
 
-def stage_setup(stage, plan, t_size, names, received, x_ref, u_ref, shared_refs, shared_ref, alone_ref):
+def stage_setup(stage, plan, t_size, names, received, perm_ref, x_ref, u_ref, shared_refs, shared_ref, alone_ref):
     buffers = {("own", "x"): x_ref, ("own", "u"): u_ref}
     buffers.update(zip(names, received))
     shared, alone = field_split()
     stores = [(alone_ref, alone[stage][0])]
     if shared_ref is not None:
         stores.append((shared_ref, shared[stage][0]))
-    build_fields(Locator(plan, t_size, buffers), stores)
+    build_fields(Locator(plan, t_size, buffers), perm_ref, stores)
     earlier = [(ref, shared[name][0]) for name, ref in zip(STAGES, shared_refs)]
     return Fields(x_ref, u_ref, earlier + stores)
 
 
-def z_kernel(plan, t_size, names, scale_ref, x_ref, u_ref, own_shared, own_part, *rest):
+def z_kernel(plan, t_size, names, scale_ref, perm_ref, x_ref, u_ref, own_shared, own_part, *rest):
     received = rest[: len(names)]
     shared_ref, part_ref, alone_ref, acc = rest[len(names) :]
-    fields = stage_setup("z", plan, t_size, names, received, x_ref, u_ref, [own_shared], shared_ref, alone_ref)
+    fields = stage_setup(
+        "z", plan, t_size, names, received, perm_ref, x_ref, u_ref, [own_shared], shared_ref, alone_ref
+    )
     near, both, weight = scale_tiles(scale_ref)
     add_terms(fields, "z", near, acc)
     direct = own_force(fields, 2, both)
@@ -479,11 +501,11 @@
         part_ref[pl.ds((18 + k) * 8, 8), :] = direct[k] + weight[2] * staple
 
 
-def t_kernel(plan, t_size, names, scale_ref, x_ref, u_ref, own_shared, z_shared, z_part, *rest):
+def t_kernel(plan, t_size, names, scale_ref, perm_ref, x_ref, u_ref, own_shared, z_shared, z_part, *rest):
     received = rest[: len(names)]
     shared_ref, part_ref, out_ref, alone_ref, acc, ready, sem = rest[len(names) :]
     fields = stage_setup(
-        "t", plan, t_size, names, received, x_ref, u_ref, [own_shared, z_shared], shared_ref, alone_ref
+        "t", plan, t_size, names, received, perm_ref, x_ref, u_ref, [own_shared, z_shared], shared_ref, alone_ref
     )
     near, both, weight = scale_tiles(scale_ref)
     add_terms(fields, "t", near, acc)
@@ -500,7 +522,7 @@
     leaving.wait()
 
 
-def last_kernel(plan, t_size, names, scale_ref, x_ref, u_ref, *rest):
+def last_kernel(plan, t_size, names, scale_ref, perm_ref, x_ref, u_ref, *rest):
     own_shared, z_shared, t_shared, z_part, t_part, _ = rest[:6]
     received = rest[6 : 6 + len(names)]
     out_ref, alone_ref, acc, ready, sem = rest[6 + len(names) :]
@@ -510,6 +532,7 @@
         t_size,
         names,
         received,
+        perm_ref,
         x_ref,
         u_ref,
         [own_shared, z_shared, t_shared],
@@ -558,12 +581,17 @@
     beyond_rows = 8 * max([plan["z", 2].count] + [plan[name].count for name in corner_names])
     ahead_rows, behind_rows = [8 * plan["z", step].count for step in (1, -1)]
     shared_rows = max(ahead_rows, behind_rows)
-    within, between, beyond, scale, *own = pl.pallas_call(
+    within, between, beyond, scale, perm, *own = pl.pallas_call(
         functools.partial(pack_z_kernel, plan),
         out_shape=[rows_of(shared_rows), rows_of(shared_rows + 8), rows_of(beyond_rows)]
-        + [rows_of(8 * 3 * NP), rows_of(x_rows), rows_of(u_rows)],
+        + [
+            rows_of(8 * 3 * NP),
+            jax.ShapeDtypeStruct((len(all_shifts()) * LANES, LANES), jnp.bfloat16),
+            rows_of(x_rows),
+            rows_of(u_rows),
+        ],
         in_specs=[hbm] * 5,
-        out_specs=[vmem] * 6,
+        out_specs=[vmem] * 7,
         scratch_shapes=[pltpu.SMEM((NP,), F32)] * 3
         + [pltpu.VMEM((u_rows, LANES), jnp.bfloat16), pltpu.SemaphoreType.DMA((5,))],
         compiler_params=limit,
@@ -600,11 +628,11 @@
     own_shared, own_alone = pl.pallas_call(
         functools.partial(own_fields_kernel, plan, t_size),
         out_shape=[rows_of(shared["own"][1]), rows_of(alone["own"][1])],
-        in_specs=[vmem] * 2,
+        in_specs=[vmem] * 3,
         out_specs=[vmem] * 2,
         compiler_params=wide_limit,
         name="fields_own",
-    )(*own)
+    )(perm, *own)
     own_part = pl.pallas_call(
         own_kernel,
         out_shape=rows_of(2 * part_rows),
@@ -615,7 +643,7 @@
         compiler_params=wide_limit,
         name="force_own",
     )(scale, *own, own_shared, own_alone)
-    local = [scale, *own]
+    local = [scale, perm, *own]
     received["z", 1], received["z", -1], *corners = pl.pallas_call(
         functools.partial(corner_kernel, plan, corner_names),
         out_shape=[rows_of(ahead_rows), rows_of(behind_rows)]
@@ -630,7 +658,7 @@
     z_shared, z_part = pl.pallas_call(
         functools.partial(z_kernel, plan, t_size, names),
         out_shape=[rows_of(shared["z"][1]), rows_of(3 * part_rows)],
-        in_specs=[vmem] * (5 + len(names)),
+        in_specs=[vmem] * (6 + len(names)),
         out_specs=[vmem] * 2,
         scratch_shapes=scratch("z"),
         cost_estimate=cost(COSTS["z"]),
@@ -640,7 +668,7 @@
     t_shared, t_part, force = pl.pallas_call(
         functools.partial(t_kernel, plan, t_size, t_names),
         out_shape=[rows_of(shared["t"][1]), rows_of(part_rows), rows_of(u_rows)],
-        in_specs=[vmem] * (6 + len(t_names)),
+        in_specs=[vmem] * (7 + len(t_names)),
         out_specs=[vmem] * 2 + [hbm],
         scratch_shapes=scratch("t") + [pltpu.VMEM((2 * part_rows, LANES), F32), pltpu.SemaphoreType.DMA],
         cost_estimate=cost(COSTS["t"]),
@@ -651,9 +679,9 @@
     force = pl.pallas_call(
         functools.partial(last_kernel, plan, t_size, names),
         out_shape=rows_of(u_rows),
-        in_specs=[vmem] * 8 + [hbm] + [vmem] * len(names),
+        in_specs=[vmem] * 9 + [hbm] + [vmem] * len(names),
         out_specs=hbm,
-        input_output_aliases={8: 0},
+        input_output_aliases={9: 0},
         scratch_shapes=scratch("corner")
         + [pltpu.VMEM((2 * part_rows, LANES), F32), pltpu.SemaphoreType.DMA],
         cost_estimate=cost(COSTS["corner"]),

time: 15.6 us -> 14.5 us (0.929)
  starting transfers between devices: 7.7 us -> 9.04 us
  waiting for transfers between devices: 1.62 us -> 0.33 us
  Pallas kernels: 6.11 us -> 4.93 us
    pallas_call x1, Pallas kernels: 1.83 us -> 0.48 us  [on_device(): pl.pallas_call(functools.partial(own_fields_kernel, plan, t_size), out_sh...]
    ppermute x2, starting transfers between devices: 2.25 us -> 3.59 us  [moved(): lax.ppermute(value, 'ta', [((j + step) % t_size, j) for j in range(t_size)])]
    ppermute x2, waiting for transfers between devices: 1.3 us -> 0.01 us  [moved(): lax.ppermute(value, 'ta', [((j + step) % t_size, j) for j in range(t_size)])]
  transfers between devices with their start and end apart: 5 -> 5, of which waited for: 2 -> 1; matrix products, arithmetic and copies ran while one was open for 0% -> 0% of each run, Pallas kernels for 27% -> 21%
where the time goes in v9:
time: 14.5 us; the launch traced here: 14.4 us
  starting transfers between devices  9.04 us (62%)
  Pallas kernels  4.93 us (34%)
  waiting for transfers between devices  0.33 us (2%)
    ppermute x2, starting transfers between devices, exchanged(): return lax.ppermute(value, ('gz', 'gy'), pairs + [(j, i) for i, j in pairs])  4.56 us
    ppermute x2, starting transfers between devices, moved(): lax.ppermute(value, 'ta', [((j + step) % t_size, j) for j in range(t_size)])  3.59 us
    pallas_call x1, Pallas kernels, on_device(): pl.pallas_call(functools.partial(t_kernel, plan, t_size, t_names), out_sh...  1.32 us
    pallas_call x1, Pallas kernels, on_device(): pl.pallas_call(functools.partial(pack_z_kernel, plan), out_shape=[rows_of...  1 us
    pallas_call x1, Pallas kernels, on_device(): pl.pallas_call(functools.partial(last_kernel, plan, t_size, names), out_s...  0.96 us
    ppermute x1, starting transfers between devices, moved(): lax.ppermute(value, ('gz', 'gy'), [((i + step) % z_size, i) for i in rang...  0.89 us
    pallas_call x1, Pallas kernels, on_device(): pl.pallas_call(functools.partial(z_kernel, plan, t_size, names), out_shap...  0.75 us
    pallas_call x1, Pallas kernels, on_device(): pl.pallas_call(functools.partial(own_fields_kernel, plan, t_size), out_sh...  0.48 us
  transfers between devices with their start and end apart: 5, of which 1 were waited for; matrix products, arithmetic and copies ran while one was open for 0% of the time, Pallas kernels for 21%

profile of v9, /device:TPU:0, one launch (start us, length us, event | category | flops | bytes accessed | tf_op | source)
XLA Modules:
  0.0 14.4 jit_solution(14321047604963329240)
XLA Ops:
  0.0 1.0 %pack_z.1 = (f32[208,128]{1,0:T(8,128)S(1)}, f32[216,128]{1,0:T(8,128)S(1)}, f32[112,128]{1,0:T(8,128)S(1)}, f32[96,128]{1,0:T(8,128)S(1)}, bf16[1152,128]{1,0:T...) custom-call(f32[4]{0:T(128)} %near_in.1, f32[4]{0:T(128)} %far_in.1, f32[4]{0:T(128)} %weight_in.1, ...), custom_call_target="tpu_custom_call" | custom-call | tf_op jit(solution)/shard_map/pack_z/pallas_call | solution.py:584
  1.0 4.6 %collective-permute-start.1 = (f32[216,128]{1,0:T(8,128)S(1)}, f32[216,128]{1,0:T(8,128)S(1)}, u32[]{:S(2)}, u32[]{:S(2)}) collective-permute-start(f32[216,128]{1,0:T(8,128)S(1)} %get-tuple-element.29), channel_id=1, source_target_pairs={{1,4},{5,8},{9,12},{13,0},{4,1},{8,5},{12,9},{0,13},{3,6},{7,10},{... | collective-permute-start | bytes 331784 | tf_op jit(solution)/shard_map/ppermute | solution.py:575
  5.6 0.0 collective-permute-start
  5.6 1.6 %collective-permute-start.3 = (f32[240,128]{1,0:T(8,128)S(1)}, f32[240,128]{1,0:T(8,128)S(1)}, u32[]{:S(2)}, u32[]{:S(2)}) collective-permute-start(f32[240,128]{1,0:T(8,128)S(1)} %pack_t.1), channel_id=1, source_target_pairs={{2,0},{0,2},{3,1},{1,3},{6,4},{4,6},{7,5},{5,7},{10,8},{8,10},{11,... | collective-permute-start | bytes 368648 | tf_op jit(solution)/shard_map/ppermute | solution.py:571
  7.1 0.9 %collective-permute-start.2 = (f32[112,128]{1,0:T(8,128)S(1)}, f32[112,128]{1,0:T(8,128)S(1)}, u32[]{:S(2)}, u32[]{:S(2)}) collective-permute-start(f32[112,128]{1,0:T(8,128)S(1)} %get-tuple-element.32), channel_id=1, source_target_pairs={{4,0},{5,1},{8,4},{9,5},{12,8},{13,9},{0,12},{1,13},{6,2},{7,3},{1... | collective-permute-start | bytes 172040 | tf_op jit(solution)/shard_map/ppermute | solution.py:570
  8.0 0.5 %fields_own.1 = (f32[816,128]{1,0:T(8,128)S(1)}, f32[768,128]{1,0:T(8,128)S(1)}) custom-call(bf16[1152,128]{1,0:T(8,128)(2,1)S(1)} %get-tuple-element.23.perm_ref, f32[96,128]{1,0:T(8,128)S(1)} %get-tuple-element.24.x_ref, f32[288,128]{1,0:T(8,128)S(1)} %get-tuple-element.25.u_ref), custom_call_target="tpu_custom_call" | custom-call | tf_op jit(solution)/shard_map/fields_own/pallas_call | solution.py:628
  8.5 0.4 %force_own.1._.own_part = f32[144,128]{1,0:T(8,128)S(1)} custom-call(f32[96,128]{1,0:T(8,128)S(1)} %get-tuple-element.22.scale_ref, f32[96,128]{1,0:T(8,128)S(1)} %get-tuple-element.24.x_ref, f32[288,128]{1,0:T(8,128)S(1)} %get-tuple-element.25.u_ref, f32[816,128]{1,0:T(8,128)S(1)} %get-tuple-element.26.shared_ref.own_shared.rest_0_, ...), custom_call_target="tpu_custom_call" | custom-call | flops 1000000 | bytes 7380000 | tf_op jit(solution)/shard_map/force_own/pallas_call | solution.py:636
  8.9 0.0 collective-permute-done.within_ref
  8.9 0.0 collective-permute-done.1.between_ref
  9.0 2.0 %collective-permute-start.4 = (f32[112,128]{1,0:T(8,128)S(1)}, f32[112,128]{1,0:T(8,128)S(1)}, u32[]{:S(2)}, u32[]{:S(2)}) collective-permute-start(f32[112,128]{1,0:T(8,128)S(1)} %get-tuple-element.38), channel_id=1, source_target_pairs={{2,0},{0,2},{3,1},{1,3},{6,4},{4,6},{7,5},{5,7},{10,8},{8,10},{11,... | collective-permute-start | bytes 172040 | tf_op jit(solution)/shard_map/ppermute | solution.py:571
  11.0 0.3 %collective-permute-done.2.rest_2_ = f32[112,128]{1,0:T(8,128)S(1)} collective-permute-done((f32[112,128]{1,0:T(8,128)S(1)}, f32[112,128]{1,0:T(8,128)S(1)}, u32[]{:S(2)}, u32[]{:S(2)}) %collective-permute-start.2) | collective-permute-done | bytes 57376 | tf_op jit(solution)/shard_map/ppermute | solution.py:570
  11.3 0.7 %force_z.1 = (f32[336,128]{1,0:T(8,128)S(1)}, f32[216,128]{1,0:T(8,128)S(1)}) custom-call(f32[96,128]{1,0:T(8,128)S(1)} %get-tuple-element.22.scale_ref, bf16[1152,128]{1,0:T(8,128)(2,1)S(1)} %get-tuple-element.23.perm_ref, f32[96,128]{1,0:T(8,128)S(1)} %get-tuple-element.24.x_ref, f32[288,128]{1,0:T(8,128)S(1)} %get-tuple-element.25.u_ref, ...), custom_call_target="tpu_custom_call" | custom-call | flops 1000000 | bytes 7380000 | tf_op jit(solution)/shard_map/force_z/pallas_call | solution.py:658
  12.1 0.0 collective-permute-done.3.rest_0_.rest_6_
  12.1 1.3 %force_t.1 = (f32[336,128]{1,0:T(8,128)S(1)}, f32[72,128]{1,0:T(8,128)S(1)}, f32[288,128]{1,0:T(8,128)}) custom-call(f32[96,128]{1,0:T(8,128)S(1)} %get-tuple-element.22.scale_ref, bf16[1152,128]{1,0:T(8,128)(2,1)S(1)} %get-tuple-element.23.perm_ref, f32[96,128]{1,0:T(8,128)S(1)} %get-tuple-element.24.x_ref, f32[288,128]{1,0:T(8,128)S(1)} %get-tuple-element.25.u_ref, ...), custom_call_target="tpu_custom_call" | custom-call | flops 1000000 | bytes 7380000 | tf_op jit(solution)/shard_map/force_t/pallas_call | solution.py:668
  13.4 0.0 collective-permute-done.4.rest_9_
  13.4 1.0 %force_corner.1 = f32[288,128]{1,0:T(8,128)} custom-call(f32[96,128]{1,0:T(8,128)S(1)} %get-tuple-element.22.scale_ref, bf16[1152,128]{1,0:T(8,128)(2,1)S(1)} %get-tuple-element.23.perm_ref, f32[96,128]{1,0:T(8,128)S(1)} %get-tuple-element.24.x_ref, f32[288,128]{1,0:T(8,128)S(1)} %get-tuple-element.25.u_ref, ...), custom_call_target="tpu_custom_call", output_to_operand_aliasing={{}: (9, {})} | custom-call | flops 1000000 | bytes 3690000 | tf_op jit(solution)/shard_map/force_corner/pallas_call | solution.py:679
  (2 shorter events, 0.1 us)
Async XLA Ops:
  1.0 7.9 %collective-permute-start.1 = (f32[216,128]{1,0:T(8,128)S(1)}, f32[216,128]{1,0:T(8,128)S(1)}, u32[]{:S(2)}, u32[]{:S(2)}) collective-permute-start(f32[216,128]{1,0:T(8,128)S(1)} %get-tuple-element.29), channel_id=1, source_target_pairs={{1,4},{5,8},{9,12},{13,0},{4,1},{8,5},{12,9},{0,13},{3,6},{7,10},{... | collective-permute-start | bytes 331784 | tf_op jit(solution)/shard_map/ppermute | solution.py:575
  5.6 3.3 %collective-permute-start = (f32[208,128]{1,0:T(8,128)S(1)}, f32[208,128]{1,0:T(8,128)S(1)}, u32[]{:S(2)}, u32[]{:S(2)}) collective-permute-start(f32[208,128]{1,0:T(8,128)S(1)} %get-tuple-element.28), channel_id=1, source_target_pairs={{0,1},{4,5},{8,9},{12,13},{1,0},{5,4},{9,8},{13,12},{2,3},{6,7},{1... | collective-permute-start | bytes 319496 | tf_op jit(solution)/shard_map/ppermute | solution.py:575
  5.6 6.5 %collective-permute-start.3 = (f32[240,128]{1,0:T(8,128)S(1)}, f32[240,128]{1,0:T(8,128)S(1)}, u32[]{:S(2)}, u32[]{:S(2)}) collective-permute-start(f32[240,128]{1,0:T(8,128)S(1)} %pack_t.1), channel_id=1, source_target_pairs={{2,0},{0,2},{3,1},{1,3},{6,4},{4,6},{7,5},{5,7},{10,8},{8,10},{11,... | collective-permute-start | bytes 368648 | tf_op jit(solution)/shard_map/ppermute | solution.py:571
  7.1 4.2 %collective-permute-start.2 = (f32[112,128]{1,0:T(8,128)S(1)}, f32[112,128]{1,0:T(8,128)S(1)}, u32[]{:S(2)}, u32[]{:S(2)}) collective-permute-start(f32[112,128]{1,0:T(8,128)S(1)} %get-tuple-element.32), channel_id=1, source_target_pairs={{4,0},{5,1},{8,4},{9,5},{12,8},{13,9},{0,12},{1,13},{6,2},{7,3},{1... | collective-permute-start | bytes 172040 | tf_op jit(solution)/shard_map/ppermute | solution.py:570
  9.0 4.4 %collective-permute-start.4 = (f32[112,128]{1,0:T(8,128)S(1)}, f32[112,128]{1,0:T(8,128)S(1)}, u32[]{:S(2)}, u32[]{:S(2)}) collective-permute-start(f32[112,128]{1,0:T(8,128)S(1)} %get-tuple-element.38), channel_id=1, source_target_pairs={{2,0},{0,2},{3,1},{1,3},{6,4},{4,6},{7,5},{5,7},{10,8},{8,10},{11,... | collective-permute-start | bytes 172040 | tf_op jit(solution)/shard_map/ppermute | solution.py:571

commit v10 on v9

--- a/solution.py
+++ b/solution.py
@@ -25,7 +25,7 @@
     "corner": ((0, ((2, 3), (3, 2))),),
 }
 COSTS = {"own": 2.0, "z": 2.0, "t": 2.0, "corner": 1.0}
-DIRECT = {"own": (0, 1), "z": (2,), "t": (3,), "corner": ()}
+DIRECT = {"own": (0, 1), "z": (), "t": (3,), "corner": (2,)}
 
 
 def plus(left, right, scale=1):
@@ -174,7 +174,7 @@
 
 def stage_of(key):
     dz, dt = key[2][2:]
-    if dz != 0 and dt != 0:
+    if abs(dz) == 3 or (dz != 0 and dt != 0):
         return "corner"
     return "t" if dt != 0 else "z" if dz != 0 else "own"
 
@@ -490,20 +490,19 @@
     fields = stage_setup(
         "z", plan, t_size, names, received, perm_ref, x_ref, u_ref, [own_shared], shared_ref, alone_ref
     )
-    near, both, weight = scale_tiles(scale_ref)
+    near, _, weight = scale_tiles(scale_ref)
     add_terms(fields, "z", near, acc)
-    direct = own_force(fields, 2, both)
     for k in range(9):
         staples = fields.compact_halves(acc_tile(acc, 0, 2 * k), acc_tile(acc, 0, 2 * k + 1))
         for m in range(2):
             part_ref[pl.ds((9 * m + k) * 8, 8), :] = part_reg(own_part, m, k) + weight[m] * staples[m]
         staple = fields.compact_sum(acc_tile(acc, 1, 2 * k), acc_tile(acc, 1, 2 * k + 1))
-        part_ref[pl.ds((18 + k) * 8, 8), :] = direct[k] + weight[2] * staple
+        part_ref[pl.ds((18 + k) * 8, 8), :] = weight[2] * staple
 
 
 def t_kernel(plan, t_size, names, scale_ref, perm_ref, x_ref, u_ref, own_shared, z_shared, z_part, *rest):
     received = rest[: len(names)]
-    shared_ref, part_ref, out_ref, alone_ref, acc, ready, sem = rest[len(names) :]
+    shared_ref, part_ref, ready, alone_ref, acc = rest[len(names) :]
     fields = stage_setup(
         "t", plan, t_size, names, received, perm_ref, x_ref, u_ref, [own_shared, z_shared], shared_ref, alone_ref
     )
@@ -513,19 +512,19 @@
         staples = fields.compact_halves(acc_tile(acc, 0, 2 * k), acc_tile(acc, 0, 2 * k + 1))
         for m in range(2):
             ready[pl.ds((9 * m + k) * 8, 8), :] = part_reg(z_part, m, k) + weight[m] * staples[m]
-    leaving = pltpu.make_async_copy(ready, out_ref.at[pl.ds(0, ready.shape[0])], sem)
-    leaving.start()
     direct = own_force(fields, 3, both)
     for k in range(9):
         staple = fields.compact_sum(acc_tile(acc, 1, 2 * k), acc_tile(acc, 1, 2 * k + 1))
         part_ref[pl.ds(k * 8, 8), :] = direct[k] + weight[3] * staple
-    leaving.wait()
 
 
 def last_kernel(plan, t_size, names, scale_ref, perm_ref, x_ref, u_ref, *rest):
-    own_shared, z_shared, t_shared, z_part, t_part, _ = rest[:6]
+    own_shared, z_shared, t_shared, z_part, t_part, earlier = rest[:6]
     received = rest[6 : 6 + len(names)]
-    out_ref, alone_ref, acc, ready, sem = rest[6 + len(names) :]
+    out_ref, alone_ref, acc, ready, sems = rest[6 + len(names) :]
+    rows = ready.shape[0]
+    first = pltpu.make_async_copy(earlier, out_ref.at[pl.ds(0, rows)], sems.at[0])
+    first.start()
     fields = stage_setup(
         "corner",
         plan,
@@ -539,16 +538,17 @@
         None,
         alone_ref,
     )
-    near, _, weight = scale_tiles(scale_ref)
+    near, both, weight = scale_tiles(scale_ref)
     add_terms(fields, "corner", near, acc)
+    direct = own_force(fields, 2, both)
     for k in range(9):
         staples = fields.compact_halves(acc_tile(acc, 0, 2 * k), acc_tile(acc, 0, 2 * k + 1))
-        ready[pl.ds(k * 8, 8), :] = part_reg(z_part, 2, k) + weight[2] * staples[0]
+        ready[pl.ds(k * 8, 8), :] = part_reg(z_part, 2, k) + direct[k] + weight[2] * staples[0]
         ready[pl.ds((9 + k) * 8, 8), :] = part_reg(t_part, 0, k) + weight[3] * staples[1]
-    rows = ready.shape[0]
-    leaving = pltpu.make_async_copy(ready, out_ref.at[pl.ds(rows, rows)], sem)
-    leaving.start()
-    leaving.wait()
+    second = pltpu.make_async_copy(ready, out_ref.at[pl.ds(rows, rows)], sems.at[1])
+    second.start()
+    first.wait()
+    second.wait()
 
 
 def rows_of(count):
@@ -654,7 +654,7 @@
         name="pack_corners",
     )(within, between, own_part)
     received.update({name: moved(name, value) for name, value in zip(corner_names, corners)})
-    names = [("z", 1), ("z", -1), ("z", 2)]
+    names = [("z", 1), ("z", -1)]
     z_shared, z_part = pl.pallas_call(
         functools.partial(z_kernel, plan, t_size, names),
         out_shape=[rows_of(shared["z"][1]), rows_of(3 * part_rows)],
@@ -665,25 +665,24 @@
         compiler_params=wide_limit,
         name="force_z",
     )(*local, own_shared, own_part, *[received[name] for name in names])
-    t_shared, t_part, force = pl.pallas_call(
+    t_shared, t_part, earlier = pl.pallas_call(
         functools.partial(t_kernel, plan, t_size, t_names),
-        out_shape=[rows_of(shared["t"][1]), rows_of(part_rows), rows_of(u_rows)],
+        out_shape=[rows_of(shared["t"][1]), rows_of(part_rows), rows_of(2 * part_rows)],
         in_specs=[vmem] * (7 + len(t_names)),
-        out_specs=[vmem] * 2 + [hbm],
-        scratch_shapes=scratch("t") + [pltpu.VMEM((2 * part_rows, LANES), F32), pltpu.SemaphoreType.DMA],
+        out_specs=[vmem] * 3,
+        scratch_shapes=scratch("t"),
         cost_estimate=cost(COSTS["t"]),
         compiler_params=wide_limit,
         name="force_t",
     )(*local, own_shared, z_shared, z_part, *[received[name] for name in t_names])
-    names = [name for name in received if name != ("z", 2)]
+    names = list(received)
     force = pl.pallas_call(
         functools.partial(last_kernel, plan, t_size, names),
         out_shape=rows_of(u_rows),
-        in_specs=[vmem] * 9 + [hbm] + [vmem] * len(names),
+        in_specs=[vmem] * (10 + len(names)),
         out_specs=hbm,
-        input_output_aliases={9: 0},
         scratch_shapes=scratch("corner")
-        + [pltpu.VMEM((2 * part_rows, LANES), F32), pltpu.SemaphoreType.DMA],
+        + [pltpu.VMEM((2 * part_rows, LANES), F32), pltpu.SemaphoreType.DMA((2,))],
         cost_estimate=cost(COSTS["corner"]),
         compiler_params=wide_limit,
         name="force_corner",
@@ -694,7 +693,7 @@
         t_shared,
         z_part,
         t_part,
-        force,
+        earlier,
         *[received[name] for name in names],
     )
     return force.reshape(gauge_links.shape)

time: 14.5 us -> 14.4 us (level)
  Pallas kernels: 4.93 us -> 4.37 us
  waiting for transfers between devices: 0.33 us -> 0.73 us
    ppermute x2, waiting for transfers between devices: 0.01 us -> 0.73 us  [moved(): lax.ppermute(value, 'ta', [((j + step) % t_size, j) for j in range(t_size)])]
    pallas_call x1, Pallas kernels: 1.32 us -> 0.76 us  [on_device(): pl.pallas_call(functools.partial(t_kernel, plan, t_size, t_names), out_sh...]
    ppermute x1, waiting for transfers between devices: 0.32 us -> 0.01 us  [moved(): lax.ppermute(value, ('gz', 'gy'), [((i + step) % z_size, i) for i in rang...]
  transfers between devices with their start and end apart: 5 -> 5, of which waited for: 1 -> 1; matrix products, arithmetic and copies ran while one was open for 0% -> 0% of each run, Pallas kernels for 21% -> 17%
where the time goes in v10:
time: 14.4 us; the launch traced here: 14.2 us
  starting transfers between devices  9.04 us (63%)
  Pallas kernels  4.37 us (30%)
  waiting for transfers between devices  0.73 us (5%)
    ppermute x2, starting transfers between devices, exchanged(): return lax.ppermute(value, ('gz', 'gy'), pairs + [(j, i) for i, j in pairs])  4.56 us
    ppermute x2, starting transfers between devices, moved(): lax.ppermute(value, 'ta', [((j + step) % t_size, j) for j in range(t_size)])  3.59 us
    pallas_call x1, Pallas kernels, on_device(): pl.pallas_call(functools.partial(last_kernel, plan, t_size, names), out_s...  1.02 us
    pallas_call x1, Pallas kernels, on_device(): pl.pallas_call(functools.partial(pack_z_kernel, plan), out_shape=[rows_of...  1 us
    ppermute x1, starting transfers between devices, moved(): lax.ppermute(value, ('gz', 'gy'), [((i + step) % z_size, i) for i in rang...  0.89 us
    pallas_call x1, Pallas kernels, on_device(): pl.pallas_call(functools.partial(t_kernel, plan, t_size, t_names), out_sh...  0.76 us
    ppermute x2, waiting for transfers between devices, moved(): lax.ppermute(value, 'ta', [((j + step) % t_size, j) for j in range(t_size)])  0.73 us
    pallas_call x1, Pallas kernels, on_device(): pl.pallas_call(functools.partial(z_kernel, plan, t_size, names), out_shap...  0.69 us
  transfers between devices with their start and end apart: 5, of which 1 were waited for; matrix products, arithmetic and copies ran while one was open for 0% of the time, Pallas kernels for 17%

profile of v10, /device:TPU:0, one launch (start us, length us, event | category | flops | bytes accessed | tf_op | source)
XLA Modules:
  0.0 14.2 jit_solution(2636873665962462941)
XLA Ops:
  0.0 1.0 %pack_z.1 = (f32[208,128]{1,0:T(8,128)S(1)}, f32[216,128]{1,0:T(8,128)S(1)}, f32[112,128]{1,0:T(8,128)S(1)}, f32[96,128]{1,0:T(8,128)S(1)}, bf16[1152,128]{1,0:T...) custom-call(f32[4]{0:T(128)} %near_in.1, f32[4]{0:T(128)} %far_in.1, f32[4]{0:T(128)} %weight_in.1, ...), custom_call_target="tpu_custom_call" | custom-call | tf_op jit(solution)/shard_map/pack_z/pallas_call | solution.py:584
  1.0 4.6 %collective-permute-start.1 = (f32[216,128]{1,0:T(8,128)S(1)}, f32[216,128]{1,0:T(8,128)S(1)}, u32[]{:S(2)}, u32[]{:S(2)}) collective-permute-start(f32[216,128]{1,0:T(8,128)S(1)} %get-tuple-element.29), channel_id=1, source_target_pairs={{1,4},{5,8},{9,12},{13,0},{4,1},{8,5},{12,9},{0,13},{3,6},{7,10},{... | collective-permute-start | bytes 331784 | tf_op jit(solution)/shard_map/ppermute | solution.py:575
  5.6 0.0 collective-permute-start
  5.6 1.6 %collective-permute-start.2 = (f32[240,128]{1,0:T(8,128)S(1)}, f32[240,128]{1,0:T(8,128)S(1)}, u32[]{:S(2)}, u32[]{:S(2)}) collective-permute-start(f32[240,128]{1,0:T(8,128)S(1)} %pack_t.1), channel_id=1, source_target_pairs={{2,0},{0,2},{3,1},{1,3},{6,4},{4,6},{7,5},{5,7},{10,8},{8,10},{11,... | collective-permute-start | bytes 368648 | tf_op jit(solution)/shard_map/ppermute | solution.py:571
  7.1 0.9 %collective-permute-start.3 = (f32[112,128]{1,0:T(8,128)S(1)}, f32[112,128]{1,0:T(8,128)S(1)}, u32[]{:S(2)}, u32[]{:S(2)}) collective-permute-start(f32[112,128]{1,0:T(8,128)S(1)} %get-tuple-element.37), channel_id=1, source_target_pairs={{4,0},{5,1},{8,4},{9,5},{12,8},{13,9},{0,12},{1,13},{6,2},{7,3},{1... | collective-permute-start | bytes 172040 | tf_op jit(solution)/shard_map/ppermute | solution.py:570
  8.0 0.5 %fields_own.1 = (f32[816,128]{1,0:T(8,128)S(1)}, f32[768,128]{1,0:T(8,128)S(1)}) custom-call(bf16[1152,128]{1,0:T(8,128)(2,1)S(1)} %get-tuple-element.23.perm_ref, f32[96,128]{1,0:T(8,128)S(1)} %get-tuple-element.24.x_ref, f32[288,128]{1,0:T(8,128)S(1)} %get-tuple-element.25.u_ref), custom_call_target="tpu_custom_call" | custom-call | tf_op jit(solution)/shard_map/fields_own/pallas_call | solution.py:628
  8.5 0.4 %force_own.1._.own_part = f32[144,128]{1,0:T(8,128)S(1)} custom-call(f32[96,128]{1,0:T(8,128)S(1)} %get-tuple-element.22.scale_ref, f32[96,128]{1,0:T(8,128)S(1)} %get-tuple-element.24.x_ref, f32[288,128]{1,0:T(8,128)S(1)} %get-tuple-element.25.u_ref, f32[816,128]{1,0:T(8,128)S(1)} %get-tuple-element.26.shared_ref.own_shared.rest_0_, ...), custom_call_target="tpu_custom_call" | custom-call | flops 1000000 | bytes 7380000 | tf_op jit(solution)/shard_map/force_own/pallas_call | solution.py:636
  8.9 0.0 collective-permute-done.within_ref
  8.9 0.0 collective-permute-done.1.between_ref
  9.0 2.0 %collective-permute-start.4 = (f32[112,128]{1,0:T(8,128)S(1)}, f32[112,128]{1,0:T(8,128)S(1)}, u32[]{:S(2)}, u32[]{:S(2)}) collective-permute-start(f32[112,128]{1,0:T(8,128)S(1)} %get-tuple-element.38), channel_id=1, source_target_pairs={{2,0},{0,2},{3,1},{1,3},{6,4},{4,6},{7,5},{5,7},{10,8},{8,10},{11,... | collective-permute-start | bytes 172040 | tf_op jit(solution)/shard_map/ppermute | solution.py:571
  11.0 0.7 %force_z.1 = (f32[336,128]{1,0:T(8,128)S(1)}, f32[216,128]{1,0:T(8,128)S(1)}) custom-call(f32[96,128]{1,0:T(8,128)S(1)} %get-tuple-element.22.scale_ref, bf16[1152,128]{1,0:T(8,128)(2,1)S(1)} %get-tuple-element.23.perm_ref, f32[96,128]{1,0:T(8,128)S(1)} %get-tuple-element.24.x_ref, f32[288,128]{1,0:T(8,128)S(1)} %get-tuple-element.25.u_ref, ...), custom_call_target="tpu_custom_call" | custom-call | flops 1000000 | bytes 7380000 | tf_op jit(solution)/shard_map/force_z/pallas_call | solution.py:658
  11.7 0.0 collective-permute-done.2.rest_0_.rest_7_
  11.7 0.8 %force_t.1 = (f32[336,128]{1,0:T(8,128)S(1)}, f32[72,128]{1,0:T(8,128)S(1)}, f32[144,128]{1,0:T(8,128)S(1)}) custom-call(f32[96,128]{1,0:T(8,128)S(1)} %get-tuple-element.22.scale_ref, bf16[1152,128]{1,0:T(8,128)(2,1)S(1)} %get-tuple-element.23.perm_ref, f32[96,128]{1,0:T(8,128)S(1)} %get-tuple-element.24.x_ref, f32[288,128]{1,0:T(8,128)S(1)} %get-tuple-element.25.u_ref, ...), custom_call_target="tpu_custom_call" | custom-call | flops 1000000 | bytes 7380000 | tf_op jit(solution)/shard_map/force_t/pallas_call | solution.py:668
  12.5 0.0 collective-permute-done.3.rest_6_
  12.5 0.7 %collective-permute-done.4.rest_10_ = f32[112,128]{1,0:T(8,128)S(1)} collective-permute-done((f32[112,128]{1,0:T(8,128)S(1)}, f32[112,128]{1,0:T(8,128)S(1)}, u32[]{:S(2)}, u32[]{:S(2)}) %collective-permute-start.4) | collective-permute-done | bytes 57376 | tf_op jit(solution)/shard_map/ppermute | solution.py:571
  13.2 1.0 %force_corner.1 = f32[288,128]{1,0:T(8,128)} custom-call(f32[96,128]{1,0:T(8,128)S(1)} %get-tuple-element.22.scale_ref, bf16[1152,128]{1,0:T(8,128)(2,1)S(1)} %get-tuple-element.23.perm_ref, f32[96,128]{1,0:T(8,128)S(1)} %get-tuple-element.24.x_ref, f32[288,128]{1,0:T(8,128)S(1)} %get-tuple-element.25.u_ref, ...), custom_call_target="tpu_custom_call" | custom-call | flops 1000000 | bytes 3690000 | tf_op jit(solution)/shard_map/force_corner/pallas_call | solution.py:679
  (2 shorter events, 0.1 us)
Async XLA Ops:
  1.0 7.9 %collective-permute-start.1 = (f32[216,128]{1,0:T(8,128)S(1)}, f32[216,128]{1,0:T(8,128)S(1)}, u32[]{:S(2)}, u32[]{:S(2)}) collective-permute-start(f32[216,128]{1,0:T(8,128)S(1)} %get-tuple-element.29), channel_id=1, source_target_pairs={{1,4},{5,8},{9,12},{13,0},{4,1},{8,5},{12,9},{0,13},{3,6},{7,10},{... | collective-permute-start | bytes 331784 | tf_op jit(solution)/shard_map/ppermute | solution.py:575
  5.6 3.3 %collective-permute-start = (f32[208,128]{1,0:T(8,128)S(1)}, f32[208,128]{1,0:T(8,128)S(1)}, u32[]{:S(2)}, u32[]{:S(2)}) collective-permute-start(f32[208,128]{1,0:T(8,128)S(1)} %get-tuple-element.28), channel_id=1, source_target_pairs={{0,1},{4,5},{8,9},{12,13},{1,0},{5,4},{9,8},{13,12},{2,3},{6,7},{1... | collective-permute-start | bytes 319496 | tf_op jit(solution)/shard_map/ppermute | solution.py:575
  5.6 6.1 %collective-permute-start.2 = (f32[240,128]{1,0:T(8,128)S(1)}, f32[240,128]{1,0:T(8,128)S(1)}, u32[]{:S(2)}, u32[]{:S(2)}) collective-permute-start(f32[240,128]{1,0:T(8,128)S(1)} %pack_t.1), channel_id=1, source_target_pairs={{2,0},{0,2},{3,1},{1,3},{6,4},{4,6},{7,5},{5,7},{10,8},{8,10},{11,... | collective-permute-start | bytes 368648 | tf_op jit(solution)/shard_map/ppermute | solution.py:571
  7.1 5.3 %collective-permute-start.3 = (f32[112,128]{1,0:T(8,128)S(1)}, f32[112,128]{1,0:T(8,128)S(1)}, u32[]{:S(2)}, u32[]{:S(2)}) collective-permute-start(f32[112,128]{1,0:T(8,128)S(1)} %get-tuple-element.37), channel_id=1, source_target_pairs={{4,0},{5,1},{8,4},{9,5},{12,8},{13,9},{0,12},{1,13},{6,2},{7,3},{1... | collective-permute-start | bytes 172040 | tf_op jit(solution)/shard_map/ppermute | solution.py:570
  9.0 4.2 %collective-permute-start.4 = (f32[112,128]{1,0:T(8,128)S(1)}, f32[112,128]{1,0:T(8,128)S(1)}, u32[]{:S(2)}, u32[]{:S(2)}) collective-permute-start(f32[112,128]{1,0:T(8,128)S(1)} %get-tuple-element.38), channel_id=1, source_target_pairs={{2,0},{0,2},{3,1},{1,3},{6,4},{4,6},{7,5},{5,7},{10,8},{8,10},{11,... | collective-permute-start | bytes 172040 | tf_op jit(solution)/shard_map/ppermute | solution.py:571

commit v11 on v10

--- a/solution.py
+++ b/solution.py
@@ -578,7 +578,7 @@
     corner_names = [name for name in plan if name[0] == "c"]
     t_names = [name for name in first_names if name[0] == "t"]
     in_hbm = functools.partial(pltpu.with_memory_space_constraint, memory_space=pltpu.HBM)
-    beyond_rows = 8 * max([plan["z", 2].count] + [plan[name].count for name in corner_names])
+    beyond_rows = 8 * plan["z", 2].count
     ahead_rows, behind_rows = [8 * plan["z", step].count for step in (1, -1)]
     shared_rows = max(ahead_rows, behind_rows)
     within, between, beyond, scale, perm, *own = pl.pallas_call(

time: 14.4 us -> 16 us (1.11)
  waiting for transfers between devices: 0.73 us -> 1.82 us
  starting transfers between devices: 9.04 us -> 9.62 us
    ppermute x1, waiting for transfers between devices: 0.01 us -> 1.47 us  [moved(): lax.ppermute(value, ('gz', 'gy'), [((i + step) % z_size, i) for i in rang...]
    ppermute x2, waiting for transfers between devices: 0.73 us -> 0.01 us  [moved(): lax.ppermute(value, 'ta', [((j + step) % t_size, j) for j in range(t_size)])]
    ppermute x2, starting transfers between devices: 3.59 us -> 4.17 us  [moved(): lax.ppermute(value, 'ta', [((j + step) % t_size, j) for j in range(t_size)])]
    ppermute x2, waiting for transfers between devices: 0.01 us -> 0.35 us  [exchanged(): return lax.ppermute(value, ('gz', 'gy'), pairs + [(j, i) for i, j in pairs])]
  transfers between devices with their start and end apart: 5 -> 5, of which waited for: 1 -> 2; matrix products, arithmetic and copies ran while one was open for 0% -> 0% of each run, Pallas kernels for 17% -> 15%
where the time goes in v11:
time: 16 us; the launch traced here: 15.8 us
  starting transfers between devices  9.62 us (60%)
  Pallas kernels  4.35 us (27%)
  waiting for transfers between devices  1.82 us (11%)
    ppermute x2, starting transfers between devices, exchanged(): return lax.ppermute(value, ('gz', 'gy'), pairs + [(j, i) for i, j in pairs])  4.56 us
    ppermute x2, starting transfers between devices, moved(): lax.ppermute(value, 'ta', [((j + step) % t_size, j) for j in range(t_size)])  4.17 us
    ppermute x1, waiting for transfers between devices, moved(): lax.ppermute(value, ('gz', 'gy'), [((i + step) % z_size, i) for i in rang...  1.47 us
    pallas_call x1, Pallas kernels, on_device(): pl.pallas_call(functools.partial(last_kernel, plan, t_size, names), out_s...  1.02 us
    pallas_call x1, Pallas kernels, on_device(): pl.pallas_call(functools.partial(pack_z_kernel, plan), out_shape=[rows_of...  1 us
    ppermute x1, starting transfers between devices, moved(): lax.ppermute(value, ('gz', 'gy'), [((i + step) % z_size, i) for i in rang...  0.89 us
    pallas_call x1, Pallas kernels, on_device(): pl.pallas_call(functools.partial(t_kernel, plan, t_size, t_names), out_sh...  0.76 us
    pallas_call x1, Pallas kernels, on_device(): pl.pallas_call(functools.partial(z_kernel, plan, t_size, names), out_shap...  0.69 us
  transfers between devices with their start and end apart: 5, of which 2 were waited for; matrix products, arithmetic and copies ran while one was open for 0% of the time, Pallas kernels for 15%

profile of v11, /device:TPU:0, one launch (start us, length us, event | category | flops | bytes accessed | tf_op | source)
XLA Modules:
  0.0 15.8 jit_solution(534436102150790644)
XLA Ops:
  0.0 1.0 %pack_z.1 = (f32[208,128]{1,0:T(8,128)S(1)}, f32[216,128]{1,0:T(8,128)S(1)}, f32[48,128]{1,0:T(8,128)S(1)}, f32[96,128]{1,0:T(8,128)S(1)}, bf16[1152,128]{1,0:T(...) custom-call(f32[4]{0:T(128)} %near_in.1, f32[4]{0:T(128)} %far_in.1, f32[4]{0:T(128)} %weight_in.1, ...), custom_call_target="tpu_custom_call" | custom-call | tf_op jit(solution)/shard_map/pack_z/pallas_call | solution.py:584
  1.0 4.6 %collective-permute-start.1 = (f32[216,128]{1,0:T(8,128)S(1)}, f32[216,128]{1,0:T(8,128)S(1)}, u32[]{:S(2)}, u32[]{:S(2)}) collective-permute-start(f32[216,128]{1,0:T(8,128)S(1)} %get-tuple-element.29), channel_id=1, source_target_pairs={{1,4},{5,8},{9,12},{13,0},{4,1},{8,5},{12,9},{0,13},{3,6},{7,10},{... | collective-permute-start | bytes 331784 | tf_op jit(solution)/shard_map/ppermute | solution.py:575
  5.6 0.0 collective-permute-start
  5.6 1.6 %collective-permute-start.2 = (f32[240,128]{1,0:T(8,128)S(1)}, f32[240,128]{1,0:T(8,128)S(1)}, u32[]{:S(2)}, u32[]{:S(2)}) collective-permute-start(f32[240,128]{1,0:T(8,128)S(1)} %pack_t.1), channel_id=1, source_target_pairs={{2,0},{0,2},{3,1},{1,3},{6,4},{4,6},{7,5},{5,7},{10,8},{8,10},{11,... | collective-permute-start | bytes 368648 | tf_op jit(solution)/shard_map/ppermute | solution.py:571
  7.1 0.5 %fields_own.1 = (f32[816,128]{1,0:T(8,128)S(1)}, f32[768,128]{1,0:T(8,128)S(1)}) custom-call(bf16[1152,128]{1,0:T(8,128)(2,1)S(1)} %get-tuple-element.23.perm_ref, f32[96,128]{1,0:T(8,128)S(1)} %get-tuple-element.24.x_ref, f32[288,128]{1,0:T(8,128)S(1)} %get-tuple-element.25.u_ref), custom_call_target="tpu_custom_call" | custom-call | tf_op jit(solution)/shard_map/fields_own/pallas_call | solution.py:628
  7.6 0.4 %force_own.1._.own_part = f32[144,128]{1,0:T(8,128)S(1)} custom-call(f32[96,128]{1,0:T(8,128)S(1)} %get-tuple-element.22.scale_ref, f32[96,128]{1,0:T(8,128)S(1)} %get-tuple-element.24.x_ref, f32[288,128]{1,0:T(8,128)S(1)} %get-tuple-element.25.u_ref, f32[816,128]{1,0:T(8,128)S(1)} %get-tuple-element.26.shared_ref.own_shared.rest_0_, ...), custom_call_target="tpu_custom_call" | custom-call | flops 1000000 | bytes 7380000 | tf_op jit(solution)/shard_map/force_own/pallas_call | solution.py:636
  8.0 0.0 collective-permute-done.within_ref
  8.0 0.3 %collective-permute-done.1.between_ref = f32[216,128]{1,0:T(8,128)S(1)} collective-permute-done((f32[216,128]{1,0:T(8,128)S(1)}, f32[216,128]{1,0:T(8,128)S(1)}, u32[]{:S(2)}, u32[]{:S(2)}) %collective-permute-start.1) | collective-permute-done | bytes 110624 | tf_op jit(solution)/shard_map/ppermute | solution.py:575
  8.4 2.6 %collective-permute-start.4 = (f32[112,128]{1,0:T(8,128)S(1)}, f32[112,128]{1,0:T(8,128)S(1)}, u32[]{:S(2)}, u32[]{:S(2)}) collective-permute-start(f32[112,128]{1,0:T(8,128)S(1)} %get-tuple-element.38), channel_id=1, source_target_pairs={{2,0},{0,2},{3,1},{1,3},{6,4},{4,6},{7,5},{5,7},{10,8},{8,10},{11,... | collective-permute-start | bytes 172040 | tf_op jit(solution)/shard_map/ppermute | solution.py:571
  11.0 0.9 %collective-permute-start.3 = (f32[48,128]{1,0:T(8,128)S(1)}, f32[48,128]{1,0:T(8,128)S(1)}, u32[]{:S(2)}, u32[]{:S(2)}) collective-permute-start(f32[48,128]{1,0:T(8,128)S(1)} %get-tuple-element.37), channel_id=1, source_target_pairs={{4,0},{5,1},{8,4},{9,5},{12,8},{13,9},{0,12},{1,13},{6,2},{7,3},{1... | collective-permute-start | bytes 73736 | tf_op jit(solution)/shard_map/ppermute | solution.py:570
  11.9 0.7 %force_z.1 = (f32[336,128]{1,0:T(8,128)S(1)}, f32[216,128]{1,0:T(8,128)S(1)}) custom-call(f32[96,128]{1,0:T(8,128)S(1)} %get-tuple-element.22.scale_ref, bf16[1152,128]{1,0:T(8,128)(2,1)S(1)} %get-tuple-element.23.perm_ref, f32[96,128]{1,0:T(8,128)S(1)} %get-tuple-element.24.x_ref, f32[288,128]{1,0:T(8,128)S(1)} %get-tuple-element.25.u_ref, ...), custom_call_target="tpu_custom_call" | custom-call | flops 1000000 | bytes 7380000 | tf_op jit(solution)/shard_map/force_z/pallas_call | solution.py:658
  12.6 0.0 collective-permute-done.2.rest_0_.rest_7_
  12.6 0.8 %force_t.1 = (f32[336,128]{1,0:T(8,128)S(1)}, f32[72,128]{1,0:T(8,128)S(1)}, f32[144,128]{1,0:T(8,128)S(1)}) custom-call(f32[96,128]{1,0:T(8,128)S(1)} %get-tuple-element.22.scale_ref, bf16[1152,128]{1,0:T(8,128)(2,1)S(1)} %get-tuple-element.23.perm_ref, f32[96,128]{1,0:T(8,128)S(1)} %get-tuple-element.24.x_ref, f32[288,128]{1,0:T(8,128)S(1)} %get-tuple-element.25.u_ref, ...), custom_call_target="tpu_custom_call" | custom-call | flops 1000000 | bytes 7380000 | tf_op jit(solution)/shard_map/force_t/pallas_call | solution.py:668
  13.4 1.5 %collective-permute-done.3.rest_6_ = f32[48,128]{1,0:T(8,128)S(1)} collective-permute-done((f32[48,128]{1,0:T(8,128)S(1)}, f32[48,128]{1,0:T(8,128)S(1)}, u32[]{:S(2)}, u32[]{:S(2)}) %collective-permute-start.3) | collective-permute-done | bytes 24608 | tf_op jit(solution)/shard_map/ppermute | solution.py:570
  14.8 0.0 collective-permute-done.4.rest_10_
  14.8 1.0 %force_corner.1 = f32[288,128]{1,0:T(8,128)} custom-call(f32[96,128]{1,0:T(8,128)S(1)} %get-tuple-element.22.scale_ref, bf16[1152,128]{1,0:T(8,128)(2,1)S(1)} %get-tuple-element.23.perm_ref, f32[96,128]{1,0:T(8,128)S(1)} %get-tuple-element.24.x_ref, f32[288,128]{1,0:T(8,128)S(1)} %get-tuple-element.25.u_ref, ...), custom_call_target="tpu_custom_call" | custom-call | flops 1000000 | bytes 3690000 | tf_op jit(solution)/shard_map/force_corner/pallas_call | solution.py:679
  (2 shorter events, 0.0 us)
Async XLA Ops:
  1.0 7.3 %collective-permute-start.1 = (f32[216,128]{1,0:T(8,128)S(1)}, f32[216,128]{1,0:T(8,128)S(1)}, u32[]{:S(2)}, u32[]{:S(2)}) collective-permute-start(f32[216,128]{1,0:T(8,128)S(1)} %get-tuple-element.29), channel_id=1, source_target_pairs={{1,4},{5,8},{9,12},{13,0},{4,1},{8,5},{12,9},{0,13},{3,6},{7,10},{... | collective-permute-start | bytes 331784 | tf_op jit(solution)/shard_map/ppermute | solution.py:575
  5.6 2.4 %collective-permute-start = (f32[208,128]{1,0:T(8,128)S(1)}, f32[208,128]{1,0:T(8,128)S(1)}, u32[]{:S(2)}, u32[]{:S(2)}) collective-permute-start(f32[208,128]{1,0:T(8,128)S(1)} %get-tuple-element.28), channel_id=1, source_target_pairs={{0,1},{4,5},{8,9},{12,13},{1,0},{5,4},{9,8},{13,12},{2,3},{6,7},{1... | collective-permute-start | bytes 319496 | tf_op jit(solution)/shard_map/ppermute | solution.py:575
  5.6 7.0 %collective-permute-start.2 = (f32[240,128]{1,0:T(8,128)S(1)}, f32[240,128]{1,0:T(8,128)S(1)}, u32[]{:S(2)}, u32[]{:S(2)}) collective-permute-start(f32[240,128]{1,0:T(8,128)S(1)} %pack_t.1), channel_id=1, source_target_pairs={{2,0},{0,2},{3,1},{1,3},{6,4},{4,6},{7,5},{5,7},{10,8},{8,10},{11,... | collective-permute-start | bytes 368648 | tf_op jit(solution)/shard_map/ppermute | solution.py:571
  8.4 6.4 %collective-permute-start.4 = (f32[112,128]{1,0:T(8,128)S(1)}, f32[112,128]{1,0:T(8,128)S(1)}, u32[]{:S(2)}, u32[]{:S(2)}) collective-permute-start(f32[112,128]{1,0:T(8,128)S(1)} %get-tuple-element.38), channel_id=1, source_target_pairs={{2,0},{0,2},{3,1},{1,3},{6,4},{4,6},{7,5},{5,7},{10,8},{8,10},{11,... | collective-permute-start | bytes 172040 | tf_op jit(solution)/shard_map/ppermute | solution.py:571
  11.0 3.8 %collective-permute-start.3 = (f32[48,128]{1,0:T(8,128)S(1)}, f32[48,128]{1,0:T(8,128)S(1)}, u32[]{:S(2)}, u32[]{:S(2)}) collective-permute-start(f32[48,128]{1,0:T(8,128)S(1)} %get-tuple-element.37), channel_id=1, source_target_pairs={{4,0},{5,1},{8,4},{9,5},{12,8},{13,9},{0,12},{1,13},{6,2},{7,3},{1... | collective-permute-start | bytes 73736 | tf_op jit(solution)/shard_map/ppermute | solution.py:570

commit v12 on v11

--- a/solution.py
+++ b/solution.py
@@ -20,8 +20,8 @@
 STAGES = ("own", "z", "t", "corner")
 TERMS = {
     "own": ((0, ((0, 1), (1, 0))),),
-    "z": ((0, ((0, 2), (1, 2))), (1, ((2, 0), (2, 1)))),
-    "t": ((0, ((0, 3), (1, 3))), (1, ((3, 0), (3, 1)))),
+    "z": ((0, ((0, 2), (1, 2))),),
+    "t": ((0, ((0, 3), (1, 3))), (1, ((3, 0), (3, 1))), (2, ((2, 0), (2, 1)))),
     "corner": ((0, ((2, 3), (3, 2))),),
 }
 COSTS = {"own": 2.0, "z": 2.0, "t": 2.0, "corner": 1.0}
@@ -73,8 +73,9 @@
 def message_plan(t_size):
     plan = collections.OrderedDict()
     ahead = plan["z", 1] = Message()
-    ahead.add_full("x", 0)
-    ahead.add_halves(regs_of("u", (0, 1, 3), 0), "z")
+    ahead.add_halves(regs_of("x", (0,), 0) + regs_of("u", (3,), 0), "z")
+    late = plan["b", 1] = Message()
+    late.add_halves(regs_of("x", (0,), 1) + regs_of("u", (0, 1), 0), "z")
     behind = plan["z", -1] = Message()
     behind.add_halves(regs_of("x", (0,), 1) + regs_of("u", (2,), 1), "z")
     second = plan["z", 2] = Message()
@@ -121,6 +122,8 @@
             return self.local(kind, n, k, t, z)
         name = ("z", dz) if dt == 0 else ("t", dt) if dz == 0 else ("c", dt)
         item = (dz if name[0] == "c" else 0, kind, n, k, t, z)
+        if name == ("z", 1) and item not in self.plan[name].places:
+            name = ("b", 1)
         return (name,) + self.plan[name].places[item]
 
     def load(self, name, reg):
@@ -174,6 +177,8 @@
 
 def stage_of(key):
     dz, dt = key[2][2:]
+    if key[0] == "u" and key[1] < 2 and dz == 1 and dt == 0:
+        return "t"
     if abs(dz) == 3 or (dz != 0 and dt != 0):
         return "corner"
     return "t" if dt != 0 else "z" if dz != 0 else "own"
@@ -382,13 +387,9 @@
             out[pl.ds(8 * reg, 8), :] = locator.assemble(spots)
 
 
-def odd_in_z():
-    return (lax.axis_index("gz") * lax.axis_size("gy") + lax.axis_index("gy")) % 2 == 1
-
-
-def pack_z_kernel(plan, near_in, far_in, weight_in, x_in, u_in, *rest):
-    within_ref, between_ref, second_ref, scale_ref, perm_ref, x_ref, u_ref = rest[:7]
-    near_ref, far_ref, weight_ref, u_held, sems = rest[7:]
+def pack_z_kernel(plan, names, near_in, far_in, weight_in, x_in, u_in, *rest):
+    outs = rest[: len(names)]
+    scale_ref, perm_ref, x_ref, u_ref, near_ref, far_ref, weight_ref, u_held, sems = rest[len(names) :]
     copies = [
         pltpu.make_async_copy(source, target, sems.at[index])
         for index, (source, target) in enumerate(
@@ -402,17 +403,7 @@
         copy.wait()
     u_ref[...] = u_held[...].astype(F32)
     locator = Locator(plan, 1, {("own", "x"): x_ref, ("own", "u"): u_ref})
-    names = [("z", 1), ("z", -1)]
-
-    @pl.when(odd_in_z())
-    def _():
-        write_messages(locator, plan, names, (within_ref, between_ref))
-
-    @pl.when(jnp.logical_not(odd_in_z()))
-    def _():
-        write_messages(locator, plan, names, (between_ref, within_ref))
-
-    write_messages(locator, plan, [("z", 2)], [second_ref])
+    write_messages(locator, plan, names, outs)
     write_scales(near_ref, far_ref, weight_ref, scale_ref)
 
 
@@ -420,19 +411,7 @@
     write_messages(Locator(plan, 1, {("own", "x"): x_ref, ("own", "u"): u_ref}), plan, names, outs)
 
 
-def corner_kernel(plan, names, within_ref, between_ref, _, ahead_ref, behind_ref, *outs):
-    def split(from_ahead, from_behind):
-        ahead_ref[...] = from_ahead[pl.ds(0, ahead_ref.shape[0]), :]
-        behind_ref[...] = from_behind[pl.ds(0, behind_ref.shape[0]), :]
-
-    @pl.when(odd_in_z())
-    def _():
-        split(between_ref, within_ref)
-
-    @pl.when(jnp.logical_not(odd_in_z()))
-    def _():
-        split(within_ref, between_ref)
-
+def corner_kernel(plan, names, ahead_ref, behind_ref, _, *outs):
     locator = Locator(plan, 1, {("z", 1): ahead_ref, ("z", -1): behind_ref})
     for name, out in zip(names, outs):
         for reg, items in enumerate(plan[name].by_register()):
@@ -496,8 +475,6 @@
         staples = fields.compact_halves(acc_tile(acc, 0, 2 * k), acc_tile(acc, 0, 2 * k + 1))
         for m in range(2):
             part_ref[pl.ds((9 * m + k) * 8, 8), :] = part_reg(own_part, m, k) + weight[m] * staples[m]
-        staple = fields.compact_sum(acc_tile(acc, 1, 2 * k), acc_tile(acc, 1, 2 * k + 1))
-        part_ref[pl.ds((18 + k) * 8, 8), :] = weight[2] * staple
 
 
 def t_kernel(plan, t_size, names, scale_ref, perm_ref, x_ref, u_ref, own_shared, z_shared, z_part, *rest):
@@ -516,12 +493,14 @@
     for k in range(9):
         staple = fields.compact_sum(acc_tile(acc, 1, 2 * k), acc_tile(acc, 1, 2 * k + 1))
         part_ref[pl.ds(k * 8, 8), :] = direct[k] + weight[3] * staple
+        staple = fields.compact_sum(acc_tile(acc, 2, 2 * k), acc_tile(acc, 2, 2 * k + 1))
+        part_ref[pl.ds((9 + k) * 8, 8), :] = weight[2] * staple
 
 
 def last_kernel(plan, t_size, names, scale_ref, perm_ref, x_ref, u_ref, *rest):
-    own_shared, z_shared, t_shared, z_part, t_part, earlier = rest[:6]
-    received = rest[6 : 6 + len(names)]
-    out_ref, alone_ref, acc, ready, sems = rest[6 + len(names) :]
+    own_shared, z_shared, t_shared, t_part, earlier = rest[:5]
+    received = rest[5 : 5 + len(names)]
+    out_ref, alone_ref, acc, ready, sems = rest[5 + len(names) :]
     rows = ready.shape[0]
     first = pltpu.make_async_copy(earlier, out_ref.at[pl.ds(0, rows)], sems.at[0])
     first.start()
@@ -543,7 +522,7 @@
     direct = own_force(fields, 2, both)
     for k in range(9):
         staples = fields.compact_halves(acc_tile(acc, 0, 2 * k), acc_tile(acc, 0, 2 * k + 1))
-        ready[pl.ds(k * 8, 8), :] = part_reg(z_part, 2, k) + direct[k] + weight[2] * staples[0]
+        ready[pl.ds(k * 8, 8), :] = part_reg(t_part, 1, k) + direct[k] + weight[2] * staples[0]
         ready[pl.ds((9 + k) * 8, 8), :] = part_reg(t_part, 0, k) + weight[3] * staples[1]
     second = pltpu.make_async_copy(ready, out_ref.at[pl.ds(rows, rows)], sems.at[1])
     second.start()
@@ -566,24 +545,22 @@
 
     def moved(name, value):
         kind, step = name
-        if kind == "z":
+        if kind in ("z", "b"):
             return lax.ppermute(value, ("gz", "gy"), [((i + step) % z_size, i) for i in range(z_size)])
         return lax.ppermute(value, "ta", [((j + step) % t_size, j) for j in range(t_size)])
-
-    def exchanged(value, first):
-        pairs = [(i, (i + 1) % z_size) for i in range(first, z_size, 2)]
-        return lax.ppermute(value, ("gz", "gy"), pairs + [(j, i) for i, j in pairs])
 
     first_names = [name for name in plan if name[0] != "c"]
     corner_names = [name for name in plan if name[0] == "c"]
     t_names = [name for name in first_names if name[0] == "t"]
     in_hbm = functools.partial(pltpu.with_memory_space_constraint, memory_space=pltpu.HBM)
-    beyond_rows = 8 * plan["z", 2].count
-    ahead_rows, behind_rows = [8 * plan["z", step].count for step in (1, -1)]
-    shared_rows = max(ahead_rows, behind_rows)
-    within, between, beyond, scale, perm, *own = pl.pallas_call(
-        functools.partial(pack_z_kernel, plan),
-        out_shape=[rows_of(shared_rows), rows_of(shared_rows + 8), rows_of(beyond_rows)]
+    z_names = [name for name in first_names if name[0] != "t"]
+    least = {
+        ("z", 2): max(plan[name].count for name in corner_names),
+        ("z", -1): plan["z", 1].count + 1,
+    }
+    *sends, scale, perm, x_own, u_own = pl.pallas_call(
+        functools.partial(pack_z_kernel, plan, z_names),
+        out_shape=[rows_of(8 * max(plan[name].count, least.get(name, 0))) for name in z_names]
         + [
             rows_of(8 * 3 * NP),
             jax.ShapeDtypeStruct((len(all_shifts()) * LANES, LANES), jnp.bfloat16),
@@ -591,7 +568,7 @@
             rows_of(u_rows),
         ],
         in_specs=[hbm] * 5,
-        out_specs=[vmem] * 7,
+        out_specs=[vmem] * (len(z_names) + 4),
         scratch_shapes=[pltpu.SMEM((NP,), F32)] * 3
         + [pltpu.VMEM((u_rows, LANES), jnp.bfloat16), pltpu.SemaphoreType.DMA((5,))],
         compiler_params=limit,
@@ -603,8 +580,8 @@
         in_hbm(pole_vectors.reshape((x_rows, LANES))),
         in_hbm(gauge_links.reshape((u_rows, LANES))),
     )
-    between, within = exchanged(between, 1), exchanged(within, 0)
-    received = {("z", 2): moved(("z", 2), beyond)}
+    own = [x_own, u_own]
+    received = {name: moved(name, value) for name, value in zip(z_names, sends)}
     packed = pl.pallas_call(
         functools.partial(pack_t_kernel, plan, t_names),
         out_shape=[rows_of(8 * plan[name].count) for name in t_names],
@@ -644,20 +621,19 @@
         name="force_own",
     )(scale, *own, own_shared, own_alone)
     local = [scale, perm, *own]
-    received["z", 1], received["z", -1], *corners = pl.pallas_call(
+    corners = pl.pallas_call(
         functools.partial(corner_kernel, plan, corner_names),
-        out_shape=[rows_of(ahead_rows), rows_of(behind_rows)]
-        + [rows_of(8 * plan[name].count) for name in corner_names],
+        out_shape=[rows_of(8 * plan[name].count) for name in corner_names],
         in_specs=[vmem] * 3,
-        out_specs=[vmem] * (2 + len(corner_names)),
+        out_specs=[vmem] * len(corner_names),
         compiler_params=limit,
         name="pack_corners",
-    )(within, between, own_part)
+    )(received["z", 1], received["z", -1], own_part)
     received.update({name: moved(name, value) for name, value in zip(corner_names, corners)})
     names = [("z", 1), ("z", -1)]
     z_shared, z_part = pl.pallas_call(
         functools.partial(z_kernel, plan, t_size, names),
-        out_shape=[rows_of(shared["z"][1]), rows_of(3 * part_rows)],
+        out_shape=[rows_of(shared["z"][1]), rows_of(2 * part_rows)],
         in_specs=[vmem] * (6 + len(names)),
         out_specs=[vmem] * 2,
         scratch_shapes=scratch("z"),
@@ -665,21 +641,22 @@
         compiler_params=wide_limit,
         name="force_z",
     )(*local, own_shared, own_part, *[received[name] for name in names])
+    far_names = t_names + [("b", 1)]
     t_shared, t_part, earlier = pl.pallas_call(
-        functools.partial(t_kernel, plan, t_size, t_names),
-        out_shape=[rows_of(shared["t"][1]), rows_of(part_rows), rows_of(2 * part_rows)],
-        in_specs=[vmem] * (7 + len(t_names)),
+        functools.partial(t_kernel, plan, t_size, far_names),
+        out_shape=[rows_of(shared["t"][1]), rows_of(2 * part_rows), rows_of(2 * part_rows)],
+        in_specs=[vmem] * (7 + len(far_names)),
         out_specs=[vmem] * 3,
         scratch_shapes=scratch("t"),
         cost_estimate=cost(COSTS["t"]),
         compiler_params=wide_limit,
         name="force_t",
-    )(*local, own_shared, z_shared, z_part, *[received[name] for name in t_names])
+    )(*local, own_shared, z_shared, z_part, *[received[name] for name in far_names])
     names = list(received)
     force = pl.pallas_call(
         functools.partial(last_kernel, plan, t_size, names),
         out_shape=rows_of(u_rows),
-        in_specs=[vmem] * (10 + len(names)),
+        in_specs=[vmem] * (9 + len(names)),
         out_specs=hbm,
         scratch_shapes=scratch("corner")
         + [pltpu.VMEM((2 * part_rows, LANES), F32), pltpu.SemaphoreType.DMA((2,))],
@@ -691,7 +668,6 @@
         own_shared,
         z_shared,
         t_shared,
-        z_part,
         t_part,
         earlier,
         *[received[name] for name in names],

time: 16 us -> 15.7 us (0.981)
  starting transfers between devices: 9.62 us -> 8.99 us
  waiting for transfers between devices: 1.82 us -> 2.18 us
    ppermute x2 -> x0, starting transfers between devices: 4.56 us -> none  [exchanged(): return lax.ppermute(value, ('gz', 'gy'), pairs + [(j, i) for i, j in pairs])]
    ppermute x1 -> x4, starting transfers between devices: 0.89 us -> 5.38 us  [moved(): lax.ppermute(value, ('gz', 'gy'), [((i + step) % z_size, i) for i in rang...]
    ppermute x2, waiting for transfers between devices: 0.01 us -> 2.17 us  [moved(): lax.ppermute(value, 'ta', [((j + step) % t_size, j) for j in range(t_size)])]
    ppermute x1 -> x4, waiting for transfers between devices: 1.47 us -> 0.01 us  [moved(): lax.ppermute(value, ('gz', 'gy'), [((i + step) % z_size, i) for i in rang...]
    ppermute x2, starting transfers between devices: 4.17 us -> 3.61 us  [moved(): lax.ppermute(value, 'ta', [((j + step) % t_size, j) for j in range(t_size)])]
    ppermute x2 -> x0, waiting for transfers between devices: 0.35 us -> none  [exchanged(): return lax.ppermute(value, ('gz', 'gy'), pairs + [(j, i) for i, j in pairs])]
    pallas_call x1, Pallas kernels: 0.69 us -> 0.41 us  [on_device(): pl.pallas_call(functools.partial(z_kernel, plan, t_size, names), out_shap...]
    pallas_call x2, Pallas kernels: 1.75 us -> 1.99 us  [the longest x1 1.01 us: on_device(): pl.pallas_call(functools.partial(t_kernel, plan, t_size, far_names), out_...]
  transfers between devices with their start and end apart: 5 -> 6, of which waited for: 2 -> 1; matrix products, arithmetic and copies ran while one was open for 0% -> 0% of each run, Pallas kernels for 15% -> 15%
where the time goes in v12:
time: 15.7 us; the launch traced here: 15.6 us
  starting transfers between devices  8.99 us (57%)
  Pallas kernels  4.29 us (27%)
  waiting for transfers between devices  2.18 us (14%)
    ppermute x4, starting transfers between devices, moved(): lax.ppermute(value, ('gz', 'gy'), [((i + step) % z_size, i) for i in rang...  5.38 us
    ppermute x2, starting transfers between devices, moved(): lax.ppermute(value, 'ta', [((j + step) % t_size, j) for j in range(t_size)])  3.61 us
    ppermute x2, waiting for transfers between devices, moved(): lax.ppermute(value, 'ta', [((j + step) % t_size, j) for j in range(t_size)])  2.17 us
    pallas_call x1, Pallas kernels, on_device(): pl.pallas_call(functools.partial(last_kernel, plan, t_size, names), out_s...  1.01 us
    pallas_call x1, Pallas kernels, on_device(): pl.pallas_call(functools.partial(t_kernel, plan, t_size, far_names), out_...  1.01 us
    pallas_call x1, Pallas kernels, on_device(): pl.pallas_call(functools.partial(pack_z_kernel, plan, z_names), out_shape...  0.98 us
    pallas_call x1, Pallas kernels, on_device(): pl.pallas_call(functools.partial(own_fields_kernel, plan, t_size), out_sh...  0.48 us
    pallas_call x1, Pallas kernels, on_device(): pl.pallas_call(functools.partial(z_kernel, plan, t_size, names), out_shap...  0.41 us
  transfers between devices with their start and end apart: 6, of which 1 were waited for; matrix products, arithmetic and copies ran while one was open for 0% of the time, Pallas kernels for 15%

profile of v12, /device:TPU:0, one launch (start us, length us, event | category | flops | bytes accessed | tf_op | source)
XLA Modules:
  0.0 15.6 jit_solution(18155231589451255974)
XLA Ops:
  0.0 1.0 %pack_z.1 = (f32[88,128]{1,0:T(8,128)S(1)}, f32[120,128]{1,0:T(8,128)S(1)}, f32[96,128]{1,0:T(8,128)S(1)}, f32[112,128]{1,0:T(8,128)S(1)}, f32[96,128]{1,0:T(8,1...) custom-call(f32[4]{0:T(128)} %near_in.1, f32[4]{0:T(128)} %far_in.1, ...), custom_call_target="tpu_custom_call" | custom-call | tf_op jit(solution)/shard_map/pack_z/pallas_call | solution.py:561
  1.0 3.0 %collective-permute-start.2 = (f32[240,128]{1,0:T(8,128)S(1)}, f32[240,128]{1,0:T(8,128)S(1)}, u32[]{:S(2)}, u32[]{:S(2)}) collective-permute-start(f32[240,128]{1,0:T(8,128)S(1)} %pack_t.1), channel_id=1, source_target_pairs={{2,0},{0,2},{3,1},{1,3},{6,4},{4,6},{7,5},{5,7},{10,8},{8,10},{11,... | collective-permute-start | bytes 368648 | tf_op jit(solution)/shard_map/ppermute | solution.py:550
  4.0 0.0 collective-permute-start.1
  4.0 3.5 %collective-permute-start = (f32[88,128]{1,0:T(8,128)S(1)}, f32[88,128]{1,0:T(8,128)S(1)}, u32[]{:S(2)}, u32[]{:S(2)}) collective-permute-start(f32[88,128]{1,0:T(8,128)S(1)} %get-tuple-element.26), channel_id=1, source_target_pairs={{1,0},{4,1},{5,4},{8,5},{9,8},{12,9},{13,12},{0,13},{3,2},{6,3},{7... | collective-permute-start | bytes 135176 | tf_op jit(solution)/shard_map/ppermute | solution.py:549
  7.6 0.2 %collective-permute-start.3 = (f32[120,128]{1,0:T(8,128)S(1)}, f32[120,128]{1,0:T(8,128)S(1)}, u32[]{:S(2)}, u32[]{:S(2)}) collective-permute-start(f32[120,128]{1,0:T(8,128)S(1)} %get-tuple-element.30), channel_id=1, source_target_pairs={{1,0},{4,1},{5,4},{8,5},{9,8},{12,9},{13,12},{0,13},{3,2},{6,3},{7... | collective-permute-start | bytes 184328 | tf_op jit(solution)/shard_map/ppermute | solution.py:549
  7.7 1.7 %collective-permute-start.4 = (f32[112,128]{1,0:T(8,128)S(1)}, f32[112,128]{1,0:T(8,128)S(1)}, u32[]{:S(2)}, u32[]{:S(2)}) collective-permute-start(f32[112,128]{1,0:T(8,128)S(1)} %get-tuple-element.34), channel_id=1, source_target_pairs={{4,0},{5,1},{8,4},{9,5},{12,8},{13,9},{0,12},{1,13},{6,2},{7,3},{1... | collective-permute-start | bytes 172040 | tf_op jit(solution)/shard_map/ppermute | solution.py:549
  9.4 0.5 %fields_own.1 = (f32[816,128]{1,0:T(8,128)S(1)}, f32[768,128]{1,0:T(8,128)S(1)}) custom-call(bf16[1152,128]{1,0:T(8,128)(2,1)S(1)} %get-tuple-element.21.perm_ref, f32[96,128]{1,0:T(8,128)S(1)} %get-tuple-element.22.x_ref, f32[288,128]{1,0:T(8,128)S(1)} %get-tuple-element.23.u_ref), custom_call_target="tpu_custom_call" | custom-call | tf_op jit(solution)/shard_map/fields_own/pallas_call | solution.py:605
  9.9 0.4 %force_own.1.own_part._ = f32[144,128]{1,0:T(8,128)S(1)} custom-call(f32[96,128]{1,0:T(8,128)S(1)} %get-tuple-element.20.scale_ref, f32[96,128]{1,0:T(8,128)S(1)} %get-tuple-element.22.x_ref, f32[288,128]{1,0:T(8,128)S(1)} %get-tuple-element.23.u_ref, f32[816,128]{1,0:T(8,128)S(1)} %get-tuple-element.24.shared_ref.own_shared.rest_0_, ...), custom_call_target="tpu_custom_call" | custom-call | flops 1000000 | bytes 7380000 | tf_op jit(solution)/shard_map/force_own/pallas_call | solution.py:613
  10.3 0.0 collective-permute-done.rest_0_.ahead_ref.rest_5_
  10.3 0.0 collective-permute-done.1.rest_1_.behind_ref.rest_7_
  10.3 0.6 %collective-permute-start.5 = (f32[112,128]{1,0:T(8,128)S(1)}, f32[112,128]{1,0:T(8,128)S(1)}, u32[]{:S(2)}, u32[]{:S(2)}) collective-permute-start(f32[112,128]{1,0:T(8,128)S(1)} %pack_corners.1), channel_id=1, source_target_pairs={{2,0},{0,2},{3,1},{1,3},{6,4},{4,6},{7,5},{5,7},{10,8},{8,10},{11,... | collective-permute-start | bytes 172040 | tf_op jit(solution)/shard_map/ppermute | solution.py:550
  10.9 0.4 %force_z.1 = (f32[720,128]{1,0:T(8,128)S(1)}, f32[144,128]{1,0:T(8,128)S(1)}) custom-call(f32[96,128]{1,0:T(8,128)S(1)} %get-tuple-element.20.scale_ref, bf16[1152,128]{1,0:T(8,128)(2,1)S(1)} %get-tuple-element.21.perm_ref, f32[96,128]{1,0:T(8,128)S(1)} %get-tuple-element.22.x_ref, f32[288,128]{1,0:T(8,128)S(1)} %get-tuple-element.23.u_ref, ...), custom_call_target="tpu_custom_call" | custom-call | flops 1000000 | bytes 7380000 | tf_op jit(solution)/shard_map/force_z/pallas_call | solution.py:634
  11.3 0.0 collective-permute-done.3.rest_1_.rest_6_
  11.3 0.0 collective-permute-done.2.rest_0_.rest_9_
  11.3 1.0 %force_t.1 = (f32[336,128]{1,0:T(8,128)S(1)}, f32[144,128]{1,0:T(8,128)S(1)}, f32[144,128]{1,0:T(8,128)S(1)}) custom-call(f32[96,128]{1,0:T(8,128)S(1)} %get-tuple-element.20.scale_ref, bf16[1152,128]{1,0:T(8,128)(2,1)S(1)} %get-tuple-element.21.perm_ref, f32[96,128]{1,0:T(8,128)S(1)} %get-tuple-element.22.x_ref, f32[288,128]{1,0:T(8,128)S(1)} %get-tuple-element.23.u_ref, ...), custom_call_target="tpu_custom_call" | custom-call | flops 1000000 | bytes 7380000 | tf_op jit(solution)/shard_map/force_t/pallas_call | solution.py:645
  12.4 0.0 collective-permute-done.4.rest_8_
  12.4 2.2 %collective-permute-done.5.rest_10_ = f32[112,128]{1,0:T(8,128)S(1)} collective-permute-done((f32[112,128]{1,0:T(8,128)S(1)}, f32[112,128]{1,0:T(8,128)S(1)}, u32[]{:S(2)}, u32[]{:S(2)}) %collective-permute-start.5) | collective-permute-done | bytes 57376 | tf_op jit(solution)/shard_map/ppermute | solution.py:550
  14.5 1.0 %force_corner.1 = f32[288,128]{1,0:T(8,128)} custom-call(f32[96,128]{1,0:T(8,128)S(1)} %get-tuple-element.20.scale_ref, bf16[1152,128]{1,0:T(8,128)(2,1)S(1)} %get-tuple-element.21.perm_ref, f32[96,128]{1,0:T(8,128)S(1)} %get-tuple-element.22.x_ref, f32[288,128]{1,0:T(8,128)S(1)} %get-tuple-element.23.u_ref, ...), custom_call_target="tpu_custom_call" | custom-call | flops 1000000 | bytes 3690000 | tf_op jit(solution)/shard_map/force_corner/pallas_call | solution.py:656
  (2 shorter events, 0.0 us)
Async XLA Ops:
  1.0 10.3 %collective-permute-start.2 = (f32[240,128]{1,0:T(8,128)S(1)}, f32[240,128]{1,0:T(8,128)S(1)}, u32[]{:S(2)}, u32[]{:S(2)}) collective-permute-start(f32[240,128]{1,0:T(8,128)S(1)} %pack_t.1), channel_id=1, source_target_pairs={{2,0},{0,2},{3,1},{1,3},{6,4},{4,6},{7,5},{5,7},{10,8},{8,10},{11,... | collective-permute-start | bytes 368648 | tf_op jit(solution)/shard_map/ppermute | solution.py:550
  4.0 6.3 %collective-permute-start.1 = (f32[96,128]{1,0:T(8,128)S(1)}, f32[96,128]{1,0:T(8,128)S(1)}, u32[]{:S(2)}, u32[]{:S(2)}) collective-permute-start(f32[96,128]{1,0:T(8,128)S(1)} %get-tuple-element.27), channel_id=1, source_target_pairs={{13,0},{0,1},{1,4},{4,5},{5,8},{8,9},{9,12},{12,13},{15,2},{2,3},{... | collective-permute-start | bytes 147464 | tf_op jit(solution)/shard_map/ppermute | solution.py:549
  4.0 6.2 %collective-permute-start = (f32[88,128]{1,0:T(8,128)S(1)}, f32[88,128]{1,0:T(8,128)S(1)}, u32[]{:S(2)}, u32[]{:S(2)}) collective-permute-start(f32[88,128]{1,0:T(8,128)S(1)} %get-tuple-element.26), channel_id=1, source_target_pairs={{1,0},{4,1},{5,4},{8,5},{9,8},{12,9},{13,12},{0,13},{3,2},{6,3},{7... | collective-permute-start | bytes 135176 | tf_op jit(solution)/shard_map/ppermute | solution.py:549
  7.6 3.8 %collective-permute-start.3 = (f32[120,128]{1,0:T(8,128)S(1)}, f32[120,128]{1,0:T(8,128)S(1)}, u32[]{:S(2)}, u32[]{:S(2)}) collective-permute-start(f32[120,128]{1,0:T(8,128)S(1)} %get-tuple-element.30), channel_id=1, source_target_pairs={{1,0},{4,1},{5,4},{8,5},{9,8},{12,9},{13,12},{0,13},{3,2},{6,3},{7... | collective-permute-start | bytes 184328 | tf_op jit(solution)/shard_map/ppermute | solution.py:549
  7.7 4.6 %collective-permute-start.4 = (f32[112,128]{1,0:T(8,128)S(1)}, f32[112,128]{1,0:T(8,128)S(1)}, u32[]{:S(2)}, u32[]{:S(2)}) collective-permute-start(f32[112,128]{1,0:T(8,128)S(1)} %get-tuple-element.34), channel_id=1, source_target_pairs={{4,0},{5,1},{8,4},{9,5},{12,8},{13,9},{0,12},{1,13},{6,2},{7,3},{1... | collective-permute-start | bytes 172040 | tf_op jit(solution)/shard_map/ppermute | solution.py:549
  10.3 4.2 %collective-permute-start.5 = (f32[112,128]{1,0:T(8,128)S(1)}, f32[112,128]{1,0:T(8,128)S(1)}, u32[]{:S(2)}, u32[]{:S(2)}) collective-permute-start(f32[112,128]{1,0:T(8,128)S(1)} %pack_corners.1), channel_id=1, source_target_pairs={{2,0},{0,2},{3,1},{1,3},{6,4},{4,6},{7,5},{5,7},{10,8},{8,10},{11,... | collective-permute-start | bytes 172040 | tf_op jit(solution)/shard_map/ppermute | solution.py:550

commit v13 on v12

--- a/solution.py
+++ b/solution.py
@@ -411,7 +411,7 @@
     write_messages(Locator(plan, 1, {("own", "x"): x_ref, ("own", "u"): u_ref}), plan, names, outs)
 
 
-def corner_kernel(plan, names, ahead_ref, behind_ref, _, *outs):
+def corner_kernel(plan, names, ahead_ref, behind_ref, *outs):
     locator = Locator(plan, 1, {("z", 1): ahead_ref, ("z", -1): behind_ref})
     for name, out in zip(names, outs):
         for reg, items in enumerate(plan[name].by_register()):
@@ -554,10 +554,9 @@
     t_names = [name for name in first_names if name[0] == "t"]
     in_hbm = functools.partial(pltpu.with_memory_space_constraint, memory_space=pltpu.HBM)
     z_names = [name for name in first_names if name[0] != "t"]
-    least = {
-        ("z", 2): max(plan[name].count for name in corner_names),
-        ("z", -1): plan["z", 1].count + 1,
-    }
+    corner_count = max(plan[name].count for name in corner_names)
+    ahead_count = max(plan["z", 1].count, plan["t", 1].count - corner_count + 1)
+    least = {("z", 2): corner_count, ("z", 1): ahead_count, ("z", -1): ahead_count + 1}
     *sends, scale, perm, x_own, u_own = pl.pallas_call(
         functools.partial(pack_z_kernel, plan, z_names),
         out_shape=[rows_of(8 * max(plan[name].count, least.get(name, 0))) for name in z_names]
@@ -624,11 +623,11 @@
     corners = pl.pallas_call(
         functools.partial(corner_kernel, plan, corner_names),
         out_shape=[rows_of(8 * plan[name].count) for name in corner_names],
-        in_specs=[vmem] * 3,
+        in_specs=[vmem] * 2,
         out_specs=[vmem] * len(corner_names),
         compiler_params=limit,
         name="pack_corners",
-    )(received["z", 1], received["z", -1], own_part)
+    )(received["z", 1], received["z", -1])
     received.update({name: moved(name, value) for name, value in zip(corner_names, corners)})
     names = [("z", 1), ("z", -1)]
     z_shared, z_part = pl.pallas_call(

time: 15.7 us -> 14.8 us (0.943)
  waiting for transfers between devices: 2.18 us -> 1.33 us
    ppermute x4, starting transfers between devices: 5.38 us -> 6.41 us  [moved(): lax.ppermute(value, ('gz', 'gy'), [((i + step) % z_size, i) for i in rang...]
    ppermute x2, starting transfers between devices: 3.61 us -> 2.59 us  [moved(): lax.ppermute(value, 'ta', [((j + step) % t_size, j) for j in range(t_size)])]
    ppermute x2, waiting for transfers between devices: 2.17 us -> 1.32 us  [moved(): lax.ppermute(value, 'ta', [((j + step) % t_size, j) for j in range(t_size)])]
  transfers between devices with their start and end apart: 6 -> 6, of which waited for: 1 -> 1; matrix products, arithmetic and copies ran while one was open for 0% -> 0% of each run, Pallas kernels for 15% -> 16%
where the time goes in v13:
time: 14.8 us; the launch traced here: 14.7 us
  starting transfers between devices  9.01 us (61%)
  Pallas kernels  4.29 us (29%)
  waiting for transfers between devices  1.33 us (9%)
    ppermute x4, starting transfers between devices, moved(): lax.ppermute(value, ('gz', 'gy'), [((i + step) % z_size, i) for i in rang...  6.41 us
    ppermute x2, starting transfers between devices, moved(): lax.ppermute(value, 'ta', [((j + step) % t_size, j) for j in range(t_size)])  2.59 us
    ppermute x2, waiting for transfers between devices, moved(): lax.ppermute(value, 'ta', [((j + step) % t_size, j) for j in range(t_size)])  1.32 us
    pallas_call x1, Pallas kernels, on_device(): pl.pallas_call(functools.partial(t_kernel, plan, t_size, far_names), out_...  1.01 us
    pallas_call x1, Pallas kernels, on_device(): pl.pallas_call(functools.partial(last_kernel, plan, t_size, names), out_s...  1.01 us
    pallas_call x1, Pallas kernels, on_device(): pl.pallas_call(functools.partial(pack_z_kernel, plan, z_names), out_shape...  0.98 us
    pallas_call x1, Pallas kernels, on_device(): pl.pallas_call(functools.partial(own_fields_kernel, plan, t_size), out_sh...  0.48 us
    pallas_call x1, Pallas kernels, on_device(): pl.pallas_call(functools.partial(z_kernel, plan, t_size, names), out_shap...  0.41 us
  transfers between devices with their start and end apart: 6, of which 1 were waited for; matrix products, arithmetic and copies ran while one was open for 0% of the time, Pallas kernels for 16%

profile of v13, /device:TPU:0, one launch (start us, length us, event | category | flops | bytes accessed | tf_op | source)
XLA Modules:
  0.0 14.7 jit_solution(8609911123046049189)
XLA Ops:
  0.0 1.0 %pack_z.1 = (f32[136,128]{1,0:T(8,128)S(1)}, f32[120,128]{1,0:T(8,128)S(1)}, f32[144,128]{1,0:T(8,128)S(1)}, f32[112,128]{1,0:T(8,128)S(1)}, f32[96,128]{1,0:T(8...) custom-call(f32[4]{0:T(128)} %near_in.1, f32[4]{0:T(128)} %far_in.1, ...), custom_call_target="tpu_custom_call" | custom-call | tf_op jit(solution)/shard_map/pack_z/pallas_call | solution.py:560
  1.0 0.5 %collective-permute-start.1 = (f32[144,128]{1,0:T(8,128)S(1)}, f32[144,128]{1,0:T(8,128)S(1)}, u32[]{:S(2)}, u32[]{:S(2)}) collective-permute-start(f32[144,128]{1,0:T(8,128)S(1)} %get-tuple-element.27), channel_id=1, source_target_pairs={{13,0},{0,1},{1,4},{4,5},{5,8},{8,9},{9,12},{12,13},{15,2},{2,3},{... | collective-permute-start | bytes 221192 | tf_op jit(solution)/shard_map/ppermute | solution.py:549
  1.5 4.1 %collective-permute-start = (f32[136,128]{1,0:T(8,128)S(1)}, f32[136,128]{1,0:T(8,128)S(1)}, u32[]{:S(2)}, u32[]{:S(2)}) collective-permute-start(f32[136,128]{1,0:T(8,128)S(1)} %get-tuple-element.26), channel_id=1, source_target_pairs={{1,0},{4,1},{5,4},{8,5},{9,8},{12,9},{13,12},{0,13},{3,2},{6,3},{7... | collective-permute-start | bytes 208904 | tf_op jit(solution)/shard_map/ppermute | solution.py:549
  5.6 2.0 %collective-permute-start.2 = (f32[240,128]{1,0:T(8,128)S(1)}, f32[240,128]{1,0:T(8,128)S(1)}, u32[]{:S(2)}, u32[]{:S(2)}) collective-permute-start(f32[240,128]{1,0:T(8,128)S(1)} %pack_t.1), channel_id=1, source_target_pairs={{2,0},{0,2},{3,1},{1,3},{6,4},{4,6},{7,5},{5,7},{10,8},{8,10},{11,... | collective-permute-start | bytes 368648 | tf_op jit(solution)/shard_map/ppermute | solution.py:550
  7.6 0.0 collective-permute-start.3
  7.6 1.8 %collective-permute-start.4 = (f32[112,128]{1,0:T(8,128)S(1)}, f32[112,128]{1,0:T(8,128)S(1)}, u32[]{:S(2)}, u32[]{:S(2)}) collective-permute-start(f32[112,128]{1,0:T(8,128)S(1)} %get-tuple-element.34), channel_id=1, source_target_pairs={{4,0},{5,1},{8,4},{9,5},{12,8},{13,9},{0,12},{1,13},{6,2},{7,3},{1... | collective-permute-start | bytes 172040 | tf_op jit(solution)/shard_map/ppermute | solution.py:549
  9.4 0.0 collective-permute-done.rest_0_.ahead_ref.rest_5_
  9.4 0.0 collective-permute-done.1.rest_1_.behind_ref.rest_7_
  9.4 0.6 %collective-permute-start.5 = (f32[112,128]{1,0:T(8,128)S(1)}, f32[112,128]{1,0:T(8,128)S(1)}, u32[]{:S(2)}, u32[]{:S(2)}) collective-permute-start(f32[112,128]{1,0:T(8,128)S(1)} %pack_corners.1), channel_id=1, source_target_pairs={{2,0},{0,2},{3,1},{1,3},{6,4},{4,6},{7,5},{5,7},{10,8},{8,10},{11,... | collective-permute-start | bytes 172040 | tf_op jit(solution)/shard_map/ppermute | solution.py:550
  10.0 0.5 %fields_own.1 = (f32[816,128]{1,0:T(8,128)S(1)}, f32[768,128]{1,0:T(8,128)S(1)}) custom-call(bf16[1152,128]{1,0:T(8,128)(2,1)S(1)} %get-tuple-element.21.perm_ref, f32[96,128]{1,0:T(8,128)S(1)} %get-tuple-element.22.x_ref, f32[288,128]{1,0:T(8,128)S(1)} %get-tuple-element.23.u_ref), custom_call_target="tpu_custom_call" | custom-call | tf_op jit(solution)/shard_map/fields_own/pallas_call | solution.py:604
  10.5 0.4 %force_own.1.own_part = f32[144,128]{1,0:T(8,128)S(1)} custom-call(f32[96,128]{1,0:T(8,128)S(1)} %get-tuple-element.20.scale_ref, f32[96,128]{1,0:T(8,128)S(1)} %get-tuple-element.22.x_ref, f32[288,128]{1,0:T(8,128)S(1)} %get-tuple-element.23.u_ref, f32[816,128]{1,0:T(8,128)S(1)} %get-tuple-element.24.shared_ref.own_shared.rest_0_, ...), custom_call_target="tpu_custom_call" | custom-call | flops 1000000 | bytes 7380000 | tf_op jit(solution)/shard_map/force_own/pallas_call | solution.py:612
  10.9 0.4 %force_z.1 = (f32[720,128]{1,0:T(8,128)S(1)}, f32[144,128]{1,0:T(8,128)S(1)}) custom-call(f32[96,128]{1,0:T(8,128)S(1)} %get-tuple-element.20.scale_ref, bf16[1152,128]{1,0:T(8,128)(2,1)S(1)} %get-tuple-element.21.perm_ref, f32[96,128]{1,0:T(8,128)S(1)} %get-tuple-element.22.x_ref, f32[288,128]{1,0:T(8,128)S(1)} %get-tuple-element.23.u_ref, ...), custom_call_target="tpu_custom_call" | custom-call | flops 1000000 | bytes 7380000 | tf_op jit(solution)/shard_map/force_z/pallas_call | solution.py:633
  11.3 0.0 collective-permute-done.3.rest_1_.rest_6_
  11.3 0.0 collective-permute-done.2.rest_0_.rest_9_
  11.3 1.0 %force_t.1 = (f32[336,128]{1,0:T(8,128)S(1)}, f32[144,128]{1,0:T(8,128)S(1)}, f32[144,128]{1,0:T(8,128)S(1)}) custom-call(f32[96,128]{1,0:T(8,128)S(1)} %get-tuple-element.20.scale_ref, bf16[1152,128]{1,0:T(8,128)(2,1)S(1)} %get-tuple-element.21.perm_ref, f32[96,128]{1,0:T(8,128)S(1)} %get-tuple-element.22.x_ref, f32[288,128]{1,0:T(8,128)S(1)} %get-tuple-element.23.u_ref, ...), custom_call_target="tpu_custom_call" | custom-call | flops 1000000 | bytes 7380000 | tf_op jit(solution)/shard_map/force_t/pallas_call | solution.py:644
  12.4 0.0 collective-permute-done.4.rest_8_
  12.4 1.3 %collective-permute-done.5.rest_10_ = f32[112,128]{1,0:T(8,128)S(1)} collective-permute-done((f32[112,128]{1,0:T(8,128)S(1)}, f32[112,128]{1,0:T(8,128)S(1)}, u32[]{:S(2)}, u32[]{:S(2)}) %collective-permute-start.5) | collective-permute-done | bytes 57376 | tf_op jit(solution)/shard_map/ppermute | solution.py:550
  13.7 1.0 %force_corner.1 = f32[288,128]{1,0:T(8,128)} custom-call(f32[96,128]{1,0:T(8,128)S(1)} %get-tuple-element.20.scale_ref, bf16[1152,128]{1,0:T(8,128)(2,1)S(1)} %get-tuple-element.21.perm_ref, f32[96,128]{1,0:T(8,128)S(1)} %get-tuple-element.22.x_ref, f32[288,128]{1,0:T(8,128)S(1)} %get-tuple-element.23.u_ref, ...), custom_call_target="tpu_custom_call" | custom-call | flops 1000000 | bytes 3690000 | tf_op jit(solution)/shard_map/force_corner/pallas_call | solution.py:655
  (2 shorter events, 0.0 us)
Async XLA Ops:
  1.0 8.4 %collective-permute-start.1 = (f32[144,128]{1,0:T(8,128)S(1)}, f32[144,128]{1,0:T(8,128)S(1)}, u32[]{:S(2)}, u32[]{:S(2)}) collective-permute-start(f32[144,128]{1,0:T(8,128)S(1)} %get-tuple-element.27), channel_id=1, source_target_pairs={{13,0},{0,1},{1,4},{4,5},{5,8},{8,9},{9,12},{12,13},{15,2},{2,3},{... | collective-permute-start | bytes 221192 | tf_op jit(solution)/shard_map/ppermute | solution.py:549
  1.5 7.9 %collective-permute-start = (f32[136,128]{1,0:T(8,128)S(1)}, f32[136,128]{1,0:T(8,128)S(1)}, u32[]{:S(2)}, u32[]{:S(2)}) collective-permute-start(f32[136,128]{1,0:T(8,128)S(1)} %get-tuple-element.26), channel_id=1, source_target_pairs={{1,0},{4,1},{5,4},{8,5},{9,8},{12,9},{13,12},{0,13},{3,2},{6,3},{7... | collective-permute-start | bytes 208904 | tf_op jit(solution)/shard_map/ppermute | solution.py:549
  5.6 5.7 %collective-permute-start.2 = (f32[240,128]{1,0:T(8,128)S(1)}, f32[240,128]{1,0:T(8,128)S(1)}, u32[]{:S(2)}, u32[]{:S(2)}) collective-permute-start(f32[240,128]{1,0:T(8,128)S(1)} %pack_t.1), channel_id=1, source_target_pairs={{2,0},{0,2},{3,1},{1,3},{6,4},{4,6},{7,5},{5,7},{10,8},{8,10},{11,... | collective-permute-start | bytes 368648 | tf_op jit(solution)/shard_map/ppermute | solution.py:550
  7.6 3.7 %collective-permute-start.3 = (f32[120,128]{1,0:T(8,128)S(1)}, f32[120,128]{1,0:T(8,128)S(1)}, u32[]{:S(2)}, u32[]{:S(2)}) collective-permute-start(f32[120,128]{1,0:T(8,128)S(1)} %get-tuple-element.30), channel_id=1, source_target_pairs={{1,0},{4,1},{5,4},{8,5},{9,8},{12,9},{13,12},{0,13},{3,2},{6,3},{7... | collective-permute-start | bytes 184328 | tf_op jit(solution)/shard_map/ppermute | solution.py:549
  7.6 4.8 %collective-permute-start.4 = (f32[112,128]{1,0:T(8,128)S(1)}, f32[112,128]{1,0:T(8,128)S(1)}, u32[]{:S(2)}, u32[]{:S(2)}) collective-permute-start(f32[112,128]{1,0:T(8,128)S(1)} %get-tuple-element.34), channel_id=1, source_target_pairs={{4,0},{5,1},{8,4},{9,5},{12,8},{13,9},{0,12},{1,13},{6,2},{7,3},{1... | collective-permute-start | bytes 172040 | tf_op jit(solution)/shard_map/ppermute | solution.py:549
  9.4 4.2 %collective-permute-start.5 = (f32[112,128]{1,0:T(8,128)S(1)}, f32[112,128]{1,0:T(8,128)S(1)}, u32[]{:S(2)}, u32[]{:S(2)}) collective-permute-start(f32[112,128]{1,0:T(8,128)S(1)} %pack_corners.1), channel_id=1, source_target_pairs={{2,0},{0,2},{3,1},{1,3},{6,4},{4,6},{7,5},{5,7},{10,8},{8,10},{11,... | collective-permute-start | bytes 172040 | tf_op jit(solution)/shard_map/ppermute | solution.py:550

commit v14 on v13

--- a/solution.py
+++ b/solution.py
@@ -387,9 +387,14 @@
             out[pl.ds(8 * reg, 8), :] = locator.assemble(spots)
 
 
+def odd_in_z():
+    return (lax.axis_index("gz") * lax.axis_size("gy") + lax.axis_index("gy")) % 2 == 1
+
+
 def pack_z_kernel(plan, names, near_in, far_in, weight_in, x_in, u_in, *rest):
-    outs = rest[: len(names)]
-    scale_ref, perm_ref, x_ref, u_ref, near_ref, far_ref, weight_ref, u_held, sems = rest[len(names) :]
+    within_ref, between_ref = rest[:2]
+    outs = rest[2 : 2 + len(names)]
+    scale_ref, perm_ref, x_ref, u_ref, near_ref, far_ref, weight_ref, u_held, sems = rest[2 + len(names) :]
     copies = [
         pltpu.make_async_copy(source, target, sems.at[index])
         for index, (source, target) in enumerate(
@@ -403,6 +408,16 @@
         copy.wait()
     u_ref[...] = u_held[...].astype(F32)
     locator = Locator(plan, 1, {("own", "x"): x_ref, ("own", "u"): u_ref})
+    both = [("z", 1), ("z", -1)]
+
+    @pl.when(odd_in_z())
+    def _():
+        write_messages(locator, plan, both, (within_ref, between_ref))
+
+    @pl.when(jnp.logical_not(odd_in_z()))
+    def _():
+        write_messages(locator, plan, both, (between_ref, within_ref))
+
     write_messages(locator, plan, names, outs)
     write_scales(near_ref, far_ref, weight_ref, scale_ref)
 
@@ -411,7 +426,19 @@
     write_messages(Locator(plan, 1, {("own", "x"): x_ref, ("own", "u"): u_ref}), plan, names, outs)
 
 
-def corner_kernel(plan, names, ahead_ref, behind_ref, *outs):
+def corner_kernel(plan, names, within_ref, between_ref, _, ahead_ref, behind_ref, *outs):
+    def split(from_ahead, from_behind):
+        ahead_ref[...] = from_ahead[pl.ds(0, ahead_ref.shape[0]), :]
+        behind_ref[...] = from_behind[pl.ds(0, behind_ref.shape[0]), :]
+
+    @pl.when(odd_in_z())
+    def _():
+        split(between_ref, within_ref)
+
+    @pl.when(jnp.logical_not(odd_in_z()))
+    def _():
+        split(within_ref, between_ref)
+
     locator = Locator(plan, 1, {("z", 1): ahead_ref, ("z", -1): behind_ref})
     for name, out in zip(names, outs):
         for reg, items in enumerate(plan[name].by_register()):
@@ -549,17 +576,22 @@
             return lax.ppermute(value, ("gz", "gy"), [((i + step) % z_size, i) for i in range(z_size)])
         return lax.ppermute(value, "ta", [((j + step) % t_size, j) for j in range(t_size)])
 
+    def exchanged(value, first):
+        pairs = [(i, (i + 1) % z_size) for i in range(first, z_size, 2)]
+        return lax.ppermute(value, ("gz", "gy"), pairs + [(j, i) for i, j in pairs])
+
     first_names = [name for name in plan if name[0] != "c"]
     corner_names = [name for name in plan if name[0] == "c"]
     t_names = [name for name in first_names if name[0] == "t"]
     in_hbm = functools.partial(pltpu.with_memory_space_constraint, memory_space=pltpu.HBM)
-    z_names = [name for name in first_names if name[0] != "t"]
+    z_names = [("b", 1), ("z", 2)]
     corner_count = max(plan[name].count for name in corner_names)
-    ahead_count = max(plan["z", 1].count, plan["t", 1].count - corner_count + 1)
-    least = {("z", 2): corner_count, ("z", 1): ahead_count, ("z", -1): ahead_count + 1}
-    *sends, scale, perm, x_own, u_own = pl.pallas_call(
+    exchange_counts = [plan["z", step].count for step in (1, -1)]
+    exchange = max(exchange_counts + [plan["t", 1].count - corner_count + 1])
+    within, between, *sends, scale, perm, x_own, u_own = pl.pallas_call(
         functools.partial(pack_z_kernel, plan, z_names),
-        out_shape=[rows_of(8 * max(plan[name].count, least.get(name, 0))) for name in z_names]
+        out_shape=[rows_of(8 * exchange), rows_of(8 * (exchange + 1))]
+        + [rows_of(8 * max(plan[name].count, corner_count)) for name in z_names]
         + [
             rows_of(8 * 3 * NP),
             jax.ShapeDtypeStruct((len(all_shifts()) * LANES, LANES), jnp.bfloat16),
@@ -567,7 +599,7 @@
             rows_of(u_rows),
         ],
         in_specs=[hbm] * 5,
-        out_specs=[vmem] * (len(z_names) + 4),
+        out_specs=[vmem] * (len(z_names) + 6),
         scratch_shapes=[pltpu.SMEM((NP,), F32)] * 3
         + [pltpu.VMEM((u_rows, LANES), jnp.bfloat16), pltpu.SemaphoreType.DMA((5,))],
         compiler_params=limit,
@@ -580,6 +612,7 @@
         in_hbm(gauge_links.reshape((u_rows, LANES))),
     )
     own = [x_own, u_own]
+    between, within = exchanged(between, 1), exchanged(within, 0)
     received = {name: moved(name, value) for name, value in zip(z_names, sends)}
     packed = pl.pallas_call(
         functools.partial(pack_t_kernel, plan, t_names),
@@ -620,14 +653,15 @@
         name="force_own",
     )(scale, *own, own_shared, own_alone)
     local = [scale, perm, *own]
-    corners = pl.pallas_call(
+    received["z", 1], received["z", -1], *corners = pl.pallas_call(
         functools.partial(corner_kernel, plan, corner_names),
-        out_shape=[rows_of(8 * plan[name].count) for name in corner_names],
-        in_specs=[vmem] * 2,
-        out_specs=[vmem] * len(corner_names),
+        out_shape=[rows_of(8 * count) for count in exchange_counts]
+        + [rows_of(8 * plan[name].count) for name in corner_names],
+        in_specs=[vmem] * 3,
+        out_specs=[vmem] * (2 + len(corner_names)),
         compiler_params=limit,
         name="pack_corners",
-    )(received["z", 1], received["z", -1])
+    )(within, between, own_part)
     received.update({name: moved(name, value) for name, value in zip(corner_names, corners)})
     names = [("z", 1), ("z", -1)]
     z_shared, z_part = pl.pallas_call(

time: 14.8 us -> 15.5 us (1.047)
  waiting for transfers between devices: 1.33 us -> 2.19 us
  starting transfers between devices: 9.01 us -> 8.74 us
    ppermute x0 -> x2, starting transfers between devices: none -> 4.55 us  [exchanged(): return lax.ppermute(value, ('gz', 'gy'), pairs + [(j, i) for i, j in pairs])]
    ppermute x4 -> x2, starting transfers between devices: 6.41 us -> 2.03 us  [moved(): lax.ppermute(value, ('gz', 'gy'), [((i + step) % z_size, i) for i in rang...]
    ppermute x2, waiting for transfers between devices: 1.32 us -> 2.18 us  [moved(): lax.ppermute(value, 'ta', [((j + step) % t_size, j) for j in range(t_size)])]
    ppermute x2, starting transfers between devices: 2.59 us -> 2.15 us  [moved(): lax.ppermute(value, 'ta', [((j + step) % t_size, j) for j in range(t_size)])]
  transfers between devices with their start and end apart: 6 -> 6, of which waited for: 1 -> 2; matrix products, arithmetic and copies ran while one was open for 0% -> 0% of each run, Pallas kernels for 16% -> 15%
where the time goes in v14:
time: 15.5 us; the launch traced here: 15.3 us
  starting transfers between devices  8.74 us (56%)
  Pallas kernels  4.35 us (28%)
  waiting for transfers between devices  2.19 us (14%)
    ppermute x2, starting transfers between devices, exchanged(): return lax.ppermute(value, ('gz', 'gy'), pairs + [(j, i) for i, j in pairs])  4.55 us
    ppermute x2, waiting for transfers between devices, moved(): lax.ppermute(value, 'ta', [((j + step) % t_size, j) for j in range(t_size)])  2.18 us
    ppermute x2, starting transfers between devices, moved(): lax.ppermute(value, 'ta', [((j + step) % t_size, j) for j in range(t_size)])  2.15 us
    ppermute x2, starting transfers between devices, moved(): lax.ppermute(value, ('gz', 'gy'), [((i + step) % z_size, i) for i in rang...  2.03 us
    pallas_call x1, Pallas kernels, on_device(): pl.pallas_call(functools.partial(last_kernel, plan, t_size, names), out_s...  1.02 us
    pallas_call x1, Pallas kernels, on_device(): pl.pallas_call(functools.partial(t_kernel, plan, t_size, far_names), out_...  1.01 us
    pallas_call x1, Pallas kernels, on_device(): pl.pallas_call(functools.partial(pack_z_kernel, plan, z_names), out_shape...  1 us
    pallas_call x1, Pallas kernels, on_device(): pl.pallas_call(functools.partial(own_fields_kernel, plan, t_size), out_sh...  0.48 us
  transfers between devices with their start and end apart: 6, of which 2 were waited for; matrix products, arithmetic and copies ran while one was open for 0% of the time, Pallas kernels for 15%

profile of v14, /device:TPU:0, one launch (start us, length us, event | category | flops | bytes accessed | tf_op | source)
XLA Modules:
  0.0 15.3 jit_solution(285724219645096250)
XLA Ops:
  0.0 1.0 %pack_z.1 = (f32[136,128]{1,0:T(8,128)S(1)}, f32[144,128]{1,0:T(8,128)S(1)}, f32[120,128]{1,0:T(8,128)S(1)}, f32[112,128]{1,0:T(8,128)S(1)}, f32[96,128]{1,0:T(8...) custom-call(f32[4]{0:T(128)} %near_in.1, f32[4]{0:T(128)} %far_in.1, ...), custom_call_target="tpu_custom_call" | custom-call | tf_op jit(solution)/shard_map/pack_z/pallas_call | solution.py:591
  1.0 4.6 %collective-permute-start.1 = (f32[144,128]{1,0:T(8,128)S(1)}, f32[144,128]{1,0:T(8,128)S(1)}, u32[]{:S(2)}, u32[]{:S(2)}) collective-permute-start(f32[144,128]{1,0:T(8,128)S(1)} %get-tuple-element.30), channel_id=1, source_target_pairs={{1,4},{5,8},{9,12},{13,0},{4,1},{8,5},{12,9},{0,13},{3,6},{7,10},{... | collective-permute-start | bytes 221192 | tf_op jit(solution)/shard_map/ppermute | solution.py:581
  5.6 0.0 collective-permute-start
  5.6 1.6 %collective-permute-start.2 = (f32[240,128]{1,0:T(8,128)S(1)}, f32[240,128]{1,0:T(8,128)S(1)}, u32[]{:S(2)}, u32[]{:S(2)}) collective-permute-start(f32[240,128]{1,0:T(8,128)S(1)} %pack_t.1), channel_id=1, source_target_pairs={{2,0},{0,2},{3,1},{1,3},{6,4},{4,6},{7,5},{5,7},{10,8},{8,10},{11,... | collective-permute-start | bytes 368648 | tf_op jit(solution)/shard_map/ppermute | solution.py:577
  7.1 0.5 %collective-permute-start.3 = (f32[120,128]{1,0:T(8,128)S(1)}, f32[120,128]{1,0:T(8,128)S(1)}, u32[]{:S(2)}, u32[]{:S(2)}) collective-permute-start(f32[120,128]{1,0:T(8,128)S(1)} %get-tuple-element.35), channel_id=1, source_target_pairs={{1,0},{4,1},{5,4},{8,5},{9,8},{12,9},{13,12},{0,13},{3,2},{6,3},{7... | collective-permute-start | bytes 184328 | tf_op jit(solution)/shard_map/ppermute | solution.py:576
  7.6 1.6 %collective-permute-start.4 = (f32[112,128]{1,0:T(8,128)S(1)}, f32[112,128]{1,0:T(8,128)S(1)}, u32[]{:S(2)}, u32[]{:S(2)}) collective-permute-start(f32[112,128]{1,0:T(8,128)S(1)} %get-tuple-element.39), channel_id=1, source_target_pairs={{4,0},{5,1},{8,4},{9,5},{12,8},{13,9},{0,12},{1,13},{6,2},{7,3},{1... | collective-permute-start | bytes 172040 | tf_op jit(solution)/shard_map/ppermute | solution.py:576
  9.2 0.5 %fields_own.1 = (f32[816,128]{1,0:T(8,128)S(1)}, f32[768,128]{1,0:T(8,128)S(1)}) custom-call(bf16[1152,128]{1,0:T(8,128)(2,1)S(1)} %get-tuple-element.24.perm_ref, f32[96,128]{1,0:T(8,128)S(1)} %get-tuple-element.25.x_ref, f32[288,128]{1,0:T(8,128)S(1)} %get-tuple-element.26.u_ref), custom_call_target="tpu_custom_call" | custom-call | tf_op jit(solution)/shard_map/fields_own/pallas_call | solution.py:637
  9.7 0.4 %force_own.1._.own_part = f32[144,128]{1,0:T(8,128)S(1)} custom-call(f32[96,128]{1,0:T(8,128)S(1)} %get-tuple-element.23.scale_ref, f32[96,128]{1,0:T(8,128)S(1)} %get-tuple-element.25.x_ref, f32[288,128]{1,0:T(8,128)S(1)} %get-tuple-element.26.u_ref, f32[816,128]{1,0:T(8,128)S(1)} %get-tuple-element.27.shared_ref.own_shared.rest_0_, ...), custom_call_target="tpu_custom_call" | custom-call | flops 1000000 | bytes 7380000 | tf_op jit(solution)/shard_map/force_own/pallas_call | solution.py:645
  10.0 0.0 collective-permute-done.within_ref
  10.0 0.0 collective-permute-done.1.between_ref
  10.1 0.6 %collective-permute-start.5 = (f32[112,128]{1,0:T(8,128)S(1)}, f32[112,128]{1,0:T(8,128)S(1)}, u32[]{:S(2)}, u32[]{:S(2)}) collective-permute-start(f32[112,128]{1,0:T(8,128)S(1)} %get-tuple-element.40), channel_id=1, source_target_pairs={{2,0},{0,2},{3,1},{1,3},{6,4},{4,6},{7,5},{5,7},{10,8},{8,10},{11,... | collective-permute-start | bytes 172040 | tf_op jit(solution)/shard_map/ppermute | solution.py:577
  10.7 0.4 %force_z.1 = (f32[720,128]{1,0:T(8,128)S(1)}, f32[144,128]{1,0:T(8,128)S(1)}) custom-call(f32[96,128]{1,0:T(8,128)S(1)} %get-tuple-element.23.scale_ref, bf16[1152,128]{1,0:T(8,128)(2,1)S(1)} %get-tuple-element.24.perm_ref, f32[96,128]{1,0:T(8,128)S(1)} %get-tuple-element.25.x_ref, f32[288,128]{1,0:T(8,128)S(1)} %get-tuple-element.26.u_ref, ...), custom_call_target="tpu_custom_call" | custom-call | flops 1000000 | bytes 7380000 | tf_op jit(solution)/shard_map/force_z/pallas_call | solution.py:667
  11.1 0.0 collective-permute-done.3.rest_1_.rest_5_
  11.1 0.3 %collective-permute-done.2.rest_0_.rest_7_ = f32[240,128]{1,0:T(8,128)S(1)} collective-permute-done((f32[240,128]{1,0:T(8,128)S(1)}, f32[240,128]{1,0:T(8,128)S(1)}, u32[]{:S(2)}, u32[]{:S(2)}) %collective-permute-start.2) | collective-permute-done | bytes 122912 | tf_op jit(solution)/shard_map/ppermute | solution.py:577
  11.4 1.0 %force_t.1 = (f32[336,128]{1,0:T(8,128)S(1)}, f32[144,128]{1,0:T(8,128)S(1)}, f32[144,128]{1,0:T(8,128)S(1)}) custom-call(f32[96,128]{1,0:T(8,128)S(1)} %get-tuple-element.23.scale_ref, bf16[1152,128]{1,0:T(8,128)(2,1)S(1)} %get-tuple-element.24.perm_ref, f32[96,128]{1,0:T(8,128)S(1)} %get-tuple-element.25.x_ref, f32[288,128]{1,0:T(8,128)S(1)} %get-tuple-element.26.u_ref, ...), custom_call_target="tpu_custom_call" | custom-call | flops 1000000 | bytes 7380000 | tf_op jit(solution)/shard_map/force_t/pallas_call | solution.py:678
  12.4 0.0 collective-permute-done.4.rest_6_
  12.4 1.9 %collective-permute-done.5.rest_10_ = f32[112,128]{1,0:T(8,128)S(1)} collective-permute-done((f32[112,128]{1,0:T(8,128)S(1)}, f32[112,128]{1,0:T(8,128)S(1)}, u32[]{:S(2)}, u32[]{:S(2)}) %collective-permute-start.5) | collective-permute-done | bytes 57376 | tf_op jit(solution)/shard_map/ppermute | solution.py:577
  14.3 1.0 %force_corner.1 = f32[288,128]{1,0:T(8,128)} custom-call(f32[96,128]{1,0:T(8,128)S(1)} %get-tuple-element.23.scale_ref, bf16[1152,128]{1,0:T(8,128)(2,1)S(1)} %get-tuple-element.24.perm_ref, f32[96,128]{1,0:T(8,128)S(1)} %get-tuple-element.25.x_ref, f32[288,128]{1,0:T(8,128)S(1)} %get-tuple-element.26.u_ref, ...), custom_call_target="tpu_custom_call" | custom-call | flops 1000000 | bytes 3690000 | tf_op jit(solution)/shard_map/force_corner/pallas_call | solution.py:689
  (2 shorter events, 0.1 us)
Async XLA Ops:
  1.0 9.0 %collective-permute-start.1 = (f32[144,128]{1,0:T(8,128)S(1)}, f32[144,128]{1,0:T(8,128)S(1)}, u32[]{:S(2)}, u32[]{:S(2)}) collective-permute-start(f32[144,128]{1,0:T(8,128)S(1)} %get-tuple-element.30), channel_id=1, source_target_pairs={{1,4},{5,8},{9,12},{13,0},{4,1},{8,5},{12,9},{0,13},{3,6},{7,10},{... | collective-permute-start | bytes 221192 | tf_op jit(solution)/shard_map/ppermute | solution.py:581
  5.6 4.5 %collective-permute-start = (f32[136,128]{1,0:T(8,128)S(1)}, f32[136,128]{1,0:T(8,128)S(1)}, u32[]{:S(2)}, u32[]{:S(2)}) collective-permute-start(f32[136,128]{1,0:T(8,128)S(1)} %get-tuple-element.29), channel_id=1, source_target_pairs={{0,1},{4,5},{8,9},{12,13},{1,0},{5,4},{9,8},{13,12},{2,3},{6,7},{1... | collective-permute-start | bytes 208904 | tf_op jit(solution)/shard_map/ppermute | solution.py:581
  5.6 5.8 %collective-permute-start.2 = (f32[240,128]{1,0:T(8,128)S(1)}, f32[240,128]{1,0:T(8,128)S(1)}, u32[]{:S(2)}, u32[]{:S(2)}) collective-permute-start(f32[240,128]{1,0:T(8,128)S(1)} %pack_t.1), channel_id=1, source_target_pairs={{2,0},{0,2},{3,1},{1,3},{6,4},{4,6},{7,5},{5,7},{10,8},{8,10},{11,... | collective-permute-start | bytes 368648 | tf_op jit(solution)/shard_map/ppermute | solution.py:577
  7.1 4.0 %collective-permute-start.3 = (f32[120,128]{1,0:T(8,128)S(1)}, f32[120,128]{1,0:T(8,128)S(1)}, u32[]{:S(2)}, u32[]{:S(2)}) collective-permute-start(f32[120,128]{1,0:T(8,128)S(1)} %get-tuple-element.35), channel_id=1, source_target_pairs={{1,0},{4,1},{5,4},{8,5},{9,8},{12,9},{13,12},{0,13},{3,2},{6,3},{7... | collective-permute-start | bytes 184328 | tf_op jit(solution)/shard_map/ppermute | solution.py:576
  7.6 4.8 %collective-permute-start.4 = (f32[112,128]{1,0:T(8,128)S(1)}, f32[112,128]{1,0:T(8,128)S(1)}, u32[]{:S(2)}, u32[]{:S(2)}) collective-permute-start(f32[112,128]{1,0:T(8,128)S(1)} %get-tuple-element.39), channel_id=1, source_target_pairs={{4,0},{5,1},{8,4},{9,5},{12,8},{13,9},{0,12},{1,13},{6,2},{7,3},{1... | collective-permute-start | bytes 172040 | tf_op jit(solution)/shard_map/ppermute | solution.py:576
  10.1 4.2 %collective-permute-start.5 = (f32[112,128]{1,0:T(8,128)S(1)}, f32[112,128]{1,0:T(8,128)S(1)}, u32[]{:S(2)}, u32[]{:S(2)}) collective-permute-start(f32[112,128]{1,0:T(8,128)S(1)} %get-tuple-element.40), channel_id=1, source_target_pairs={{2,0},{0,2},{3,1},{1,3},{6,4},{4,6},{7,5},{5,7},{10,8},{8,10},{11,... | collective-permute-start | bytes 172040 | tf_op jit(solution)/shard_map/ppermute | solution.py:577

commit v15 on v14

--- a/solution.py
+++ b/solution.py
@@ -426,7 +426,7 @@
     write_messages(Locator(plan, 1, {("own", "x"): x_ref, ("own", "u"): u_ref}), plan, names, outs)
 
 
-def corner_kernel(plan, names, within_ref, between_ref, _, ahead_ref, behind_ref, *outs):
+def corner_kernel(plan, names, within_ref, between_ref, ahead_ref, behind_ref, *outs):
     def split(from_ahead, from_behind):
         ahead_ref[...] = from_ahead[pl.ds(0, ahead_ref.shape[0]), :]
         behind_ref[...] = from_behind[pl.ds(0, behind_ref.shape[0]), :]
@@ -586,12 +586,14 @@
     in_hbm = functools.partial(pltpu.with_memory_space_constraint, memory_space=pltpu.HBM)
     z_names = [("b", 1), ("z", 2)]
     corner_count = max(plan[name].count for name in corner_names)
+    late = max(plan["b", 1].count, corner_count)
+    late_counts = [late, late + 1]
     exchange_counts = [plan["z", step].count for step in (1, -1)]
     exchange = max(exchange_counts + [plan["t", 1].count - corner_count + 1])
     within, between, *sends, scale, perm, x_own, u_own = pl.pallas_call(
         functools.partial(pack_z_kernel, plan, z_names),
         out_shape=[rows_of(8 * exchange), rows_of(8 * (exchange + 1))]
-        + [rows_of(8 * max(plan[name].count, corner_count)) for name in z_names]
+        + [rows_of(8 * max(plan[name].count, least)) for name, least in zip(z_names, late_counts)]
         + [
             rows_of(8 * 3 * NP),
             jax.ShapeDtypeStruct((len(all_shifts()) * LANES, LANES), jnp.bfloat16),
@@ -657,11 +659,11 @@
         functools.partial(corner_kernel, plan, corner_names),
         out_shape=[rows_of(8 * count) for count in exchange_counts]
         + [rows_of(8 * plan[name].count) for name in corner_names],
-        in_specs=[vmem] * 3,
+        in_specs=[vmem] * 2,
         out_specs=[vmem] * (2 + len(corner_names)),
         compiler_params=limit,
         name="pack_corners",
-    )(within, between, own_part)
+    )(within, between)
     received.update({name: moved(name, value) for name, value in zip(corner_names, corners)})
     names = [("z", 1), ("z", -1)]
     z_shared, z_part = pl.pallas_call(

time: 15.5 us -> 14.3 us (0.923)
  waiting for transfers between devices: 2.19 us -> 0.64 us
  starting transfers between devices: 8.74 us -> 9.14 us
    ppermute x2, waiting for transfers between devices: 2.18 us -> 0.63 us  [moved(): lax.ppermute(value, 'ta', [((j + step) % t_size, j) for j in range(t_size)])]
    ppermute x2, starting transfers between devices: 2.15 us -> 2.84 us  [moved(): lax.ppermute(value, 'ta', [((j + step) % t_size, j) for j in range(t_size)])]
    ppermute x2, starting transfers between devices: 2.03 us -> 1.75 us  [moved(): lax.ppermute(value, ('gz', 'gy'), [((i + step) % z_size, i) for i in rang...]
  transfers between devices with their start and end apart: 6 -> 6, of which waited for: 2 -> 1; matrix products, arithmetic and copies ran while one was open for 0% -> 0% of each run, Pallas kernels for 15% -> 16%
where the time goes in v15:
time: 14.3 us; the launch traced here: 14.2 us
  starting transfers between devices  9.14 us (64%)
  Pallas kernels  4.33 us (30%)
  waiting for transfers between devices  0.64 us (4%)
    ppermute x2, starting transfers between devices, exchanged(): return lax.ppermute(value, ('gz', 'gy'), pairs + [(j, i) for i, j in pairs])  4.56 us
    ppermute x2, starting transfers between devices, moved(): lax.ppermute(value, 'ta', [((j + step) % t_size, j) for j in range(t_size)])  2.84 us
    ppermute x2, starting transfers between devices, moved(): lax.ppermute(value, ('gz', 'gy'), [((i + step) % z_size, i) for i in rang...  1.75 us
    pallas_call x1, Pallas kernels, on_device(): pl.pallas_call(functools.partial(last_kernel, plan, t_size, names), out_s...  1.03 us
    pallas_call x1, Pallas kernels, on_device(): pl.pallas_call(functools.partial(t_kernel, plan, t_size, far_names), out_...  1.02 us
    pallas_call x1, Pallas kernels, on_device(): pl.pallas_call(functools.partial(pack_z_kernel, plan, z_names), out_shape...  1 us
    ppermute x2, waiting for transfers between devices, moved(): lax.ppermute(value, 'ta', [((j + step) % t_size, j) for j in range(t_size)])  0.63 us
    pallas_call x1, Pallas kernels, on_device(): pl.pallas_call(functools.partial(own_fields_kernel, plan, t_size), out_sh...  0.48 us
  transfers between devices with their start and end apart: 6, of which 1 were waited for; matrix products, arithmetic and copies ran while one was open for 0% of the time, Pallas kernels for 16%

profile of v15, /device:TPU:0, one launch (start us, length us, event | category | flops | bytes accessed | tf_op | source)
XLA Modules:
  0.0 14.2 jit_solution(14552911212327648107)
XLA Ops:
  0.0 1.0 %pack_z.1 = (f32[136,128]{1,0:T(8,128)S(1)}, f32[144,128]{1,0:T(8,128)S(1)}, f32[120,128]{1,0:T(8,128)S(1)}, f32[128,128]{1,0:T(8,128)S(1)}, f32[96,128]{1,0:T(8...) custom-call(f32[4]{0:T(128)} %near_in.1, f32[4]{0:T(128)} %far_in.1, ...), custom_call_target="tpu_custom_call" | custom-call | tf_op jit(solution)/shard_map/pack_z/pallas_call | solution.py:593
  1.0 4.6 %collective-permute-start.1 = (f32[144,128]{1,0:T(8,128)S(1)}, f32[144,128]{1,0:T(8,128)S(1)}, u32[]{:S(2)}, u32[]{:S(2)}) collective-permute-start(f32[144,128]{1,0:T(8,128)S(1)} %get-tuple-element.30), channel_id=1, source_target_pairs={{1,4},{5,8},{9,12},{13,0},{4,1},{8,5},{12,9},{0,13},{3,6},{7,10},{... | collective-permute-start | bytes 221192 | tf_op jit(solution)/shard_map/ppermute | solution.py:581
  5.6 0.0 collective-permute-start
  5.6 1.6 %collective-permute-start.2 = (f32[240,128]{1,0:T(8,128)S(1)}, f32[240,128]{1,0:T(8,128)S(1)}, u32[]{:S(2)}, u32[]{:S(2)}) collective-permute-start(f32[240,128]{1,0:T(8,128)S(1)} %pack_t.1), channel_id=1, source_target_pairs={{2,0},{0,2},{3,1},{1,3},{6,4},{4,6},{7,5},{5,7},{10,8},{8,10},{11,... | collective-permute-start | bytes 368648 | tf_op jit(solution)/shard_map/ppermute | solution.py:577
  7.1 0.9 %collective-permute-start.4 = (f32[128,128]{1,0:T(8,128)S(1)}, f32[128,128]{1,0:T(8,128)S(1)}, u32[]{:S(2)}, u32[]{:S(2)}) collective-permute-start(f32[128,128]{1,0:T(8,128)S(1)} %get-tuple-element.39), channel_id=1, source_target_pairs={{4,0},{5,1},{8,4},{9,5},{12,8},{13,9},{0,12},{1,13},{6,2},{7,3},{1... | collective-permute-start | bytes 196616 | tf_op jit(solution)/shard_map/ppermute | solution.py:576
  8.0 0.9 %collective-permute-start.3 = (f32[120,128]{1,0:T(8,128)S(1)}, f32[120,128]{1,0:T(8,128)S(1)}, u32[]{:S(2)}, u32[]{:S(2)}) collective-permute-start(f32[120,128]{1,0:T(8,128)S(1)} %get-tuple-element.35), channel_id=1, source_target_pairs={{1,0},{4,1},{5,4},{8,5},{9,8},{12,9},{13,12},{0,13},{3,2},{6,3},{7... | collective-permute-start | bytes 184328 | tf_op jit(solution)/shard_map/ppermute | solution.py:576
  8.9 0.0 collective-permute-done.within_ref
  8.9 0.0 collective-permute-done.1.between_ref
  8.9 1.3 %collective-permute-start.5 = (f32[112,128]{1,0:T(8,128)S(1)}, f32[112,128]{1,0:T(8,128)S(1)}, u32[]{:S(2)}, u32[]{:S(2)}) collective-permute-start(f32[112,128]{1,0:T(8,128)S(1)} %get-tuple-element.40), channel_id=1, source_target_pairs={{2,0},{0,2},{3,1},{1,3},{6,4},{4,6},{7,5},{5,7},{10,8},{8,10},{11,... | collective-permute-start | bytes 172040 | tf_op jit(solution)/shard_map/ppermute | solution.py:577
  10.2 0.5 %fields_own.1 = (f32[816,128]{1,0:T(8,128)S(1)}, f32[768,128]{1,0:T(8,128)S(1)}) custom-call(bf16[1152,128]{1,0:T(8,128)(2,1)S(1)} %get-tuple-element.24.perm_ref, f32[96,128]{1,0:T(8,128)S(1)} %get-tuple-element.25.x_ref, f32[288,128]{1,0:T(8,128)S(1)} %get-tuple-element.26.u_ref), custom_call_target="tpu_custom_call" | custom-call | tf_op jit(solution)/shard_map/fields_own/pallas_call | solution.py:639
  10.7 0.4 %force_own.1.own_part = f32[144,128]{1,0:T(8,128)S(1)} custom-call(f32[96,128]{1,0:T(8,128)S(1)} %get-tuple-element.23.scale_ref, f32[96,128]{1,0:T(8,128)S(1)} %get-tuple-element.25.x_ref, f32[288,128]{1,0:T(8,128)S(1)} %get-tuple-element.26.u_ref, f32[816,128]{1,0:T(8,128)S(1)} %get-tuple-element.27.shared_ref.own_shared.rest_0_, ...), custom_call_target="tpu_custom_call" | custom-call | flops 1000000 | bytes 7380000 | tf_op jit(solution)/shard_map/force_own/pallas_call | solution.py:647
  11.1 0.4 %force_z.1 = (f32[720,128]{1,0:T(8,128)S(1)}, f32[144,128]{1,0:T(8,128)S(1)}) custom-call(f32[96,128]{1,0:T(8,128)S(1)} %get-tuple-element.23.scale_ref, bf16[1152,128]{1,0:T(8,128)(2,1)S(1)} %get-tuple-element.24.perm_ref, f32[96,128]{1,0:T(8,128)S(1)} %get-tuple-element.25.x_ref, f32[288,128]{1,0:T(8,128)S(1)} %get-tuple-element.26.u_ref, ...), custom_call_target="tpu_custom_call" | custom-call | flops 1000000 | bytes 7380000 | tf_op jit(solution)/shard_map/force_z/pallas_call | solution.py:669
  11.5 0.0 collective-permute-done.3.rest_1_.rest_5_
  11.5 0.0 collective-permute-done.2.rest_0_.rest_7_
  11.5 1.0 %force_t.1 = (f32[336,128]{1,0:T(8,128)S(1)}, f32[144,128]{1,0:T(8,128)S(1)}, f32[144,128]{1,0:T(8,128)S(1)}) custom-call(f32[96,128]{1,0:T(8,128)S(1)} %get-tuple-element.23.scale_ref, bf16[1152,128]{1,0:T(8,128)(2,1)S(1)} %get-tuple-element.24.perm_ref, f32[96,128]{1,0:T(8,128)S(1)} %get-tuple-element.25.x_ref, f32[288,128]{1,0:T(8,128)S(1)} %get-tuple-element.26.u_ref, ...), custom_call_target="tpu_custom_call" | custom-call | flops 1000000 | bytes 7380000 | tf_op jit(solution)/shard_map/force_t/pallas_call | solution.py:680
  12.5 0.0 collective-permute-done.4.rest_6_
  12.5 0.6 %collective-permute-done.5.rest_10_ = f32[112,128]{1,0:T(8,128)S(1)} collective-permute-done((f32[112,128]{1,0:T(8,128)S(1)}, f32[112,128]{1,0:T(8,128)S(1)}, u32[]{:S(2)}, u32[]{:S(2)}) %collective-permute-start.5) | collective-permute-done | bytes 57376 | tf_op jit(solution)/shard_map/ppermute | solution.py:577
  13.2 1.0 %force_corner.1 = f32[288,128]{1,0:T(8,128)} custom-call(f32[96,128]{1,0:T(8,128)S(1)} %get-tuple-element.23.scale_ref, bf16[1152,128]{1,0:T(8,128)(2,1)S(1)} %get-tuple-element.24.perm_ref, f32[96,128]{1,0:T(8,128)S(1)} %get-tuple-element.25.x_ref, f32[288,128]{1,0:T(8,128)S(1)} %get-tuple-element.26.u_ref, ...), custom_call_target="tpu_custom_call" | custom-call | flops 1000000 | bytes 3690000 | tf_op jit(solution)/shard_map/force_corner/pallas_call | solution.py:691
  (2 shorter events, 0.0 us)
Async XLA Ops:
  1.0 7.9 %collective-permute-start.1 = (f32[144,128]{1,0:T(8,128)S(1)}, f32[144,128]{1,0:T(8,128)S(1)}, u32[]{:S(2)}, u32[]{:S(2)}) collective-permute-start(f32[144,128]{1,0:T(8,128)S(1)} %get-tuple-element.30), channel_id=1, source_target_pairs={{1,4},{5,8},{9,12},{13,0},{4,1},{8,5},{12,9},{0,13},{3,6},{7,10},{... | collective-permute-start | bytes 221192 | tf_op jit(solution)/shard_map/ppermute | solution.py:581
  5.6 3.3 %collective-permute-start = (f32[136,128]{1,0:T(8,128)S(1)}, f32[136,128]{1,0:T(8,128)S(1)}, u32[]{:S(2)}, u32[]{:S(2)}) collective-permute-start(f32[136,128]{1,0:T(8,128)S(1)} %get-tuple-element.29), channel_id=1, source_target_pairs={{0,1},{4,5},{8,9},{12,13},{1,0},{5,4},{9,8},{13,12},{2,3},{6,7},{1... | collective-permute-start | bytes 208904 | tf_op jit(solution)/shard_map/ppermute | solution.py:581
  5.6 5.9 %collective-permute-start.2 = (f32[240,128]{1,0:T(8,128)S(1)}, f32[240,128]{1,0:T(8,128)S(1)}, u32[]{:S(2)}, u32[]{:S(2)}) collective-permute-start(f32[240,128]{1,0:T(8,128)S(1)} %pack_t.1), channel_id=1, source_target_pairs={{2,0},{0,2},{3,1},{1,3},{6,4},{4,6},{7,5},{5,7},{10,8},{8,10},{11,... | collective-permute-start | bytes 368648 | tf_op jit(solution)/shard_map/ppermute | solution.py:577
  7.1 5.4 %collective-permute-start.4 = (f32[128,128]{1,0:T(8,128)S(1)}, f32[128,128]{1,0:T(8,128)S(1)}, u32[]{:S(2)}, u32[]{:S(2)}) collective-permute-start(f32[128,128]{1,0:T(8,128)S(1)} %get-tuple-element.39), channel_id=1, source_target_pairs={{4,0},{5,1},{8,4},{9,5},{12,8},{13,9},{0,12},{1,13},{6,2},{7,3},{1... | collective-permute-start | bytes 196616 | tf_op jit(solution)/shard_map/ppermute | solution.py:576
  8.0 3.4 %collective-permute-start.3 = (f32[120,128]{1,0:T(8,128)S(1)}, f32[120,128]{1,0:T(8,128)S(1)}, u32[]{:S(2)}, u32[]{:S(2)}) collective-permute-start(f32[120,128]{1,0:T(8,128)S(1)} %get-tuple-element.35), channel_id=1, source_target_pairs={{1,0},{4,1},{5,4},{8,5},{9,8},{12,9},{13,12},{0,13},{3,2},{6,3},{7... | collective-permute-start | bytes 184328 | tf_op jit(solution)/shard_map/ppermute | solution.py:576
  8.9 4.2 %collective-permute-start.5 = (f32[112,128]{1,0:T(8,128)S(1)}, f32[112,128]{1,0:T(8,128)S(1)}, u32[]{:S(2)}, u32[]{:S(2)}) collective-permute-start(f32[112,128]{1,0:T(8,128)S(1)} %get-tuple-element.40), channel_id=1, source_target_pairs={{2,0},{0,2},{3,1},{1,3},{6,4},{4,6},{7,5},{5,7},{10,8},{8,10},{11,... | collective-permute-start | bytes 172040 | tf_op jit(solution)/shard_map/ppermute | solution.py:577

commit v16 on v15

--- a/solution.py
+++ b/solution.py
@@ -25,7 +25,7 @@
     "corner": ((0, ((2, 3), (3, 2))),),
 }
 COSTS = {"own": 2.0, "z": 2.0, "t": 2.0, "corner": 1.0}
-DIRECT = {"own": (0, 1), "z": (), "t": (3,), "corner": (2,)}
+DIRECT = {"own": (0, 1), "z": (), "t": (2, 3), "corner": ()}
 
 
 def plus(left, right, scale=1):
@@ -179,9 +179,9 @@
     dz, dt = key[2][2:]
     if key[0] == "u" and key[1] < 2 and dz == 1 and dt == 0:
         return "t"
-    if abs(dz) == 3 or (dz != 0 and dt != 0):
+    if dz != 0 and dt != 0:
         return "corner"
-    return "t" if dt != 0 else "z" if dz != 0 else "own"
+    return "t" if dt != 0 or abs(dz) == 3 else "z" if dz != 0 else "own"
 
 
 def lay_out(keys):
@@ -404,7 +404,7 @@
     for copy in copies:
         copy.start()
     write_shifts(perm_ref)
-    for copy in copies:
+    for copy in copies[:2]:
         copy.wait()
     u_ref[...] = u_held[...].astype(F32)
     locator = Locator(plan, 1, {("own", "x"): x_ref, ("own", "u"): u_ref})
@@ -419,6 +419,8 @@
         write_messages(locator, plan, both, (between_ref, within_ref))
 
     write_messages(locator, plan, names, outs)
+    for copy in copies[2:]:
+        copy.wait()
     write_scales(near_ref, far_ref, weight_ref, scale_ref)
 
 
@@ -516,12 +518,12 @@
         staples = fields.compact_halves(acc_tile(acc, 0, 2 * k), acc_tile(acc, 0, 2 * k + 1))
         for m in range(2):
             ready[pl.ds((9 * m + k) * 8, 8), :] = part_reg(z_part, m, k) + weight[m] * staples[m]
-    direct = own_force(fields, 3, both)
+    own_z, own_t = [own_force(fields, m, both) for m in DIRECT["t"]]
     for k in range(9):
         staple = fields.compact_sum(acc_tile(acc, 1, 2 * k), acc_tile(acc, 1, 2 * k + 1))
-        part_ref[pl.ds(k * 8, 8), :] = direct[k] + weight[3] * staple
+        part_ref[pl.ds(k * 8, 8), :] = own_t[k] + weight[3] * staple
         staple = fields.compact_sum(acc_tile(acc, 2, 2 * k), acc_tile(acc, 2, 2 * k + 1))
-        part_ref[pl.ds((9 + k) * 8, 8), :] = weight[2] * staple
+        part_ref[pl.ds((9 + k) * 8, 8), :] = own_z[k] + weight[2] * staple
 
 
 def last_kernel(plan, t_size, names, scale_ref, perm_ref, x_ref, u_ref, *rest):
@@ -544,12 +546,11 @@
         None,
         alone_ref,
     )
-    near, both, weight = scale_tiles(scale_ref)
+    near, _, weight = scale_tiles(scale_ref)
     add_terms(fields, "corner", near, acc)
-    direct = own_force(fields, 2, both)
     for k in range(9):
         staples = fields.compact_halves(acc_tile(acc, 0, 2 * k), acc_tile(acc, 0, 2 * k + 1))
-        ready[pl.ds(k * 8, 8), :] = part_reg(t_part, 1, k) + direct[k] + weight[2] * staples[0]
+        ready[pl.ds(k * 8, 8), :] = part_reg(t_part, 1, k) + weight[2] * staples[0]
         ready[pl.ds((9 + k) * 8, 8), :] = part_reg(t_part, 0, k) + weight[3] * staples[1]
     second = pltpu.make_async_copy(ready, out_ref.at[pl.ds(rows, rows)], sems.at[1])
     second.start()
@@ -676,7 +677,7 @@
         compiler_params=wide_limit,
         name="force_z",
     )(*local, own_shared, own_part, *[received[name] for name in names])
-    far_names = t_names + [("b", 1)]
+    far_names = t_names + [("b", 1), ("z", 2)]
     t_shared, t_part, earlier = pl.pallas_call(
         functools.partial(t_kernel, plan, t_size, far_names),
         out_shape=[rows_of(shared["t"][1]), rows_of(2 * part_rows), rows_of(2 * part_rows)],
@@ -687,7 +688,7 @@
         compiler_params=wide_limit,
         name="force_t",
     )(*local, own_shared, z_shared, z_part, *[received[name] for name in far_names])
-    names = list(received)
+    names = [name for name in received if name not in (("b", 1), ("z", 2))]
     force = pl.pallas_call(
         functools.partial(last_kernel, plan, t_size, names),
         out_shape=rows_of(u_rows),

time: 14.3 us -> 14.3 us (level)
  transfers between devices with their start and end apart: 6 -> 6, of which waited for: 1 -> 1; matrix products, arithmetic and copies ran while one was open for 0% -> 0% of each run, Pallas kernels for 16% -> 17%
where the time goes in v16:
time: 14.3 us; the launch traced here: 14.1 us
  starting transfers between devices  9.14 us (64%)
  Pallas kernels  4.33 us (30%)
  waiting for transfers between devices  0.58 us (4%)
    ppermute x2, starting transfers between devices, exchanged(): return lax.ppermute(value, ('gz', 'gy'), pairs + [(j, i) for i, j in pairs])  4.55 us
    ppermute x2, starting transfers between devices, moved(): lax.ppermute(value, 'ta', [((j + step) % t_size, j) for j in range(t_size)])  2.84 us
    ppermute x2, starting transfers between devices, moved(): lax.ppermute(value, ('gz', 'gy'), [((i + step) % z_size, i) for i in rang...  1.75 us
    pallas_call x1, Pallas kernels, on_device(): pl.pallas_call(functools.partial(t_kernel, plan, t_size, far_names), out_...  1.08 us
    pallas_call x1, Pallas kernels, on_device(): pl.pallas_call(functools.partial(pack_z_kernel, plan, z_names), out_shape...  1 us
    pallas_call x1, Pallas kernels, on_device(): pl.pallas_call(functools.partial(last_kernel, plan, t_size, names), out_s...  0.96 us
    ppermute x2, waiting for transfers between devices, moved(): lax.ppermute(value, 'ta', [((j + step) % t_size, j) for j in range(t_size)])  0.57 us
    pallas_call x1, Pallas kernels, on_device(): pl.pallas_call(functools.partial(own_fields_kernel, plan, t_size), out_sh...  0.48 us
  transfers between devices with their start and end apart: 6, of which 1 were waited for; matrix products, arithmetic and copies ran while one was open for 0% of the time, Pallas kernels for 17%

profile of v16, /device:TPU:0, one launch (start us, length us, event | category | flops | bytes accessed | tf_op | source)
XLA Modules:
  0.0 14.1 jit_solution(2745426697431797986)
XLA Ops:
  0.0 1.0 %pack_z.1 = (f32[136,128]{1,0:T(8,128)S(1)}, f32[144,128]{1,0:T(8,128)S(1)}, f32[120,128]{1,0:T(8,128)S(1)}, f32[128,128]{1,0:T(8,128)S(1)}, f32[96,128]{1,0:T(8...) custom-call(f32[4]{0:T(128)} %near_in.1, f32[4]{0:T(128)} %far_in.1, ...), custom_call_target="tpu_custom_call" | custom-call | tf_op jit(solution)/shard_map/pack_z/pallas_call | solution.py:594
  1.0 4.6 %collective-permute-start.1 = (f32[144,128]{1,0:T(8,128)S(1)}, f32[144,128]{1,0:T(8,128)S(1)}, u32[]{:S(2)}, u32[]{:S(2)}) collective-permute-start(f32[144,128]{1,0:T(8,128)S(1)} %get-tuple-element.30), channel_id=1, source_target_pairs={{1,4},{5,8},{9,12},{13,0},{4,1},{8,5},{12,9},{0,13},{3,6},{7,10},{... | collective-permute-start | bytes 221192 | tf_op jit(solution)/shard_map/ppermute | solution.py:582
  5.6 0.0 collective-permute-start
  5.6 1.6 %collective-permute-start.2 = (f32[240,128]{1,0:T(8,128)S(1)}, f32[240,128]{1,0:T(8,128)S(1)}, u32[]{:S(2)}, u32[]{:S(2)}) collective-permute-start(f32[240,128]{1,0:T(8,128)S(1)} %pack_t.1), channel_id=1, source_target_pairs={{2,0},{0,2},{3,1},{1,3},{6,4},{4,6},{7,5},{5,7},{10,8},{8,10},{11,... | collective-permute-start | bytes 368648 | tf_op jit(solution)/shard_map/ppermute | solution.py:578
  7.1 0.9 %collective-permute-start.4 = (f32[128,128]{1,0:T(8,128)S(1)}, f32[128,128]{1,0:T(8,128)S(1)}, u32[]{:S(2)}, u32[]{:S(2)}) collective-permute-start(f32[128,128]{1,0:T(8,128)S(1)} %get-tuple-element.36), channel_id=1, source_target_pairs={{4,0},{5,1},{8,4},{9,5},{12,8},{13,9},{0,12},{1,13},{6,2},{7,3},{1... | collective-permute-start | bytes 196616 | tf_op jit(solution)/shard_map/ppermute | solution.py:577
  8.0 0.9 %collective-permute-start.3 = (f32[120,128]{1,0:T(8,128)S(1)}, f32[120,128]{1,0:T(8,128)S(1)}, u32[]{:S(2)}, u32[]{:S(2)}) collective-permute-start(f32[120,128]{1,0:T(8,128)S(1)} %get-tuple-element.35), channel_id=1, source_target_pairs={{1,0},{4,1},{5,4},{8,5},{9,8},{12,9},{13,12},{0,13},{3,2},{6,3},{7... | collective-permute-start | bytes 184328 | tf_op jit(solution)/shard_map/ppermute | solution.py:577
  8.9 0.0 collective-permute-done.within_ref
  8.9 0.0 collective-permute-done.1.between_ref
  8.9 1.3 %collective-permute-start.5 = (f32[112,128]{1,0:T(8,128)S(1)}, f32[112,128]{1,0:T(8,128)S(1)}, u32[]{:S(2)}, u32[]{:S(2)}) collective-permute-start(f32[112,128]{1,0:T(8,128)S(1)} %get-tuple-element.40), channel_id=1, source_target_pairs={{2,0},{0,2},{3,1},{1,3},{6,4},{4,6},{7,5},{5,7},{10,8},{8,10},{11,... | collective-permute-start | bytes 172040 | tf_op jit(solution)/shard_map/ppermute | solution.py:578
  10.2 0.5 %fields_own.1 = (f32[816,128]{1,0:T(8,128)S(1)}, f32[768,128]{1,0:T(8,128)S(1)}) custom-call(bf16[1152,128]{1,0:T(8,128)(2,1)S(1)} %get-tuple-element.24.perm_ref, f32[96,128]{1,0:T(8,128)S(1)} %get-tuple-element.25.x_ref, f32[288,128]{1,0:T(8,128)S(1)} %get-tuple-element.26.u_ref), custom_call_target="tpu_custom_call" | custom-call | tf_op jit(solution)/shard_map/fields_own/pallas_call | solution.py:640
  10.7 0.4 %force_own.1.own_part = f32[144,128]{1,0:T(8,128)S(1)} custom-call(f32[96,128]{1,0:T(8,128)S(1)} %get-tuple-element.23.scale_ref, f32[96,128]{1,0:T(8,128)S(1)} %get-tuple-element.25.x_ref, f32[288,128]{1,0:T(8,128)S(1)} %get-tuple-element.26.u_ref, f32[816,128]{1,0:T(8,128)S(1)} %get-tuple-element.27.shared_ref.own_shared.rest_0_, ...), custom_call_target="tpu_custom_call" | custom-call | flops 1000000 | bytes 7380000 | tf_op jit(solution)/shard_map/force_own/pallas_call | solution.py:648
  11.1 0.4 %force_z.1 = (f32[720,128]{1,0:T(8,128)S(1)}, f32[144,128]{1,0:T(8,128)S(1)}) custom-call(f32[96,128]{1,0:T(8,128)S(1)} %get-tuple-element.23.scale_ref, bf16[1152,128]{1,0:T(8,128)(2,1)S(1)} %get-tuple-element.24.perm_ref, f32[96,128]{1,0:T(8,128)S(1)} %get-tuple-element.25.x_ref, f32[288,128]{1,0:T(8,128)S(1)} %get-tuple-element.26.u_ref, ...), custom_call_target="tpu_custom_call" | custom-call | flops 1000000 | bytes 7380000 | tf_op jit(solution)/shard_map/force_z/pallas_call | solution.py:670
  11.5 0.0 collective-permute-done.3.rest_1_
  11.5 0.0 collective-permute-done.4.rest_2_
  11.5 0.0 collective-permute-done.2.rest_0_.rest_5_
  11.5 1.1 %force_t.1 = (f32[336,128]{1,0:T(8,128)S(1)}, f32[144,128]{1,0:T(8,128)S(1)}, f32[144,128]{1,0:T(8,128)S(1)}) custom-call(f32[96,128]{1,0:T(8,128)S(1)} %get-tuple-element.23.scale_ref, bf16[1152,128]{1,0:T(8,128)(2,1)S(1)} %get-tuple-element.24.perm_ref, f32[96,128]{1,0:T(8,128)S(1)} %get-tuple-element.25.x_ref, f32[288,128]{1,0:T(8,128)S(1)} %get-tuple-element.26.u_ref, ...), custom_call_target="tpu_custom_call" | custom-call | flops 1000000 | bytes 7380000 | tf_op jit(solution)/shard_map/force_t/pallas_call | solution.py:681
  12.6 0.6 %collective-permute-done.5.rest_8_ = f32[112,128]{1,0:T(8,128)S(1)} collective-permute-done((f32[112,128]{1,0:T(8,128)S(1)}, f32[112,128]{1,0:T(8,128)S(1)}, u32[]{:S(2)}, u32[]{:S(2)}) %collective-permute-start.5) | collective-permute-done | bytes 57376 | tf_op jit(solution)/shard_map/ppermute | solution.py:578
  13.2 1.0 %force_corner.1 = f32[288,128]{1,0:T(8,128)} custom-call(f32[96,128]{1,0:T(8,128)S(1)} %get-tuple-element.23.scale_ref, bf16[1152,128]{1,0:T(8,128)(2,1)S(1)} %get-tuple-element.24.perm_ref, f32[96,128]{1,0:T(8,128)S(1)} %get-tuple-element.25.x_ref, f32[288,128]{1,0:T(8,128)S(1)} %get-tuple-element.26.u_ref, ...), custom_call_target="tpu_custom_call" | custom-call | flops 1000000 | bytes 3690000 | tf_op jit(solution)/shard_map/force_corner/pallas_call | solution.py:692
  (2 shorter events, 0.0 us)
Async XLA Ops:
  1.0 7.9 %collective-permute-start.1 = (f32[144,128]{1,0:T(8,128)S(1)}, f32[144,128]{1,0:T(8,128)S(1)}, u32[]{:S(2)}, u32[]{:S(2)}) collective-permute-start(f32[144,128]{1,0:T(8,128)S(1)} %get-tuple-element.30), channel_id=1, source_target_pairs={{1,4},{5,8},{9,12},{13,0},{4,1},{8,5},{12,9},{0,13},{3,6},{7,10},{... | collective-permute-start | bytes 221192 | tf_op jit(solution)/shard_map/ppermute | solution.py:582
  5.6 3.3 %collective-permute-start = (f32[136,128]{1,0:T(8,128)S(1)}, f32[136,128]{1,0:T(8,128)S(1)}, u32[]{:S(2)}, u32[]{:S(2)}) collective-permute-start(f32[136,128]{1,0:T(8,128)S(1)} %get-tuple-element.29), channel_id=1, source_target_pairs={{0,1},{4,5},{8,9},{12,13},{1,0},{5,4},{9,8},{13,12},{2,3},{6,7},{1... | collective-permute-start | bytes 208904 | tf_op jit(solution)/shard_map/ppermute | solution.py:582
  5.6 5.9 %collective-permute-start.2 = (f32[240,128]{1,0:T(8,128)S(1)}, f32[240,128]{1,0:T(8,128)S(1)}, u32[]{:S(2)}, u32[]{:S(2)}) collective-permute-start(f32[240,128]{1,0:T(8,128)S(1)} %pack_t.1), channel_id=1, source_target_pairs={{2,0},{0,2},{3,1},{1,3},{6,4},{4,6},{7,5},{5,7},{10,8},{8,10},{11,... | collective-permute-start | bytes 368648 | tf_op jit(solution)/shard_map/ppermute | solution.py:578
  7.1 4.4 %collective-permute-start.4 = (f32[128,128]{1,0:T(8,128)S(1)}, f32[128,128]{1,0:T(8,128)S(1)}, u32[]{:S(2)}, u32[]{:S(2)}) collective-permute-start(f32[128,128]{1,0:T(8,128)S(1)} %get-tuple-element.36), channel_id=1, source_target_pairs={{4,0},{5,1},{8,4},{9,5},{12,8},{13,9},{0,12},{1,13},{6,2},{7,3},{1... | collective-permute-start | bytes 196616 | tf_op jit(solution)/shard_map/ppermute | solution.py:577
  8.0 3.5 %collective-permute-start.3 = (f32[120,128]{1,0:T(8,128)S(1)}, f32[120,128]{1,0:T(8,128)S(1)}, u32[]{:S(2)}, u32[]{:S(2)}) collective-permute-start(f32[120,128]{1,0:T(8,128)S(1)} %get-tuple-element.35), channel_id=1, source_target_pairs={{1,0},{4,1},{5,4},{8,5},{9,8},{12,9},{13,12},{0,13},{3,2},{6,3},{7... | collective-permute-start | bytes 184328 | tf_op jit(solution)/shard_map/ppermute | solution.py:577
  8.9 4.2 %collective-permute-start.5 = (f32[112,128]{1,0:T(8,128)S(1)}, f32[112,128]{1,0:T(8,128)S(1)}, u32[]{:S(2)}, u32[]{:S(2)}) collective-permute-start(f32[112,128]{1,0:T(8,128)S(1)} %get-tuple-element.40), channel_id=1, source_target_pairs={{2,0},{0,2},{3,1},{1,3},{6,4},{4,6},{7,5},{5,7},{10,8},{8,10},{11,... | collective-permute-start | bytes 172040 | tf_op jit(solution)/shard_map/ppermute | solution.py:578
